TPU v7x, 128 devices: a whole 4x4x4 slice. The times are simulated.
128 devices in a mesh: lon: 32 (over y, x, z_lo), lat: 4 (over z_hi, core).
Axes of the slice: x: 4, y: 4, z: 4 (z_hi: 2, z_lo: 2; z = z_hi * 2 + z_lo), core: 2. Of those that a mesh axis runs over, the one named last changes fastest.
Arguments:
- first_features: bfloat16 [32, 8192, 128], P(None, ('lon', 'lat')), may hold values from -6 to 6
- second_features: bfloat16 [32, 8192, 128], P(None, ('lon', 'lat')), may hold values from -6 to 6
- hidden_state: bfloat16 [32, 8192, 128], P('lat', 'lon'), may hold values from -1 to 1
- encoder_weight: bfloat16 [289, 128], replicated, may hold values from -0.375 to 0.375
- gates_weight: bfloat16 [3, 3, 256, 256], replicated, may hold values from -0.125 to 0.125
- candidate_weight: bfloat16 [3, 3, 256, 128], replicated, may hold values from -0.125 to 0.125
- row_metric: float32 [32], replicated, may hold values from 1 to 3
Outputs:
- new_state: bfloat16 [32, 8192, 128], P('lat', 'lon')
All inputs are finite; a program needn't handle non-finite values.
Results may differ from a plain program's by a relative error of at most 0.0058.
Values may be sent and summed in bfloat16 or wider, within the bound.
No kernel may reach another device: no remote copies, remote signals or barrier semaphores. Data moves between devices by JAX's collectives and lax.ppermute only.
A program may use at most 64 MiB of HBM per device.

v0:
```python
import jax
import jax.numpy as jnp
from jax import lax
from jax.sharding import PartitionSpec as P

RADIUS = 8


def extended_2(cells, sides, width):
    for axis, dim in sides:
        count = lax.axis_size(axis)
        head = lax.slice_in_dim(cells, 0, width, axis=dim)
        tail = lax.slice_in_dim(cells, cells.shape[dim] - width, cells.shape[dim], axis=dim)
        cells = jnp.concatenate(
            [
                lax.ppermute(tail, axis, [(i, (i + 1) % count) for i in range(count)]),
                cells,
                lax.ppermute(head, axis, [((i + 1) % count, i) for i in range(count)]),
            ],
            axis=dim,
        )
    return cells


def correlate_block(first_map, second_ext):
    height, breadth, channels = first_map.shape
    window_size = second_ext.shape[0] - height + 1
    group = second_ext.shape[1] - breadth
    groups = breadth // group
    extended = 2 * group
    first_groups = first_map.reshape(height, groups, group, channels)
    planes = []
    for shift_y in range(window_size):
        strip = second_ext[shift_y : shift_y + height]
        left_part = strip[:, :breadth].reshape(height, groups, group, channels)
        right_part = strip[:, group : group + breadth].reshape(height, groups, group, channels)
        strip_groups = jnp.concatenate([left_part, right_part], axis=2)
        banded = jnp.einsum(
            "rgjc,rgkc->rgjk", first_groups, strip_groups, preferred_element_type=jnp.float32
        )
        flat = banded.reshape(height, groups, group * extended)
        flat = jnp.pad(flat, ((0, 0), (0, 0), (0, group)))
        diagonal = flat.reshape(height, groups, group, extended + 1)[:, :, :, :window_size]
        planes.append(diagonal.reshape(height, breadth, window_size))
    stacked = jnp.stack(planes, axis=2)
    return (stacked * channels ** (-0.5)).reshape(height * breadth, window_size * window_size)


def encode_motion(first_map, second_ext, encoder_weight):
    height, breadth = (first_map.shape[0], first_map.shape[1])
    correlation = correlate_block(first_map, second_ext).astype(jnp.bfloat16)
    motion = jax.nn.relu(jnp.dot(correlation, encoder_weight, preferred_element_type=jnp.float32))
    return motion.astype(jnp.bfloat16).reshape(height, breadth, -1)


def clear_poles(extended, width):
    position = lax.axis_index("lat")
    final_index = lax.axis_size("lat") - 1
    row_ids = lax.broadcasted_iota(jnp.int32, (extended.shape[0], 1, 1), 0)
    top_rim = (row_ids < width) & (position == 0)
    bottom_rim = (row_ids >= extended.shape[0] - width) & (position == final_index)
    return jnp.where(top_rim | bottom_rim, jnp.zeros_like(extended), extended)


def tap_sum(padded, weights, metric_rows):
    height = padded.shape[0] - 2
    breadth = padded.shape[1] - 2
    center = jnp.zeros((height * breadth, weights.shape[-1]), jnp.float32)
    sides = jnp.zeros((height * breadth, weights.shape[-1]), jnp.float32)
    for tap_row in range(3):
        for tap_col in range(3):
            window = padded[tap_row : tap_row + height, tap_col : tap_col + breadth].reshape(
                height * breadth, -1
            )
            contribution = jnp.dot(
                window, weights[tap_row, tap_col], preferred_element_type=jnp.float32
            )
            if tap_col == 1:
                center = center + contribution
            else:
                sides = sides + contribution
    center = center.reshape(height, breadth, -1)
    sides = sides.reshape(height, breadth, -1)
    return center + sides * metric_rows[:, None, None]


def body(
    first_features,
    second_features,
    hidden_state,
    encoder_weight,
    gates_weight,
    candidate_weight,
    row_metric,
):
    first_tile, second_tile = (
        lax.all_to_all(first_features, "lat", split_axis=0, concat_axis=1, tiled=True),
        lax.all_to_all(second_features, "lat", split_axis=0, concat_axis=1, tiled=True),
    )
    second_ext = extended_2(second_tile, (("lon", 1), ("lat", 0)), RADIUS)
    second_ext = clear_poles(second_ext, RADIUS)
    motion = encode_motion(first_tile, second_ext, encoder_weight)
    tile_rows = hidden_state.shape[0]
    hidden_dim = hidden_state.shape[2]
    start_row = lax.axis_index("lat") * tile_rows
    metric_padded = jnp.pad(row_metric, (2, 2))
    tile_metric = lax.dynamic_slice_in_dim(metric_padded, start_row + 2, tile_rows)
    state_float = hidden_state.astype(jnp.float32)
    joined = jnp.concatenate([hidden_state, motion], axis=-1)
    joined_ext = extended_2(joined, (("lon", 1), ("lat", 0)), 1)
    joined_ext = clear_poles(joined_ext, 1)
    gate_values = jax.nn.sigmoid(tap_sum(joined_ext, gates_weight, tile_metric))
    reset_state = (gate_values[..., hidden_dim:] * state_float).astype(jnp.bfloat16)
    reset_ext = extended_2(reset_state, (("lon", 1), ("lat", 0)), 1)
    reset_ext = clear_poles(reset_ext, 1)
    candidate_input = jnp.concatenate([reset_ext, joined_ext[..., hidden_dim:]], axis=-1)
    update_gate = gate_values[..., :hidden_dim]
    candidate = jnp.tanh(tap_sum(candidate_input, candidate_weight, tile_metric))
    return ((1.0 - update_gate) * state_float + update_gate * candidate).astype(jnp.bfloat16)


def solution(mesh):
    return jax.shard_map(
        body,
        mesh=mesh,
        in_specs=(
            P(None, ("lon", "lat"), None),
            P(None, ("lon", "lat"), None),
            P("lat", "lon", None),
            P(),
            P(),
            P(),
            P(),
        ),
        out_specs=P("lat", "lon", None),
        check_vma=False,
    )
```

profile of v0, /device:TPU:1, one launch (start us, length us, event | category | flops | bytes accessed | tf_op | source)
XLA Modules:
  0.0 202.2 jit_solution(7453268707154021432)
XLA Ops:
  0.0 16.1 %all_to_all.33 = bf16[32,64,128]{2,1,0:T(8,128)(2,1)S(1)} all-to-all(bf16[32,64,128]{2,1,0:T(8,128)(2,1)} %param.8), channel_id=1, replica_groups=mesh['lon'=32,'lat'=4] {'lat'}, dimensions={0} | all-to-all | bytes 1048576 | tf_op jit(solution)/shard_map/all_to_all | solution.py:98
  17.0 4.9 %collective-permute-start.1 = (bf16[8,8,128]{2,1,0:T(8,128)(2,1)S(1)}, bf16[8,8,128]{2,1,0:T(8,128)(2,1)S(1)}, u32[]{:S(2)}, u32[]{:S(2)}) collective-permute-start(bf16[8,8,128]{2,1,0:T(8,128)(2,1)S(1)} %get-tuple-element.66), channel_id=1, source_target_pairs={{4,0},{8,4},{12,8},{16,12},{20,16},{24,20},{28,24},{32,28},{36,32}... | collective-permute-start | bytes 49160 | tf_op jit(solution)/shard_map/ppermute | solution.py:18
  21.9 1.1 collective-permute-done
  23.1 2.3 %collective-permute-start.3 = (bf16[8,272,128]{2,1,0:T(8,128)(2,1)S(1)}, bf16[8,272,128]{2,1,0:T(8,128)(2,1)S(1)}, u32[]{:S(2)}, u32[]{:S(2)}) collective-permute-start(bf16[8,272,128]{2,1,0:T(8,128)(2,1)S(1)} %pad_maximum_fusion.1), channel_id=1, source_target_pairs={{1,0},{2,1},{3,2},{0,3},{5,4},{6,5},{7,6},{4,7},{9,8},{10,9},{11,1... | collective-permute-start | bytes 1671176 | tf_op jit(solution)/shard_map/ppermute | solution.py:18
  26.4 3.5 %all-to-all-start.1 = ((bf16[32,64,128]{2,1,0:T(8,128)(2,1)}), bf16[32,64,128]{2,1,0:T(8,128)(2,1)S(1)}, u32[]{:S(2)}, u32[]{:S(2)}) async-start(bf16[32,64,128]{2,1,0:T(8,128)(2,1)} %param.7), calls=%async_computation.1 | async-start | bytes 1048576 | tf_op jit(solution)/shard_map/all_to_all | solution.py:97
  29.9 15.3 %all-to-all-done.1 = bf16[32,64,128]{2,1,0:T(8,128)(2,1)S(1)} async-done(((bf16[32,64,128]{2,1,0:T(8,128)(2,1)}), bf16[32,64,128]{2,1,0:T(8,128)(2,1)S(1)}, u32[]{:S(2)}, u32[]{:S(2)}) %all-to-all-start.1) | async-done | bytes 524320 | tf_op jit(solution)/shard_map/all_to_all | solution.py:97
  45.7 2.9 %fusion.121 = (bf16[8,256,128]{2,1,0:T(8,128)(2,1)}, bf16[8,256,128]{2,1,0:T(8,128)(2,1)S(1)}, bf16[8,256,128]{2,1,0:T(8,128)(2,1)S(1)}, bf16[8,256,128]{2,1,0:T...) fusion(bf16[24,272,128]{2,1,0:T(8,128)(2,1)S(1)} %maximum_selec, ...), kind=kLoop, calls=%fused_computation.207 | loop fusion | bytes 15728640 | tf_op jit(solution)/shard_map/slice | solution.py:35
  48.6 4.0 %fusion.120 = (bf16[8,256,128]{2,1,0:T(8,128)(2,1)}, bf16[8,256,128]{2,1,0:T(8,128)(2,1)}, bf16[8,256,128]{2,1,0:T(8,128)(2,1)}, bf16[8,256,128]{2,1,0:T(8,128)(...) fusion(bf16[24,272,128]{2,1,0:T(8,128)(2,1)S(1)} %maximum_selec, ...), kind=kLoop, calls=%fused_computation.206 | loop fusion | bytes 19922944 | tf_op jit(solution)/shard_map/slice | solution.py:35
  57.1 1.8 convolution_bitcast_fusion.11
  58.9 1.1 reshape.336
  62.7 1.8 convolution_bitcast_fusion.12
  64.5 1.1 reshape.332
  68.3 1.8 convolution_bitcast_fusion.13
  70.2 1.1 reshape.328
  74.0 1.8 convolution_bitcast_fusion.14
  75.8 1.1 reshape.324
  79.6 1.8 convolution_bitcast_fusion.15
  81.4 1.1 reshape.320
  85.2 1.8 convolution_bitcast_fusion.16
  90.9 1.8 convolution_bitcast_fusion
  94.8 1.8 convolution_bitcast_fusion.9
  97.8 1.7 pad.63
  99.5 1.7 reshape.345
  104.0 1.8 convolution_bitcast_fusion.1
  105.9 1.1 reshape.376
  109.6 1.8 convolution_bitcast_fusion.2
  111.5 1.1 reshape.372
  115.3 1.8 convolution_bitcast_fusion.3
  117.1 1.1 reshape.368
  120.9 1.8 convolution_bitcast_fusion.4
  122.8 1.1 reshape.364
  126.6 1.8 convolution_bitcast_fusion.5
  128.4 1.1 reshape.360
  132.2 1.8 convolution_bitcast_fusion.6
  134.1 1.1 reshape.356
  137.9 1.7 convolution_bitcast_fusion.7
  143.6 1.7 reshape.349
  155.8 5.8 %collective-permute-start.5 = (bf16[8,1,256]{2,1,0:T(2,128)(2,1)S(1)}, bf16[8,1,256]{2,1,0:T(2,128)(2,1)S(1)}, u32[]{:S(2)}, u32[]{:S(2)}) collective-permute-start(bf16[8,1,256]{2,1,0:T(2,128)(2,1)S(1)} %get-tuple-element.60), channel_id=1, source_target_pairs={{4,0},{8,4},{12,8},{16,12},{20,16},{24,20},{28,24},{32,28},{36,32}... | collective-permute-start | bytes 12296 | tf_op jit(solution)/shard_map/ppermute | solution.py:18
  162.6 3.8 %collective-permute-start.6 = (bf16[1,258,256]{2,1,0:T(8,128)(2,1)S(1)}, bf16[1,258,256]{2,1,0:T(8,128)(2,1)S(1)}, u32[]{:S(2)}, u32[]{:S(2)}) collective-permute-start(bf16[1,258,256]{2,1,0:T(8,128)(2,1)S(1)} %get-tuple-element.57), channel_id=1, source_target_pairs={{0,1},{1,2},{2,3},{3,0},{4,5},{5,6},{6,7},{7,4},{8,9},{9,10},{10,1... | collective-permute-start | bytes 396296 | tf_op jit(solution)/shard_map/ppermute | solution.py:16
  166.6 3.2 %collective-permute-done.6 = bf16[1,258,256]{2,1,0:T(8,128)(2,1)S(1)} collective-permute-done((bf16[1,258,256]{2,1,0:T(8,128)(2,1)S(1)}, bf16[1,258,256]{2,1,0:T(8,128)(2,1)S(1)}, u32[]{:S(2)}, u32[]{:S(2)}) %collective-permute-start.6) | collective-permute-done | bytes 132128 | tf_op jit(solution)/shard_map/ppermute | solution.py:16
  169.8 2.6 %collective-permute-done.7 = bf16[1,258,256]{2,1,0:T(8,128)(2,1)S(1)} collective-permute-done((bf16[1,258,256]{2,1,0:T(8,128)(2,1)S(1)}, bf16[1,258,256]{2,1,0:T(8,128)(2,1)S(1)}, u32[]{:S(2)}, u32[]{:S(2)}) %collective-permute-start.7) | collective-permute-done | bytes 132128 | tf_op jit(solution)/shard_map/ppermute | solution.py:18
  173.0 1.7 fusion.122
  179.6 5.7 %collective-permute-start.9 = (bf16[8,1,128]{2,1,0:T(2,128)(2,1)S(1)}, bf16[8,1,128]{2,1,0:T(2,128)(2,1)S(1)}, u32[]{:S(2)}, u32[]{:S(2)}) collective-permute-start(bf16[8,1,128]{2,1,0:T(2,128)(2,1)S(1)} %get-tuple-element.64), channel_id=1, source_target_pairs={{4,0},{8,4},{12,8},{16,12},{20,16},{24,20},{28,24},{32,28},{36,32}... | collective-permute-start | bytes 6152 | tf_op jit(solution)/shard_map/ppermute | solution.py:18
  186.3 2.6 %collective-permute-start.10 = (bf16[1,258,128]{2,1,0:T(8,128)(2,1)S(1)}, bf16[1,258,128]{2,1,0:T(8,128)(2,1)S(1)}, u32[]{:S(2)}, u32[]{:S(2)}) collective-permute-start(bf16[1,258,128]{2,1,0:T(8,128)(2,1)S(1)} %get-tuple-element.61), channel_id=1, source_target_pairs={{0,1},{1,2},{2,3},{3,0},{4,5},{5,6},{6,7},{7,4},{8,9},{9,10},{10,1... | collective-permute-start | bytes 198152 | tf_op jit(solution)/shard_map/ppermute | solution.py:16
  189.0 1.8 collective-permute-done.10
  190.8 3.3 %collective-permute-done.11 = bf16[1,258,128]{2,1,0:T(8,128)(2,1)S(1)} collective-permute-done((bf16[1,258,128]{2,1,0:T(8,128)(2,1)S(1)}, bf16[1,258,128]{2,1,0:T(8,128)(2,1)S(1)}, u32[]{:S(2)}, u32[]{:S(2)}) %collective-permute-start.11) | collective-permute-done | bytes 66080 | tf_op jit(solution)/shard_map/ppermute | solution.py:18
  194.3 2.4 %pad_maximum_fusion = (bf16[8,256,256]{2,1,0:T(8,128)(2,1)S(1)}, bf16[8,256,256]{2,1,0:T(8,128)(2,1)S(1)}, bf16[8,256,256]{2,1,0:T(8,128)(2,1)S(1)}, bf16[8,256,...) fusion(bf16[10,258,128]{2,1,0:T(8,128)(2,1)S(1)} %slice.517, ...), kind=kLoop, calls=%fused_computation.66 | loop fusion | flops 18874368 | bytes 10758144 | tf_op jit(solution)/shard_map/concatenate | solution.py:116
  200.7 1.2 fusion.2
  (153 shorter events, 72.2 us)
Async XLA Ops:
  0.0 155.0 %copy-start = (bf16[289,128]{1,0:T(8,128)(2,1)S(1)}, bf16[289,128]{1,0:T(8,128)(2,1)}, u32[]{:S(2)}) copy-start(bf16[289,128]{1,0:T(8,128)(2,1)} %param.10) | copy-start | bytes 221956
  16.2 6.9 %collective-permute-start = (bf16[8,8,128]{2,1,0:T(8,128)(2,1)S(1)}, bf16[8,8,128]{2,1,0:T(8,128)(2,1)S(1)}, u32[]{:S(2)}, u32[]{:S(2)}) collective-permute-start(bf16[8,8,128]{2,1,0:T(8,128)(2,1)S(1)} %get-tuple-element.65), channel_id=1, source_target_pairs={{0,4},{4,8},{8,12},{12,16},{16,20},{20,24},{24,28},{28,32},{32,36}... | collective-permute-start | bytes 49160 | tf_op jit(solution)/shard_map/ppermute | solution.py:16
  17.0 6.1 %collective-permute-start.1 = (bf16[8,8,128]{2,1,0:T(8,128)(2,1)S(1)}, bf16[8,8,128]{2,1,0:T(8,128)(2,1)S(1)}, u32[]{:S(2)}, u32[]{:S(2)}) collective-permute-start(bf16[8,8,128]{2,1,0:T(8,128)(2,1)S(1)} %get-tuple-element.66), channel_id=1, source_target_pairs={{4,0},{8,4},{12,8},{16,12},{20,16},{24,20},{28,24},{32,28},{36,32}... | collective-permute-start | bytes 49160 | tf_op jit(solution)/shard_map/ppermute | solution.py:18
  23.1 22.2 %collective-permute-start.3 = (bf16[8,272,128]{2,1,0:T(8,128)(2,1)S(1)}, bf16[8,272,128]{2,1,0:T(8,128)(2,1)S(1)}, u32[]{:S(2)}, u32[]{:S(2)}) collective-permute-start(bf16[8,272,128]{2,1,0:T(8,128)(2,1)S(1)} %pad_maximum_fusion.1), channel_id=1, source_target_pairs={{1,0},{2,1},{3,2},{0,3},{5,4},{6,5},{7,6},{4,7},{9,8},{10,9},{11,1... | collective-permute-start | bytes 1671176 | tf_op jit(solution)/shard_map/ppermute | solution.py:18
  25.3 19.9 %collective-permute-start.2 = (bf16[8,272,128]{2,1,0:T(8,128)(2,1)S(1)}, bf16[8,272,128]{2,1,0:T(8,128)(2,1)S(1)}, u32[]{:S(2)}, u32[]{:S(2)}) collective-permute-start(bf16[8,272,128]{2,1,0:T(8,128)(2,1)S(1)} %pad_maximum_fusion.1), channel_id=1, source_target_pairs={{0,1},{1,2},{2,3},{3,0},{4,5},{5,6},{6,7},{7,4},{8,9},{9,10},{10,1... | collective-permute-start | bytes 1671176 | tf_op jit(solution)/shard_map/ppermute | solution.py:16
  26.4 18.8 %all-to-all-start.1 = ((bf16[32,64,128]{2,1,0:T(8,128)(2,1)}), bf16[32,64,128]{2,1,0:T(8,128)(2,1)S(1)}, u32[]{:S(2)}, u32[]{:S(2)}) async-start(bf16[32,64,128]{2,1,0:T(8,128)(2,1)} %param.7), calls=%async_computation.1 | async-start | bytes 1048576 | tf_op jit(solution)/shard_map/all_to_all | solution.py:97
  142.6 3.7 %copy-start.2 = (f32[8,256,17,17]{1,0,3,2:T(8,128)S(1)}, f32[8,256,17,17]{1,0,3,2:T(8,128)}, u32[]{:S(2)}) copy-start(f32[8,256,17,17]{1,0,3,2:T(8,128)} %constant_dynamic-update-slice_fusion.16) | copy-start | bytes 7102468
  146.3 7.5 %copy-start.12 = (f32[8,256,1,17]{1,0,3,2:T(8,128)S(1)}, f32[8,256,1,17]{1,0,3,2:T(8,128)}, u32[]{:S(2)}) copy-start(f32[8,256,1,17]{1,0,3,2:T(8,128)} %copy.59) | copy-start | bytes 417796
  146.3 7.5 %copy-start.11 = (f32[8,256,1,17]{1,0,3,2:T(8,128)S(1)}, f32[8,256,1,17]{1,0,3,2:T(8,128)}, u32[]{:S(2)}) copy-start(f32[8,256,1,17]{1,0,3,2:T(8,128)} %copy.60) | copy-start | bytes 417796
  146.3 7.6 %copy-start.10 = (f32[8,256,1,17]{1,0,3,2:T(8,128)S(1)}, f32[8,256,1,17]{1,0,3,2:T(8,128)}, u32[]{:S(2)}) copy-start(f32[8,256,1,17]{1,0,3,2:T(8,128)} %copy.61) | copy-start | bytes 417796
  146.3 7.6 %copy-start.9 = (f32[8,256,1,17]{1,0,3,2:T(8,128)S(1)}, f32[8,256,1,17]{1,0,3,2:T(8,128)}, u32[]{:S(2)}) copy-start(f32[8,256,1,17]{1,0,3,2:T(8,128)} %copy.62) | copy-start | bytes 417796
  146.3 7.6 %copy-start.8 = (f32[8,256,1,17]{1,0,3,2:T(8,128)S(1)}, f32[8,256,1,17]{1,0,3,2:T(8,128)}, u32[]{:S(2)}) copy-start(f32[8,256,1,17]{1,0,3,2:T(8,128)} %copy.63) | copy-start | bytes 417796
  146.3 7.6 %copy-start.7 = (f32[8,256,1,17]{1,0,3,2:T(8,128)S(1)}, f32[8,256,1,17]{1,0,3,2:T(8,128)}, u32[]{:S(2)}) copy-start(f32[8,256,1,17]{1,0,3,2:T(8,128)} %copy.64) | copy-start | bytes 417796
  146.3 7.7 %copy-start.6 = (f32[8,256,1,17]{1,0,3,2:T(8,128)S(1)}, f32[8,256,1,17]{1,0,3,2:T(8,128)}, u32[]{:S(2)}) copy-start(f32[8,256,1,17]{1,0,3,2:T(8,128)} %copy.65) | copy-start | bytes 417796
  146.3 7.7 %copy-start.5 = (f32[8,256,1,17]{1,0,3,2:T(8,128)S(1)}, f32[8,256,1,17]{1,0,3,2:T(8,128)}, u32[]{:S(2)}) copy-start(f32[8,256,1,17]{1,0,3,2:T(8,128)} %copy.66) | copy-start | bytes 417796
  154.6 1.1 copy-start.1
  155.0 11.5 %copy-start.13 = (f32[32]{0:T(128)S(1)}, f32[32]{0:T(128)}, u32[]{:S(2)}) copy-start(f32[32]{0:T(128)} %param.13) | copy-start | bytes 388
  155.7 6.8 %collective-permute-start.4 = (bf16[8,1,256]{2,1,0:T(2,128)(2,1)S(1)}, bf16[8,1,256]{2,1,0:T(2,128)(2,1)S(1)}, u32[]{:S(2)}, u32[]{:S(2)}) collective-permute-start(bf16[8,1,256]{2,1,0:T(2,128)(2,1)S(1)} %get-tuple-element.59), channel_id=1, source_target_pairs={{0,4},{4,8},{8,12},{12,16},{16,20},{20,24},{24,28},{28,32},{32,36}... | collective-permute-start | bytes 12296 | tf_op jit(solution)/shard_map/ppermute | solution.py:16
  155.8 6.7 %collective-permute-start.5 = (bf16[8,1,256]{2,1,0:T(2,128)(2,1)S(1)}, bf16[8,1,256]{2,1,0:T(2,128)(2,1)S(1)}, u32[]{:S(2)}, u32[]{:S(2)}) collective-permute-start(bf16[8,1,256]{2,1,0:T(2,128)(2,1)S(1)} %get-tuple-element.60), channel_id=1, source_target_pairs={{4,0},{8,4},{12,8},{16,12},{20,16},{24,20},{28,24},{32,28},{36,32}... | collective-permute-start | bytes 12296 | tf_op jit(solution)/shard_map/ppermute | solution.py:18
  162.6 7.2 %collective-permute-start.6 = (bf16[1,258,256]{2,1,0:T(8,128)(2,1)S(1)}, bf16[1,258,256]{2,1,0:T(8,128)(2,1)S(1)}, u32[]{:S(2)}, u32[]{:S(2)}) collective-permute-start(bf16[1,258,256]{2,1,0:T(8,128)(2,1)S(1)} %get-tuple-element.57), channel_id=1, source_target_pairs={{0,1},{1,2},{2,3},{3,0},{4,5},{5,6},{6,7},{7,4},{8,9},{9,10},{10,1... | collective-permute-start | bytes 396296 | tf_op jit(solution)/shard_map/ppermute | solution.py:16
  166.5 5.9 %collective-permute-start.7 = (bf16[1,258,256]{2,1,0:T(8,128)(2,1)S(1)}, bf16[1,258,256]{2,1,0:T(8,128)(2,1)S(1)}, u32[]{:S(2)}, u32[]{:S(2)}) collective-permute-start(bf16[1,258,256]{2,1,0:T(8,128)(2,1)S(1)} %get-tuple-element.58), channel_id=1, source_target_pairs={{1,0},{2,1},{3,2},{0,3},{5,4},{6,5},{7,6},{4,7},{9,8},{10,9},{11,1... | collective-permute-start | bytes 396296 | tf_op jit(solution)/shard_map/ppermute | solution.py:18
  173.0 1.7 copy-start.3
  179.5 6.7 %collective-permute-start.8 = (bf16[8,1,128]{2,1,0:T(2,128)(2,1)S(1)}, bf16[8,1,128]{2,1,0:T(2,128)(2,1)S(1)}, u32[]{:S(2)}, u32[]{:S(2)}) collective-permute-start(bf16[8,1,128]{2,1,0:T(2,128)(2,1)S(1)} %get-tuple-element.63), channel_id=1, source_target_pairs={{0,4},{4,8},{8,12},{12,16},{16,20},{20,24},{24,28},{28,32},{32,36}... | collective-permute-start | bytes 6152 | tf_op jit(solution)/shard_map/ppermute | solution.py:16
  179.6 6.7 %collective-permute-start.9 = (bf16[8,1,128]{2,1,0:T(2,128)(2,1)S(1)}, bf16[8,1,128]{2,1,0:T(2,128)(2,1)S(1)}, u32[]{:S(2)}, u32[]{:S(2)}) collective-permute-start(bf16[8,1,128]{2,1,0:T(2,128)(2,1)S(1)} %get-tuple-element.64), channel_id=1, source_target_pairs={{4,0},{8,4},{12,8},{16,12},{20,16},{24,20},{28,24},{32,28},{36,32}... | collective-permute-start | bytes 6152 | tf_op jit(solution)/shard_map/ppermute | solution.py:18
  186.3 4.6 %collective-permute-start.10 = (bf16[1,258,128]{2,1,0:T(8,128)(2,1)S(1)}, bf16[1,258,128]{2,1,0:T(8,128)(2,1)S(1)}, u32[]{:S(2)}, u32[]{:S(2)}) collective-permute-start(bf16[1,258,128]{2,1,0:T(8,128)(2,1)S(1)} %get-tuple-element.61), channel_id=1, source_target_pairs={{0,1},{1,2},{2,3},{3,0},{4,5},{5,6},{6,7},{7,4},{8,9},{9,10},{10,1... | collective-permute-start | bytes 198152 | tf_op jit(solution)/shard_map/ppermute | solution.py:16
  188.9 5.2 %collective-permute-start.11 = (bf16[1,258,128]{2,1,0:T(8,128)(2,1)S(1)}, bf16[1,258,128]{2,1,0:T(8,128)(2,1)S(1)}, u32[]{:S(2)}, u32[]{:S(2)}) collective-permute-start(bf16[1,258,128]{2,1,0:T(8,128)(2,1)S(1)} %get-tuple-element.62), channel_id=1, source_target_pairs={{1,0},{2,1},{3,2},{0,3},{5,4},{6,5},{7,6},{4,7},{9,8},{10,9},{11,1... | collective-permute-start | bytes 198152 | tf_op jit(solution)/shard_map/ppermute | solution.py:18
  194.3 2.5 %copy-start.4 = (bf16[3,3,256,128]{3,2,1,0:T(8,128)(2,1)S(1)}, bf16[3,3,256,128]{3,2,1,0:T(8,128)(2,1)}, u32[]{:S(2)}) copy-start(bf16[3,3,256,128]{3,2,1,0:T(8,128)(2,1)} %param.12) | copy-start | bytes 1769476
where the time goes:
time: 206 us; the launch traced here: 202 us
  local copies, waits for them, and re-layouts  81.7 us (40%)
  matrix products  37.3 us (18%)
  starting transfers between devices  30.6 us (15%)
  waiting for transfers between devices  29.3 us (14%)
  blocking collectives  16.1 us (8%)
  other arithmetic  6.1 us (3%)
    dot_general x17, matrix products, correlate_block(): jnp.einsum('rgjc,rgkc->rgjk', first_groups, strip_groups, preferred_eleme...  28.8 us
    ppermute x6, starting transfers between devices, extended_2(): lax.ppermute(head, axis, [((i + 1) % count, i) for i in range(count)])  18.6 us
    reshape x17, local copies, waits for them, and re-layouts, correlate_block(): flat = banded.reshape(height, groups, group * extended)  17.4 us
    another operation x18, local copies, waits for them, and re-layouts, correlate_block(): stacked = jnp.stack(planes, axis=2)  16.4 us
    all_to_all x1, blocking collectives, body(): lax.all_to_all(second_features, 'lat', split_axis=0, concat_axis=1, tiled...  16.1 us
    pad x17, local copies, waits for them, and re-layouts, correlate_block(): flat = jnp.pad(flat, ((0, 0), (0, 0), (0, group)))  16.1 us
    all_to_all x1, waiting for transfers between devices, body(): lax.all_to_all(first_features, 'lat', split_axis=0, concat_axis=1, tiled=...  15.3 us
    reshape x17, local copies, waits for them, and re-layouts, correlate_block(): flat.reshape(height, groups, group, extended + 1)[:, :, :, :window_size]  14.2 us
  transfers between devices with their start and end apart: 13, of which 8 were waited for; matrix products, arithmetic and copies ran while one was open for 0% of the time, Pallas kernels for 0%

commit v1 on v0

v1 whole, which is shorter than its diff:
```python
import jax
import jax.numpy as jnp
from jax import lax
from jax.experimental import pallas as pl
from jax.experimental.pallas import tpu as pltpu
from jax.sharding import PartitionSpec as P

RADIUS, WIN = 8, 17
G, S = 16, 5
BF, F32 = jnp.bfloat16, jnp.float32
NT = (((1,), (1,)), ((), ()))
BOTH = ("lon", "lat")
VM = pl.BlockSpec(memory_space=pltpu.VMEM)
SM = pl.BlockSpec(memory_space=pltpu.SMEM)


def widen(encoder_weight):
    w = encoder_weight.reshape(WIN, WIN, -1)[:, ::-1]
    w = jnp.pad(w, ((7, 7), (15, 0), (0, 0)))
    return w.reshape(31 * 32, -1)


def mirror(x):
    n = x.shape[0] // 8
    ids = 7 - lax.broadcasted_iota(jnp.int32, (8, 128), 0)
    tiles = [
        jnp.take_along_axis(x[8 * k : 8 * k + 8], ids, axis=0, mode="promise_in_bounds")
        for k in reversed(range(n))
    ]
    return jnp.concatenate(tiles, axis=0)


def correlate_kernel(t_ref, f_ref, s_ref, left_ref, right_ref, w_ref, o0, o1, o2, o3, fe, se, hal, band, acc):
    rows = f_ref.shape[0]
    blocks = rows // 8
    scale = 128**-0.5
    pad = jnp.zeros((16, 128), F32)
    for n, ref in enumerate((left_ref, right_ref)):
        hal[n, 0:16] = pad
        hal[n, 16:400] = ref[...].astype(F32)
    fpad = jnp.zeros((8, 128), F32)
    for r in range(rows):
        fe[r, 0:8] = fpad
        fe[r, 72:80] = fpad
        fe[r, 8:72] = f_ref[r].astype(F32)
        fe[r, 6:8] = hal[0, 336 + 2 * r : 338 + 2 * r]
        fe[r, 72:74] = hal[1, 336 + 2 * r : 338 + 2 * r]
        se[r, 16:80] = mirror(s_ref[r].astype(F32)).astype(BF)
        se[r, 80:96] = mirror(hal[0, 10 + 10 * r : 26 + 10 * r]).astype(BF)
        se[r, 0:16] = mirror(hal[1, 16 + 10 * r : 32 + 10 * r]).astype(BF)
    for g in range(S):
        for b in range(blocks):
            lo, hi = max(0, 8 * b - 8), min(rows, 8 * b + 16)
            keys = se[8 * b : 8 * b + 8, 64 - G * g : 96 - G * g, :].reshape(256, 128)
            query = fe[lo:hi, G * g : G * g + G, :].reshape((hi - lo) * G, 128).astype(BF)
            c = lax.dot_general(query, keys, NT, preferred_element_type=F32)
            c = (c * scale).reshape(hi - lo, G, 256)
            for h in range(2):
                part = pltpu.roll(c[:, :, 128 * h : 128 * h + 128], 0, 2, stride=1, stride_axis=1)
                band[b, lo - 8 * b + 8 : hi - 8 * b + 8, G * g : G * g + G, 128 * h : 128 * h + 128] = part.astype(BF)
    done = set()
    for d in range(-8, 16):
        bs = [b for b in range(blocks) if 0 <= 8 * b + d < rows]
        b0, b1 = bs[0], bs[-1] + 1
        lhs = band[b0:b1, d + 8].reshape((b1 - b0) * S * G, 256)
        o = 15 - d
        part = jnp.dot(lhs, w_ref[32 * o : 32 * o + 256, :], preferred_element_type=F32)
        part = part.reshape(b1 - b0, S * G, 128)
        for n, b in enumerate(bs):
            i = 8 * b + d
            if i in done:
                acc[i + 2] += part[n]
            else:
                acc[i + 2] = part[n]
                done.add(i)
    zero = jnp.zeros((2, S * G, 128), F32)
    acc[0:2] = zero
    acc[rows + 2 : rows + 4] = zero
    t = t_ref[0]
    for k, out in enumerate((o0, o1, o2, o3)):
        base = 8 * (t ^ k)
        edges = []
        for r in range(12):
            m = jnp.maximum(acc[base + r], 0.0)
            out[64 * r : 64 * r + 64, :] = m[8:72].astype(BF)
            edges.append(jnp.where(t == 0, m[6:8], m[72:74]))
        edges.append(jnp.zeros((8, 128), F32))
        out[768:800, :] = jnp.concatenate(edges, axis=0).astype(BF)


def correlate(t, f, s, left, right, w_wide):
    piece = jax.ShapeDtypeStruct((800, 128), BF)
    return pl.pallas_call(
        correlate_kernel,
        out_shape=(piece,) * 4,
        in_specs=[SM] + [VM] * 5,
        out_specs=(VM,) * 4,
        scratch_shapes=[
            pltpu.VMEM((32, 80, 128), F32),
            pltpu.VMEM((32, 96, 128), BF),
            pltpu.VMEM((2, 400, 128), F32),
            pltpu.VMEM((4, 24, S * G, 256), BF),
            pltpu.VMEM((36, S * G, 128), F32),
        ],
        compiler_params=pltpu.CompilerParams(vmem_limit_bytes=40 << 20),
        name="correlate",
    )(t, f, s, left, right, w_wide)


def gru_kernel(t_ref, metric_ref, h_ref, hl_ref, hr_ref, top_ref, bot_ref, m0, m1, m2, m3, gw_ref, cw_ref, out_ref, hf, mf, x, m3s, rf, r, ug):
    t = t_ref[0]
    for n, ref in ((0, top_ref), (10, bot_ref)):
        for i in range(2):
            hf[n + i, 0:272] = ref[272 * i : 272 * i + 272].astype(F32)
    hl, hr = hl_ref[...].astype(F32), hr_ref[...].astype(F32)
    for i in range(8):
        hf[2 + i, 2:258] = h_ref[i].astype(F32)
        hf[2 + i, 0:2] = hl[2 * i : 2 * i + 2]
        hf[2 + i, 258:260] = hr[2 * i : 2 * i + 2]
    for k, m in enumerate((m0, m1, m2, m3)):
        s = t ^ k
        for i in range(12):
            mf[i, pl.ds(2 + 64 * s, 64)] = m[64 * i : 64 * i + 64].astype(F32)
    for k, m in enumerate((m0, m1, m2, m3)):
        s = t ^ k

        @pl.when((s == 0) | (s == 3))
        def _(m=m, s=s):
            e = m[768:800].astype(F32)
            at = jnp.where(s == 0, 0, 258)
            for i in range(12):
                mf[i, pl.ds(at, 2)] = e[2 * i : 2 * i + 2]

    for q in range(3):
        for i in range(12):
            x[q, i, :, 0:128] = hf[i, q : q + 272].astype(BF)
            x[q, i, :, 128:256] = mf[i, q : q + 272].astype(BF)
    for i in range(12):
        m3s[i] = mf[i, 3:259].astype(BF)
    sides_w = jnp.concatenate([gw_ref[p, q] for q in (0, 2) for p in range(3)], axis=0)
    center_w = jnp.concatenate([gw_ref[p, 1] for p in range(3)], axis=0)
    for i in range(10):
        lhs = jnp.concatenate([x[q, i + p] for q in (0, 2) for p in range(3)], axis=1)
        sides = jnp.dot(lhs, sides_w, preferred_element_type=F32)
        lhs = jnp.concatenate([x[1, i + p] for p in range(3)], axis=1)
        center = jnp.dot(lhs, center_w, preferred_element_type=F32)
        gate = center + sides * metric_ref[8 * t + i]
        gate = 0.5 * jnp.tanh(0.5 * gate) + 0.5
        rf[i, 0:272] = gate[:, 128:] * hf[i + 1, 1:273]
        if 1 <= i < 9:
            ug[i - 1] = gate[:, 0:128]
    for q in range(3):
        for i in range(10):
            r[q, i] = rf[i, q : q + 256].astype(BF)
    zero = jnp.zeros((256, 128), BF)

    def pair(rr, q):
        first = cw_ref[rr, q] if rr < 3 else zero
        second = cw_ref[rr - 1, q] if rr > 0 else zero
        return jnp.concatenate([first, second], axis=1)

    sides_w = jnp.concatenate([pair(rr, q) for q in (0, 2) for rr in range(4)], axis=0)
    center_w = jnp.concatenate([pair(rr, 1) for rr in range(4)], axis=0)

    def taps(q, row):
        mm = m3s[row + 1] if q == 2 else x[q + 1, row + 1, 0:256, 128:256]
        return [r[q, row], mm]

    for i in range(0, 8, 2):
        lhs = jnp.concatenate(sum([taps(q, i + rr) for q in (0, 2) for rr in range(4)], []), axis=1)
        sides = jnp.dot(lhs, sides_w, preferred_element_type=F32)
        lhs = jnp.concatenate(sum([taps(1, i + rr) for rr in range(4)], []), axis=1)
        center = jnp.dot(lhs, center_w, preferred_element_type=F32)
        for n in range(2):
            part = slice(128 * n, 128 * n + 128)
            cand = jnp.tanh(center[:, part] + sides[:, part] * metric_ref[8 * t + i + n + 1])
            u = ug[i + n, 1:257]
            h = hf[i + n + 2, 2:258]
            out_ref[i + n] = ((1.0 - u) * h + u * cand).astype(BF)


def gru(t, metric, h, hl, hr, top, bot, ms, gw, cw):
    return pl.pallas_call(
        gru_kernel,
        out_shape=jax.ShapeDtypeStruct((8, 256, 128), BF),
        in_specs=[SM, SM] + [VM] * 11,
        out_specs=VM,
        scratch_shapes=[
            pltpu.VMEM((12, 280, 128), F32),
            pltpu.VMEM((12, 280, 128), F32),
            pltpu.VMEM((3, 12, 272, 256), BF),
            pltpu.VMEM((12, 256, 128), BF),
            pltpu.VMEM((10, 272, 128), F32),
            pltpu.VMEM((3, 10, 256, 128), BF),
            pltpu.VMEM((8, 272, 128), F32),
        ],
        compiler_params=pltpu.CompilerParams(vmem_limit_bytes=40 << 20),
        name="gru",
    )(t, metric, h, hl, hr, top, bot, *ms, gw, cw)


def body(first, second, hidden, encoder_weight, gates_weight, candidate_weight, row_metric):
    t = lax.axis_index("lat").astype(jnp.int32)[None]
    slabs = lax.axis_size("lon") * lax.axis_size("lat")
    up = [(i, (i + 1) % slabs) for i in range(slabs)]
    down = [((i + 1) % slabs, i) for i in range(slabs)]
    count = lax.axis_size("lon")
    east = [(i, (i + 1) % count) for i in range(count)]
    west = [((i + 1) % count, i) for i in range(count)]

    def rim(s, f):
        return jnp.concatenate([s.reshape(-1, 128), f.reshape(-1, 128)], axis=0)

    left = lax.ppermute(rim(second[:, 54:], first[:, 62:]), BOTH, up)
    right = lax.ppermute(rim(second[:, :10], first[:, :2]), BOTH, down)
    hl = lax.ppermute(hidden[:, 254:].reshape(16, 128), "lon", east)
    hr = lax.ppermute(hidden[:, :2].reshape(16, 128), "lon", west)
    pieces = correlate(t, first, second, left, right, widen(encoder_weight))

    def rows(a):
        wide = jnp.concatenate([hl.reshape(8, 2, 128)[a : a + 2], hidden[a : a + 2], hr.reshape(8, 2, 128)[a : a + 2]], axis=1)
        return jnp.pad(wide, ((0, 0), (0, 12), (0, 0))).reshape(544, 128)

    top = lax.ppermute(rows(6), "lat", [(0, 1), (1, 2), (2, 3)])
    bot = lax.ppermute(rows(0), "lat", [(1, 0), (2, 1), (3, 2)])
    ms = [pieces[0]] + [lax.ppermute(pieces[k], "lat", [(i, i ^ k) for i in range(4)]) for k in (1, 2, 3)]
    metric = jnp.pad(row_metric, (1, 1))
    return gru(t, metric, hidden, hl, hr, top, bot, ms, gates_weight, candidate_weight)


def solution(mesh):
    return jax.shard_map(
        body,
        mesh=mesh,
        in_specs=(
            P(None, BOTH, None),
            P(None, BOTH, None),
            P("lat", "lon", None),
            P(),
            P(),
            P(),
            P(),
        ),
        out_specs=P("lat", "lon", None),
        check_vma=False,
    )
```

time: 206 us -> 45.4 us (0.22); the launches traced: 202 us -> 45.2 us
  local copies, waits for them, and re-layouts: 81.7 us -> 3.12 us
  matrix products: 37.3 us -> 0 us
  waiting for transfers between devices: 29.3 us -> 9.64 us
  blocking collectives: 16.1 us -> 0 us
  Pallas kernels: 0 us -> 9.29 us
  starting transfers between devices: 30.6 us -> 22.8 us
  other arithmetic: 6.1 us -> 0.11 us
    dot_general x36 -> x0, matrix products: 37.3 us -> none  [the longest x17 28.8 us: correlate_block(): jnp.einsum('rgjc,rgkc->rgjk', first_groups, strip_groups, preferred_eleme...]
    reshape x34 -> x3, local copies, waits for them, and re-layouts: 31.6 us -> 0.11 us  [the longest x2 0.07 us: rim(): return jnp.concatenate([s.reshape(-1, 128), f.reshape(-1, 128)], axis=0)]
    another operation x18 -> x0, local copies, waits for them, and re-layouts: 16.4 us -> none  [correlate_block(): stacked = jnp.stack(planes, axis=2)]
    all_to_all x1 -> x0, blocking collectives: 16.1 us -> none  [body(): lax.all_to_all(second_features, 'lat', split_axis=0, concat_axis=1, tiled...]
    pad x17 -> x2, local copies, waits for them, and re-layouts: 16.1 us -> 0.12 us  [the longest x1 0.07 us: body(): metric = jnp.pad(row_metric, (1, 1))]
    all_to_all x1 -> x0, waiting for transfers between devices: 15.3 us -> none  [body(): lax.all_to_all(first_features, 'lat', split_axis=0, concat_axis=1, tiled=...]
    pallas_call x0 -> x2, Pallas kernels: none -> 9.29 us  [the longest x1 7.03 us: gru(): pl.pallas_call(gru_kernel, out_shape=jax.ShapeDtypeStruct((8, 256, 128),...]
    unnamed x46 -> x14, local copies, waits for them, and re-layouts: 8.69 us -> 0.04 us
  transfers between devices with their start and end apart: 13 -> 9, of which waited for: 8 -> 2; matrix products, arithmetic and copies ran while one was open for 0% -> 5% of each run, Pallas kernels for 0% -> 5%
where the time goes in v1:
time: 45.4 us; the launch traced here: 45.2 us
  starting transfers between devices  22.8 us (50%)
  waiting for transfers between devices  9.64 us (21%)
  Pallas kernels  9.29 us (20%)
  local copies, waits for them, and re-layouts  3.12 us (7%)
    ppermute x1, waiting for transfers between devices, body(): bot = lax.ppermute(rows(0), 'lat', [(1, 0), (2, 1), (3, 2)])  8.77 us
    pallas_call x1, Pallas kernels, gru(): pl.pallas_call(gru_kernel, out_shape=jax.ShapeDtypeStruct((8, 256, 128),...  7.03 us
    ppermute x1, starting transfers between devices, body(): top = lax.ppermute(rows(6), 'lat', [(0, 1), (1, 2), (2, 3)])  5.26 us
    ppermute x1, starting transfers between devices, body(): hr = lax.ppermute(hidden[:, :2].reshape(16, 128), 'lon', west)  4.73 us
    ppermute x1, starting transfers between devices, body(): left = lax.ppermute(rim(second[:, 54:], first[:, 62:]), BOTH, up)  4.21 us
    ppermute x3, starting transfers between devices, body(): lax.ppermute(pieces[k], 'lat', [(i, i ^ k) for i in range(4)])  3.93 us
    ppermute x1, starting transfers between devices, body(): hl = lax.ppermute(hidden[:, 254:].reshape(16, 128), 'lon', east)  2.54 us
    pallas_call x1, Pallas kernels, correlate(): pl.pallas_call(correlate_kernel, out_shape=(piece,) * 4, in_specs=[SM] +...  2.26 us
  transfers between devices with their start and end apart: 9, of which 2 were waited for; matrix products, arithmetic and copies ran while one was open for 5% of the time, Pallas kernels for 5%

profile of v1, /device:TPU:1, one launch (start us, length us, event | category | flops | bytes accessed | tf_op | source)
XLA Modules:
  0.0 45.2 jit_solution(3669425247999489599)
XLA Ops:
  0.0 0.0 copy-start
  0.0 0.0 copy-start.5
  0.0 0.8 %fusion.13 = (bf16[8,2,128]{2,1,0:T(2,128)(2,1)S(1)}, bf16[8,2,128]{2,1,0:T(2,128)(2,1)S(1)}) fusion(bf16[8,256,128]{2,1,0:T(8,128)(2,1)} %h_ref.1), kind=kLoop, calls=%fused_computation.16 | loop fusion | bytes 16384 | tf_op jit(solution)/shard_map/slice | solution.py:217
  0.8 2.5 %collective-permute-start = (bf16[16,128]{1,0:T(8,128)(2,1)S(1)}, bf16[16,128]{1,0:T(8,128)(2,1)S(1)}, u32[]{:S(2)}, u32[]{:S(2)}) collective-permute-start(bf16[16,128]{1,0:T(8,128)(2,1)S(1)} %bitcast.22), channel_id=1, source_target_pairs={{0,4},{4,8},{8,12},{12,16},{16,20},{20,24},{24,28},{28,32},{32,36}... | collective-permute-start | bytes 12296 | tf_op jit(solution)/shard_map/ppermute | solution.py:216
  3.3 4.7 %collective-permute-start.1 = (bf16[16,128]{1,0:T(8,128)(2,1)S(1)}, bf16[16,128]{1,0:T(8,128)(2,1)S(1)}, u32[]{:S(2)}, u32[]{:S(2)}) collective-permute-start(bf16[16,128]{1,0:T(8,128)(2,1)S(1)} %bitcast.21), channel_id=1, source_target_pairs={{4,0},{8,4},{12,8},{16,12},{20,16},{24,20},{28,24},{32,28},{36,32}... | collective-permute-start | bytes 12296 | tf_op jit(solution)/shard_map/ppermute | solution.py:217
  8.1 0.9 %fusion.11 = (bf16[32,2,128]{2,1,0:T(2,128)(2,1)S(1)}, bf16[32,2,128]{2,1,0:T(2,128)(2,1)S(1)}) fusion(bf16[32,64,128]{2,1,0:T(8,128)(2,1)} %f_ref.1), kind=kLoop, calls=%fused_computation.14 | loop fusion | bytes 65536 | tf_op jit(solution)/shard_map/slice | solution.py:215
  9.0 1.0 %fusion.10 = (bf16[32,10,128]{2,1,0:T(8,128)(2,1)S(1)}, bf16[32,10,128]{2,1,0:T(8,128)(2,1)S(1)}) fusion(bf16[32,64,128]{2,1,0:T(8,128)(2,1)} %s_ref.1), kind=kLoop, calls=%fused_computation.13 | loop fusion | bytes 327680 | tf_op jit(solution)/shard_map/slice | solution.py:215
  10.0 0.0 copy-start.1
  10.0 0.0 copy-start.3
  10.1 4.2 %collective-permute-start.4 = (bf16[384,128]{1,0:T(8,128)(2,1)S(1)}, bf16[384,128]{1,0:T(8,128)(2,1)S(1)}, u32[]{:S(2)}, u32[]{:S(2)}) collective-permute-start(bf16[384,128]{1,0:T(8,128)(2,1)S(1)} %pad_maximum_fusion), channel_id=1, source_target_pairs={{0,1},{1,2},{2,3},{3,4},{4,5},{5,6},{6,7},{7,8},{8,9},{9,10},{10,1... | collective-permute-start | bytes 294920 | tf_op jit(solution)/shard_map/ppermute | solution.py:214
  14.4 0.1 collective-permute-start.5
  14.4 0.0 copy-done
  14.5 0.0 copy-done.5
  14.5 0.1 rev.3
  14.6 0.0 copy-start.6
  14.6 0.0 copy-start.2
  14.6 0.0 copy-start.4
  14.7 0.0 collective-permute-done.hl_ref
  14.7 0.0 collective-permute-done.1.hr_ref
  14.8 5.3 %collective-permute-start.2 = (bf16[544,128]{1,0:T(8,128)(2,1)S(1)}, bf16[544,128]{1,0:T(8,128)(2,1)S(1)}, u32[]{:S(2)}, u32[]{:S(2)}) collective-permute-start(bf16[544,128]{1,0:T(8,128)(2,1)S(1)} %bitcast.13), channel_id=1, source_target_pairs={{0,1},{1,2},{2,3},{4,5},{5,6},{6,7},{8,9},{9,10},{10,11},{12,13},{... | collective-permute-start | bytes 417800 | tf_op jit(solution)/shard_map/ppermute | solution.py:224
  20.1 0.0 collective-permute-done.4.left_ref
  20.1 0.9 %collective-permute-done.5.right_ref = bf16[384,128]{1,0:T(8,128)(2,1)S(1)} collective-permute-done((bf16[384,128]{1,0:T(8,128)(2,1)S(1)}, bf16[384,128]{1,0:T(8,128)(2,1)S(1)}, u32[]{:S(2)}, u32[]{:S(2)}) %collective-permute-start.5) | collective-permute-done | bytes 98336 | tf_op jit(solution)/shard_map/ppermute | solution.py:215
  20.9 0.0 copy-done.1
  21.0 0.0 copy-done.3
  21.0 2.3 %correlate.1 = (bf16[800,128]{1,0:T(8,128)(2,1)S(1)}, bf16[800,128]{1,0:T(8,128)(2,1)S(1)}, bf16[800,128]{1,0:T(8,128)(2,1)S(1)}, bf16[800,128]{1,0:T(8,128)(2,1)S(1)}) custom-call(s32[1]{0:T(128)} %bitcast.t_ref, bf16[32,64,128]{2,1,0:T(8,128)(2,1)S(1)} %copy-done.3, bf16[32,64,128]{2,1,0:T(8,128)(2,1)S(1)} %copy-done.1, ...), custom_call_target="tpu_custom_call" | custom-call | tf_op jit(solution)/shard_map/correlate/pallas_call | solution.py:93
  23.2 0.7 %collective-permute-start.6 = (bf16[800,128]{1,0:T(8,128)(2,1)S(1)}, bf16[800,128]{1,0:T(8,128)(2,1)S(1)}, u32[]{:S(2)}, u32[]{:S(2)}) collective-permute-start(bf16[800,128]{1,0:T(8,128)(2,1)S(1)} %get-tuple-element.10), channel_id=1, source_target_pairs={{0,1},{1,0},{2,3},{3,2},{4,5},{5,4},{6,7},{7,6},{8,9},{9,8},{10,11... | collective-permute-start | bytes 614408 | tf_op jit(solution)/shard_map/ppermute | solution.py:226
  23.9 0.0 collective-permute-start.7
  23.9 3.2 %collective-permute-start.8 = (bf16[800,128]{1,0:T(8,128)(2,1)S(1)}, bf16[800,128]{1,0:T(8,128)(2,1)S(1)}, u32[]{:S(2)}, u32[]{:S(2)}) collective-permute-start(bf16[800,128]{1,0:T(8,128)(2,1)S(1)} %get-tuple-element.12), channel_id=1, source_target_pairs={{0,3},{1,2},{2,1},{3,0},{4,7},{5,6},{6,5},{7,4},{8,11},{9,10},{10,... | collective-permute-start | bytes 614408 | tf_op jit(solution)/shard_map/ppermute | solution.py:226
  27.2 2.1 %collective-permute-start.3 = (bf16[544,128]{1,0:T(8,128)(2,1)S(1)}, bf16[544,128]{1,0:T(8,128)(2,1)S(1)}, u32[]{:S(2)}, u32[]{:S(2)}) collective-permute-start(bf16[544,128]{1,0:T(8,128)(2,1)S(1)} %bitcast.14), channel_id=1, source_target_pairs={{1,0},{2,1},{3,2},{5,4},{6,5},{7,6},{9,8},{10,9},{11,10},{13,12},{... | collective-permute-start | bytes 417800 | tf_op jit(solution)/shard_map/ppermute | solution.py:225
  29.3 0.0 copy-done.6
  29.3 0.1 pad.15.metric_ref
  29.4 0.0 collective-permute-done.2.top_ref
  29.4 8.8 %collective-permute-done.3.bot_ref = bf16[544,128]{1,0:T(8,128)(2,1)S(1)} collective-permute-done((bf16[544,128]{1,0:T(8,128)(2,1)S(1)}, bf16[544,128]{1,0:T(8,128)(2,1)S(1)}, u32[]{:S(2)}, u32[]{:S(2)}) %collective-permute-start.3) | collective-permute-done | bytes 139296 | tf_op jit(solution)/shard_map/ppermute | solution.py:225
  38.1 0.0 collective-permute-done.6.m1
  38.1 0.0 collective-permute-done.7.m2
  38.1 0.0 collective-permute-done.8.m3
  38.1 0.0 copy-done.2
  38.1 0.0 copy-done.4
  38.2 7.0 %gru.1 = bf16[8,256,128]{2,1,0:T(8,128)(2,1)} custom-call(s32[1]{0:T(128)} %bitcast.t_ref, f32[34]{0:T(128)S(1)} %pad.15.metric_ref, bf16[8,256,128]{2,1,0:T(8,128)(2,1)S(1)} %copy-done, bf16[16,128]{1,0:T(8,128)(2,1)S(1)} %collective-permute-done.hl_ref, bf16[16,128]{1,0:T(8,128)(2,1)S(1)} %collective-permute-done.1.hr_ref, ...), custom_call_target="tpu_custom_call" | custom-call | tf_op jit(solution)/shard_map/gru/pallas_call | solution.py:183
  (11 shorter events, 0.3 us)
Async XLA Ops:
  0.0 14.4 %copy-start = (bf16[8,256,128]{2,1,0:T(8,128)(2,1)S(1)}, bf16[8,256,128]{2,1,0:T(8,128)(2,1)}, u32[]{:S(2)}) copy-start(bf16[8,256,128]{2,1,0:T(8,128)(2,1)} %h_ref.1) | copy-start | bytes 1572868
  0.0 14.5 %copy-start.5 = (bf16[289,128]{1,0:T(8,128)(2,1)S(1)}, bf16[289,128]{1,0:T(8,128)(2,1)}, u32[]{:S(2)}) copy-start(bf16[289,128]{1,0:T(8,128)(2,1)} %param.10) | copy-start | bytes 221956
  0.8 13.9 %collective-permute-start = (bf16[16,128]{1,0:T(8,128)(2,1)S(1)}, bf16[16,128]{1,0:T(8,128)(2,1)S(1)}, u32[]{:S(2)}, u32[]{:S(2)}) collective-permute-start(bf16[16,128]{1,0:T(8,128)(2,1)S(1)} %bitcast.22), channel_id=1, source_target_pairs={{0,4},{4,8},{8,12},{12,16},{16,20},{20,24},{24,28},{28,32},{32,36}... | collective-permute-start | bytes 12296 | tf_op jit(solution)/shard_map/ppermute | solution.py:216
  3.3 11.4 %collective-permute-start.1 = (bf16[16,128]{1,0:T(8,128)(2,1)S(1)}, bf16[16,128]{1,0:T(8,128)(2,1)S(1)}, u32[]{:S(2)}, u32[]{:S(2)}) collective-permute-start(bf16[16,128]{1,0:T(8,128)(2,1)S(1)} %bitcast.21), channel_id=1, source_target_pairs={{4,0},{8,4},{12,8},{16,12},{20,16},{24,20},{28,24},{32,28},{36,32}... | collective-permute-start | bytes 12296 | tf_op jit(solution)/shard_map/ppermute | solution.py:217
  10.0 10.9 %copy-start.1 = (bf16[32,64,128]{2,1,0:T(8,128)(2,1)S(1)}, bf16[32,64,128]{2,1,0:T(8,128)(2,1)}, u32[]{:S(2)}) copy-start(bf16[32,64,128]{2,1,0:T(8,128)(2,1)} %s_ref.1) | copy-start | bytes 1572868
  10.0 10.9 %copy-start.3 = (bf16[32,64,128]{2,1,0:T(8,128)(2,1)S(1)}, bf16[32,64,128]{2,1,0:T(8,128)(2,1)}, u32[]{:S(2)}) copy-start(bf16[32,64,128]{2,1,0:T(8,128)(2,1)} %f_ref.1) | copy-start | bytes 1572868
  10.1 10.0 %collective-permute-start.4 = (bf16[384,128]{1,0:T(8,128)(2,1)S(1)}, bf16[384,128]{1,0:T(8,128)(2,1)S(1)}, u32[]{:S(2)}, u32[]{:S(2)}) collective-permute-start(bf16[384,128]{1,0:T(8,128)(2,1)S(1)} %pad_maximum_fusion), channel_id=1, source_target_pairs={{0,1},{1,2},{2,3},{3,4},{4,5},{5,6},{6,7},{7,8},{8,9},{9,10},{10,1... | collective-permute-start | bytes 294920 | tf_op jit(solution)/shard_map/ppermute | solution.py:214
  14.4 6.6 %collective-permute-start.5 = (bf16[384,128]{1,0:T(8,128)(2,1)S(1)}, bf16[384,128]{1,0:T(8,128)(2,1)S(1)}, u32[]{:S(2)}, u32[]{:S(2)}) collective-permute-start(bf16[384,128]{1,0:T(8,128)(2,1)S(1)} %pad_maximum_fusion.1), channel_id=1, source_target_pairs={{1,0},{2,1},{3,2},{4,3},{5,4},{6,5},{7,6},{8,7},{9,8},{10,9},{11,1... | collective-permute-start | bytes 294920 | tf_op jit(solution)/shard_map/ppermute | solution.py:215
  14.6 14.6 %copy-start.6 = (f32[32]{0:T(128)S(1)}, f32[32]{0:T(128)}, u32[]{:S(2)}) copy-start(f32[32]{0:T(128)} %param.13) | copy-start | bytes 388
  14.6 23.5 %copy-start.2 = (bf16[3,3,256,256]{3,2,1,0:T(8,128)(2,1)S(1)}, bf16[3,3,256,256]{3,2,1,0:T(8,128)(2,1)}, u32[]{:S(2)}) copy-start(bf16[3,3,256,256]{3,2,1,0:T(8,128)(2,1)} %gw_ref.1) | copy-start | bytes 3538948
  14.6 23.5 %copy-start.4 = (bf16[3,3,256,128]{3,2,1,0:T(8,128)(2,1)S(1)}, bf16[3,3,256,128]{3,2,1,0:T(8,128)(2,1)}, u32[]{:S(2)}) copy-start(bf16[3,3,256,128]{3,2,1,0:T(8,128)(2,1)} %cw_ref.1) | copy-start | bytes 1769476
  14.8 14.5 %collective-permute-start.2 = (bf16[544,128]{1,0:T(8,128)(2,1)S(1)}, bf16[544,128]{1,0:T(8,128)(2,1)S(1)}, u32[]{:S(2)}, u32[]{:S(2)}) collective-permute-start(bf16[544,128]{1,0:T(8,128)(2,1)S(1)} %bitcast.13), channel_id=1, source_target_pairs={{0,1},{1,2},{2,3},{4,5},{5,6},{6,7},{8,9},{9,10},{10,11},{12,13},{... | collective-permute-start | bytes 417800 | tf_op jit(solution)/shard_map/ppermute | solution.py:224
  23.2 14.9 %collective-permute-start.6 = (bf16[800,128]{1,0:T(8,128)(2,1)S(1)}, bf16[800,128]{1,0:T(8,128)(2,1)S(1)}, u32[]{:S(2)}, u32[]{:S(2)}) collective-permute-start(bf16[800,128]{1,0:T(8,128)(2,1)S(1)} %get-tuple-element.10), channel_id=1, source_target_pairs={{0,1},{1,0},{2,3},{3,2},{4,5},{5,4},{6,7},{7,6},{8,9},{9,8},{10,11... | collective-permute-start | bytes 614408 | tf_op jit(solution)/shard_map/ppermute | solution.py:226
  23.9 14.2 %collective-permute-start.7 = (bf16[800,128]{1,0:T(8,128)(2,1)S(1)}, bf16[800,128]{1,0:T(8,128)(2,1)S(1)}, u32[]{:S(2)}, u32[]{:S(2)}) collective-permute-start(bf16[800,128]{1,0:T(8,128)(2,1)S(1)} %get-tuple-element.11), channel_id=1, source_target_pairs={{0,2},{1,3},{2,0},{3,1},{4,6},{5,7},{6,4},{7,5},{8,10},{9,11},{10,... | collective-permute-start | bytes 614408 | tf_op jit(solution)/shard_map/ppermute | solution.py:226
  23.9 14.2 %collective-permute-start.8 = (bf16[800,128]{1,0:T(8,128)(2,1)S(1)}, bf16[800,128]{1,0:T(8,128)(2,1)S(1)}, u32[]{:S(2)}, u32[]{:S(2)}) collective-permute-start(bf16[800,128]{1,0:T(8,128)(2,1)S(1)} %get-tuple-element.12), channel_id=1, source_target_pairs={{0,3},{1,2},{2,1},{3,0},{4,7},{5,6},{6,5},{7,4},{8,11},{9,10},{10,... | collective-permute-start | bytes 614408 | tf_op jit(solution)/shard_map/ppermute | solution.py:226
  27.2 10.9 %collective-permute-start.3 = (bf16[544,128]{1,0:T(8,128)(2,1)S(1)}, bf16[544,128]{1,0:T(8,128)(2,1)S(1)}, u32[]{:S(2)}, u32[]{:S(2)}) collective-permute-start(bf16[544,128]{1,0:T(8,128)(2,1)S(1)} %bitcast.14), channel_id=1, source_target_pairs={{1,0},{2,1},{3,2},{5,4},{6,5},{7,6},{9,8},{10,9},{11,10},{13,12},{... | collective-permute-start | bytes 417800 | tf_op jit(solution)/shard_map/ppermute | solution.py:225

commit v2 on v1

v2 whole, which is shorter than its diff:
```python
import functools

import jax
import jax.numpy as jnp
from jax import lax
from jax.experimental import pallas as pl
from jax.experimental.pallas import tpu as pltpu
from jax.sharding import PartitionSpec as P

RADIUS, WIN = 8, 17
G, S = 16, 5
BF, F32 = jnp.bfloat16, jnp.float32
NT = (((1,), (1,)), ((), ()))
BOTH = ("lon", "lat")
VM = pl.BlockSpec(memory_space=pltpu.VMEM)
SM = pl.BlockSpec(memory_space=pltpu.SMEM)


def widen(encoder_weight):
    w = encoder_weight.reshape(WIN, WIN, -1)[:, ::-1]
    w = jnp.pad(w, ((7, 7), (15, 0), (0, 0)))
    return w.reshape(31 * 32, -1)


def mirror(x):
    n = x.shape[0] // 8
    ids = 7 - lax.broadcasted_iota(jnp.int32, (8, 128), 0)
    tiles = [
        jnp.take_along_axis(x[8 * k : 8 * k + 8], ids, axis=0, mode="promise_in_bounds")
        for k in reversed(range(n))
    ]
    return jnp.concatenate(tiles, axis=0)


def pack_kernel(t_ref, f_ref, s_ref, h_ref, a_ref, b_ref, up, down, sb, fb, hb, sem):
    rows = f_ref.shape[0]
    moves = []
    for n, col in enumerate((48, 0)):
        moves.append((s_ref.at[:, col : col + 16], sb.at[n]))
        moves.append((f_ref.at[:, col : col + 16], fb.at[n]))
        moves.append((h_ref.at[6 - 6 * n : 8 - 6 * n], hb.at[n]))
    copies = [pltpu.make_async_copy(a, b, sem.at[k]) for k, (a, b) in enumerate(moves)]
    for c in copies:
        c.start()
    for c in copies:
        c.wait()
    for r in range(rows):
        up[10 * r : 10 * r + 10] = sb[0, r].astype(F32)[6:16]
        down[10 * r : 10 * r + 10] = sb[1, r].astype(F32)[0:10]
        up[320 + 2 * r : 322 + 2 * r] = fb[0, r].astype(F32)[14:16]
        down[320 + 2 * r : 322 + 2 * r] = fb[1, r].astype(F32)[0:2]
    even = lax.rem(t_ref[0], 2) == 0

    def put(n_ref, p_ref):
        n_ref[0:384] = up[...].astype(BF)
        p_ref[0:384] = down[...].astype(BF)
        for i in range(2):
            n_ref[384 + 256 * i : 640 + 256 * i] = hb[0, i]
            p_ref[384 + 256 * i : 640 + 256 * i] = hb[1, i]

    @pl.when(even)
    def _():
        put(a_ref, b_ref)

    @pl.when(jnp.logical_not(even))
    def _():
        put(b_ref, a_ref)


def pack(t, f, s, h):
    hbm = pl.BlockSpec(memory_space=pl.ANY)
    return pl.pallas_call(
        pack_kernel,
        out_shape=(jax.ShapeDtypeStruct((896, 128), BF),) * 2,
        in_specs=[SM, hbm, hbm, hbm],
        out_specs=(VM, VM),
        scratch_shapes=[
            pltpu.VMEM((384, 128), F32),
            pltpu.VMEM((384, 128), F32),
            pltpu.VMEM((2, 32, 16, 128), BF),
            pltpu.VMEM((2, 32, 16, 128), BF),
            pltpu.VMEM((2, 2, 256, 128), BF),
            pltpu.SemaphoreType.DMA((6,)),
        ],
        name="pack",
    )(t, f, s, h)


def correlate_groups(fe, se, w_ref, band, acc, groups):
    rows = fe.shape[0]
    blocks = rows // 8
    width = G * len(groups)
    scale = 128**-0.5
    for n, (fcol, scol) in enumerate(groups):
        for b in range(blocks):
            lo, hi = max(0, 8 * b - 8), min(rows, 8 * b + 16)
            keys = se[8 * b : 8 * b + 8, scol : scol + 32, :].reshape(256, 128)
            query = fe[lo:hi, fcol : fcol + G, :].reshape((hi - lo) * G, 128).astype(BF)
            c = lax.dot_general(query, keys, NT, preferred_element_type=F32)
            c = (c * scale).reshape(hi - lo, G, 256)
            for h in range(2):
                part = pltpu.roll(c[:, :, 128 * h : 128 * h + 128], 0, 2, stride=1, stride_axis=1)
                band[b, lo - 8 * b + 8 : hi - 8 * b + 8, G * n : G * n + G, 128 * h : 128 * h + 128] = part.astype(BF)
    done = set()
    for d in range(-8, 16):
        bs = [b for b in range(blocks) if 0 <= 8 * b + d < rows]
        b0, b1 = bs[0], bs[-1] + 1
        lhs = band[b0:b1, d + 8].reshape((b1 - b0) * width, 256)
        o = 15 - d
        part = jnp.dot(lhs, w_ref[32 * o : 32 * o + 256, :], preferred_element_type=F32)
        part = part.reshape(b1 - b0, width, 128)
        for n, b in enumerate(bs):
            i = 8 * b + d
            if i in done:
                acc[i + 2] += part[n]
            else:
                acc[i + 2] = part[n]
                done.add(i)
    zero = jnp.zeros((2, width, 128), F32)
    acc[0:2] = zero
    acc[rows + 2 : rows + 4] = zero


def inner_kernel(t_ref, f_ref, s_ref, w_ref, z_ref, o_ref, fe, se, band, acc):
    for r in range(f_ref.shape[0]):
        fe[r] = f_ref[r].astype(F32)
        se[r] = mirror(s_ref[r].astype(F32)).astype(BF)
    correlate_groups(fe, se, w_ref, band, acc, [(8 + G * g, 32 - G * g) for g in range(3)])
    high = t_ref[0] // 2
    for base, ref in ((14 * (1 - high) + 2, z_ref), (14 * high + 2, o_ref)):
        for r in range(18):
            ref[48 * r : 48 * r + 48] = jnp.maximum(acc[base + r], 0.0).astype(BF)


def inner(t, f, s, w_wide):
    return pl.pallas_call(
        inner_kernel,
        out_shape=(jax.ShapeDtypeStruct((864, 128), BF),) * 2,
        in_specs=[SM] + [VM] * 3,
        out_specs=(VM,) * 2,
        scratch_shapes=[
            pltpu.VMEM((32, 64, 128), F32),
            pltpu.VMEM((32, 64, 128), BF),
            pltpu.VMEM((4, 24, 48, 256), BF),
            pltpu.VMEM((36, 48, 128), F32),
        ],
        compiler_params=pltpu.CompilerParams(vmem_limit_bytes=24 << 20),
        name="inner",
    )(t, f, s, w_wide)


def edge_kernel(t_ref, l_ref, f_ref, s_ref, a_ref, b_ref, h_ref, w_ref, oi_ref, z_ref, o_ref, near_ref, far_ref, fe, se, hal, band, acc, top, bot):
    t = t_ref[0]
    odd = lax.rem(t, 2)
    for n, ref in ((1 - odd, a_ref), (odd, b_ref)):
        hal[n, 0:16] = jnp.zeros((16, 128), F32)
        hal[n, 16:400] = ref[0:384].astype(F32)
    fpad = jnp.zeros((8, 128), F32)
    for r in range(f_ref.shape[0]):
        fe[r, 0:8] = fpad
        fe[r, 24:32] = fpad
        fe[r, 8:16] = f_ref[r, 0:16].astype(F32)[0:8]
        fe[r, 16:24] = f_ref[r, 48:64].astype(F32)[8:16]
        fe[r, 6:8] = hal[0, 336 + 2 * r : 338 + 2 * r]
        fe[r, 24:26] = hal[1, 336 + 2 * r : 338 + 2 * r]
        se[r, 32:48] = mirror(s_ref[r, 0:16].astype(F32)).astype(BF)
        se[r, 48:64] = mirror(hal[0, 10 + 10 * r : 26 + 10 * r]).astype(BF)
        se[r, 0:16] = mirror(hal[1, 16 + 10 * r : 32 + 10 * r]).astype(BF)
        se[r, 16:32] = mirror(s_ref[r, 48:64].astype(F32)).astype(BF)
    correlate_groups(fe, se, w_ref, band, acc, [(0, 32), (16, 0)])

    def write(ref, base):
        rims = []
        for r in range(18):
            m = jnp.maximum(acc[base + r], 0.0)
            ref[16 * r : 16 * r + 16] = m[8:24].astype(BF)
            rims += [m[6:8], m[24:26]]
        rims.append(jnp.zeros((8, 128), F32))
        ref[288:368] = jnp.concatenate(rims, axis=0).astype(BF)

    write(z_ref, 14 * (1 - t // 2) + 2)
    o_ref[0:864] = oi_ref[...]
    write(o_ref.at[864:1232], 14 * (t // 2) + 2)
    side_rows(t, a_ref, b_ref, top, bot)

    def ends(col, out):
        parts = []
        for i in range(12):
            if i < 2:
                v = top[256 * i + col : 256 * i + col + 16]
            elif i < 10:
                v = h_ref[i - 2, col : col + 16].astype(F32)
            else:
                v = bot[256 * (i - 10) + col : 256 * (i - 10) + col + 16]
            parts.append(v[0:2] if col == 0 else v[14:16])
        parts.append(jnp.zeros((8, 128), F32))
        out[...] = jnp.concatenate(parts, axis=0).astype(BF)

    west_even = lax.rem(l_ref[0], 2) == 0

    @pl.when(west_even)
    def _():
        ends(240, near_ref)
        ends(0, far_ref)

    @pl.when(jnp.logical_not(west_even))
    def _():
        ends(0, near_ref)
        ends(240, far_ref)


def side_rows(t, a_ref, b_ref, top, bot):
    even = lax.rem(t, 2) == 0

    @pl.when(even)
    def _():
        bot[...] = a_ref[384:896].astype(F32)
        top[...] = jnp.where(t == 2, b_ref[384:896].astype(F32), 0.0)

    @pl.when(jnp.logical_not(even))
    def _():
        top[...] = a_ref[384:896].astype(F32)
        bot[...] = jnp.where(t == 1, b_ref[384:896].astype(F32), 0.0)


def edge(t, l, f, s, a, b, h, w_wide, oi):
    def sds(n):
        return jax.ShapeDtypeStruct((n, 128), BF)

    return pl.pallas_call(
        edge_kernel,
        out_shape=(sds(368), sds(1232), sds(32), sds(32)),
        in_specs=[SM, SM] + [VM] * 7,
        out_specs=(VM,) * 4,
        scratch_shapes=[
            pltpu.VMEM((32, 32, 128), F32),
            pltpu.VMEM((32, 64, 128), BF),
            pltpu.VMEM((2, 400, 128), F32),
            pltpu.VMEM((4, 24, 32, 256), BF),
            pltpu.VMEM((36, 32, 128), F32),
            pltpu.VMEM((512, 128), F32),
            pltpu.VMEM((512, 128), F32),
        ],
        compiler_params=pltpu.CompilerParams(vmem_limit_bytes=24 << 20),
        name="edge",
    )(t, l, f, s, a, b, h, w_wide, oi)


def join_kernel(i_ref, e_ref, near_ref, far_ref, o_ref):
    o_ref[0:864] = i_ref[...]
    o_ref[864:1232] = e_ref[...]


def join(zi, ze, near, far):
    return pl.pallas_call(
        join_kernel,
        out_shape=jax.ShapeDtypeStruct((1232, 128), BF),
        in_specs=[VM] * 4,
        out_specs=VM,
        compiler_params=pltpu.CompilerParams(vmem_limit_bytes=8 << 20),
        name="join",
    )(zi, ze, near, far)


def half_kernel(*refs, last):
    if last:
        t_ref, l_ref, metric_ref, h_ref, a_ref, b_ref, near_ref, far_ref, p_ref, q_ref, gw_ref, cw_ref, other_ref, out_ref = refs[:14]
        hf, mf, x, m3s, rf, r, ug, top, bot = refs[14:]
    else:
        t_ref, l_ref, metric_ref, h_ref, a_ref, b_ref, near_ref, far_ref, p_ref, q_ref, gw_ref, cw_ref, out_ref = refs[:13]
        hf, mf, x, m3s, rf, r, ug, top, bot = refs[13:]
    t = t_ref[0]
    high = t // 2
    part = 1 - high if last else high
    c0 = pl.multiple_of(128 * part, 128)
    left_half = part == 0
    side_rows(t, a_ref, b_ref, top, bot)
    west_even = lax.rem(l_ref[0], 2) == 0
    near, far = near_ref[...].astype(F32), far_ref[...].astype(F32)
    hr = jnp.where(west_even, near, far)
    hl = jnp.where(west_even, far, near)
    for i in range(12):
        if i < 2:
            mid = top[pl.ds(256 * i + c0, 128)]
            lo, hi = top[256 * i + 120 : 256 * i + 128], top[256 * i + 128 : 256 * i + 136]
        elif i < 10:
            mid = h_ref[i - 2, pl.ds(c0, 128)].astype(F32)
            lo, hi = h_ref[i - 2, 112:128].astype(F32)[8:16], h_ref[i - 2, 128:144].astype(F32)[0:8]
        else:
            mid = bot[pl.ds(256 * (i - 10) + c0, 128)]
            lo, hi = bot[256 * (i - 10) + 120 : 256 * (i - 10) + 128], bot[256 * (i - 10) + 128 : 256 * (i - 10) + 136]
        hf[i, 2:130] = mid
        hf[i, 0:2] = jnp.where(left_half, hl[2 * i : 2 * i + 2], lo[6:8])
        hf[i, 130:132] = jnp.where(left_half, hi[0:2], hr[2 * i : 2 * i + 2])
    start = 8 * t - 2 - 14 * high
    odd = lax.rem(t, 2)
    for i in range(12):
        row = start + i
        inside = (row >= 0) & (row < 18)
        row = jnp.clip(row, 0, 17)
        for s, ref in ((odd, p_ref), (1 - odd, q_ref)):
            mid = ref[pl.ds(pl.multiple_of(48 * row, 16), 48)].astype(F32)
            ends = ref[pl.ds(pl.multiple_of(864 + 16 * row, 16), 16)].astype(F32)
            mf[i, pl.ds(10 + 64 * s, 48)] = jnp.where(inside, mid, 0.0)
            ends = jnp.where(inside, ends, 0.0)
            mf[i, pl.ds(2 + 64 * s, 8)] = ends[0:8]
            mf[i, pl.ds(58 + 64 * s, 8)] = ends[8:16]
    rims = bot
    for s, ref in ((odd, p_ref), (1 - odd, q_ref)):
        rims[8:88] = ref[1152:1232].astype(F32)
        for i in range(12):
            row = start + i
            inside = (row >= 0) & (row < 18)
            row = jnp.clip(row, 0, 17)
            v = rims[pl.ds(8 + 4 * row + 2 * s, 2)]
            mf[i, pl.ds(130 * s, 2)] = jnp.where(inside, v, 0.0)
    for q in range(3):
        for i in range(12):
            x[q, i, :, 0:128] = hf[i, q : q + 144].astype(BF)
            x[q, i, :, 128:256] = mf[i, q : q + 144].astype(BF)
    for i in range(12):
        m3s[i] = mf[i, 3:131].astype(BF)
    sides_w = jnp.concatenate([gw_ref[p, q] for q in (0, 2) for p in range(3)], axis=0)
    center_w = jnp.concatenate([gw_ref[p, 1] for p in range(3)], axis=0)
    for i in range(0, 10, 2):
        lhs = jnp.concatenate([x[q, i + p : i + p + 2].reshape(288, 256) for q in (0, 2) for p in range(3)], axis=1)
        sides = jnp.dot(lhs, sides_w, preferred_element_type=F32)
        lhs = jnp.concatenate([x[1, i + p : i + p + 2].reshape(288, 256) for p in range(3)], axis=1)
        center = jnp.dot(lhs, center_w, preferred_element_type=F32)
        for n in range(2):
            cut = slice(144 * n, 144 * n + 144)
            gate = center[cut] + sides[cut] * metric_ref[8 * t + i + n]
            gate = 0.5 * jnp.tanh(0.5 * gate) + 0.5
            rf[i + n, 0:144] = gate[:, 128:] * hf[i + n + 1, 1:145]
            if 1 <= i + n < 9:
                ug[i + n - 1] = gate[:, 0:128]
    for q in range(3):
        for i in range(10):
            r[q, i] = rf[i, q : q + 128].astype(BF)
    zero = jnp.zeros((256, 128), BF)

    def pair(rr, q):
        first = cw_ref[rr, q] if rr < 3 else zero
        second = cw_ref[rr - 1, q] if rr > 0 else zero
        return jnp.concatenate([first, second], axis=1)

    sides_w = jnp.concatenate([pair(rr, q) for q in (0, 2) for rr in range(4)], axis=0)
    center_w = jnp.concatenate([pair(rr, 1) for rr in range(4)], axis=0)

    def taps(q, row):
        mm = m3s[row + 1] if q == 2 else x[q + 1, row + 1, 0:128, 128:256]
        return [r[q, row], mm]

    def stack(qs, i):
        one = [jnp.concatenate(sum([taps(q, i + k + rr) for q in qs for rr in range(4)], []), axis=1) for k in (0, 2)]
        return jnp.concatenate(one, axis=0)

    for i in range(0, 8, 4):
        sides = jnp.dot(stack((0, 2), i), sides_w, preferred_element_type=F32)
        center = jnp.dot(stack((1,), i), center_w, preferred_element_type=F32)
        for n in range(4):
            cut = (slice(128 * (n // 2), 128 * (n // 2) + 128), slice(128 * (n % 2), 128 * (n % 2) + 128))
            cand = jnp.tanh(center[cut] + sides[cut] * metric_ref[8 * t + i + n + 1])
            u = ug[i + n, 1:129]
            h = hf[i + n + 2, 2:130]
            new = ((1.0 - u) * h + u * cand).astype(BF)
            if last:
                out_ref[i + n, pl.ds(c0, 128)] = new
                out_ref[i + n, pl.ds(pl.multiple_of(128 - c0, 128), 128)] = other_ref[i + n]
            else:
                out_ref[i + n] = new


def half(t, l, metric, h, a, b, near, far, p, q, gw, cw, other=None):
    last = other is not None
    return pl.pallas_call(
        functools.partial(half_kernel, last=last),
        out_shape=jax.ShapeDtypeStruct((8, 256 if last else 128, 128), BF),
        in_specs=[SM, SM, SM] + [VM] * (10 if last else 9),
        out_specs=VM,
        scratch_shapes=[
            pltpu.VMEM((12, 152, 128), F32),
            pltpu.VMEM((12, 152, 128), F32),
            pltpu.VMEM((3, 12, 144, 256), BF),
            pltpu.VMEM((12, 128, 128), BF),
            pltpu.VMEM((10, 144, 128), F32),
            pltpu.VMEM((3, 10, 128, 128), BF),
            pltpu.VMEM((8, 144, 128), F32),
            pltpu.VMEM((512, 128), F32),
            pltpu.VMEM((512, 128), F32),
        ],
        compiler_params=pltpu.CompilerParams(vmem_limit_bytes=24 << 20),
        name="second_half" if last else "first_half",
    )(t, l, metric, h, a, b, near, far, p, q, gw, cw, *((other,) if last else ()))


def swaps(n, first):
    pairs = [(i % n, (i + 1) % n) for i in range(first, n, 2)]
    return pairs + [(j, i) for i, j in pairs]


def body(first, second, hidden, encoder_weight, gates_weight, candidate_weight, row_metric):
    t = lax.axis_index("lat").astype(jnp.int32)[None]
    l = lax.axis_index("lon").astype(jnp.int32)[None]
    count = lax.axis_size("lon")
    slabs = count * lax.axis_size("lat")
    w_wide = widen(encoder_weight)
    metric = jnp.pad(row_metric, (1, 1))
    core = [(i, i ^ 1) for i in range(4)]
    chip = [(i, i ^ 2) for i in range(4)]

    a_send, b_send = pack(t, first, second, hidden)
    with jax.named_scope("rim_far"):
        b = lax.ppermute(b_send, BOTH, swaps(slabs, 1))
    with jax.named_scope("rim_near"):
        a = lax.ppermute(a_send, BOTH, swaps(slabs, 0))
    z_send, oi = inner(t, first, second, w_wide)
    with jax.named_scope("inner_chip"):
        zi = lax.ppermute(z_send, "lat", chip)
    ze_send, own, near_send, far_send = edge(t, l, first, second, a, b, hidden, w_wide, oi)
    with jax.named_scope("edge_chip"):
        ze = lax.ppermute(ze_send, "lat", chip)
    with jax.named_scope("state_near"):
        near = lax.ppermute(near_send, "lon", swaps(count, 0))
    with jax.named_scope("state_far"):
        far = lax.ppermute(far_send, "lon", swaps(count, 1))
    with jax.named_scope("own_core"):
        mate = lax.ppermute(own, "lat", core)
    z = join(zi, ze, near, far)
    with jax.named_scope("chip_core"):
        k = lax.ppermute(z, "lat", core)
    shared = (t, l, metric, hidden, a, b, near, far)
    one = half(*shared, own, mate, gates_weight, candidate_weight)
    return half(*shared, z, k, gates_weight, candidate_weight, one)


def solution(mesh):
    return jax.shard_map(
        body,
        mesh=mesh,
        in_specs=(
            P(None, BOTH, None),
            P(None, BOTH, None),
            P("lat", "lon", None),
            P(),
            P(),
            P(),
            P(),
        ),
        out_specs=P("lat", "lon", None),
        check_vma=False,
    )
```

time: 45.4 us -> 37.8 us (0.83)
  waiting for transfers between devices: 9.64 us -> 3.57 us
  Pallas kernels: 9.29 us -> 13.2 us
  local copies, waits for them, and re-layouts: 3.12 us -> 0.27 us
  starting transfers between devices: 22.8 us -> 20.5 us
    ppermute x9 -> x8, waiting for transfers between devices: 9.64 us -> 3.57 us  [the longest x1 2.17 us: body(): b = lax.ppermute(b_send, BOTH, swaps(slabs, 1))]
    pallas_call x2 -> x6, Pallas kernels: 9.29 us -> 13.2 us  [the longest x2 8.34 us: half(): pl.pallas_call(functools.partial(half_kernel, last=last), out_shape=jax.S...]
    slice x6 -> x0, local copies, waits for them, and re-layouts: 2.76 us -> none  [the longest x2 1.92 us: body(): right = lax.ppermute(rim(second[:, :10], first[:, :2]), BOTH, down)]
    ppermute x9 -> x8, starting transfers between devices: 22.8 us -> 20.5 us  [the longest x1 8.01 us: body(): far = lax.ppermute(far_send, 'lon', swaps(count, 1))]
  transfers between devices with their start and end apart: 9 -> 8, of which waited for: 2 -> 3; matrix products, arithmetic and copies ran while one was open for 5% -> 1% of each run, Pallas kernels for 5% -> 17%
where the time goes in v2:
time: 37.8 us; the launch traced here: 37.7 us
  starting transfers between devices  20.5 us (54%)
  Pallas kernels  13.2 us (35%)
  waiting for transfers between devices  3.57 us (9%)
    pallas_call x2, Pallas kernels, half(): pl.pallas_call(functools.partial(half_kernel, last=last), out_shape=jax.S...  8.34 us
    ppermute x1, starting transfers between devices, body(): far = lax.ppermute(far_send, 'lon', swaps(count, 1))  8.01 us
    ppermute x1, starting transfers between devices, body(): ze = lax.ppermute(ze_send, 'lat', chip)  6.67 us
    ppermute x1, starting transfers between devices, body(): b = lax.ppermute(b_send, BOTH, swaps(slabs, 1))  3.69 us
    pallas_call x1, Pallas kernels, pack(): pl.pallas_call(pack_kernel, out_shape=(jax.ShapeDtypeStruct((896, 128), B...  2.22 us
    ppermute x1, waiting for transfers between devices, body(): b = lax.ppermute(b_send, BOTH, swaps(slabs, 1))  2.17 us
    ppermute x1, starting transfers between devices, body(): a = lax.ppermute(a_send, BOTH, swaps(slabs, 0))  1.47 us
    pallas_call x1, Pallas kernels, inner(): pl.pallas_call(inner_kernel, out_shape=(jax.ShapeDtypeStruct((864, 128),...  1.43 us
  transfers between devices with their start and end apart: 8, of which 3 were waited for; matrix products, arithmetic and copies ran while one was open for 1% of the time, Pallas kernels for 17%

profile of v2, /device:TPU:1, one launch (start us, length us, event | category | flops | bytes accessed | tf_op | source)
XLA Modules:
  0.0 37.7 jit_solution(5302462694534271846)
XLA Ops:
  0.0 0.0 copy-start.2
  0.0 0.0 copy-start.3
  0.0 0.0 copy-start.5
  0.0 2.2 %pack.1 = (bf16[896,128]{1,0:T(8,128)(2,1)}, bf16[896,128]{1,0:T(8,128)(2,1)}) custom-call(s32[1]{0:T(128)} %bitcast.t_ref.refs_0_, bf16[32,64,128]{2,1,0:T(8,128)(2,1)} %f_ref.5, bf16[32,64,128]{2,1,0:T(8,128)(2,1)} %s_ref.5, bf16[8,256,128]{2,1,0:T(8,128)(2,1)} %refs_3_.3), custom_call_target="tpu_custom_call" | custom-call | tf_op jit(solution)/shard_map/pack/pallas_call | solution.py:72
  2.2 0.0 copy-start
  2.3 1.5 %collective-permute-start = (bf16[896,128]{1,0:T(8,128)(2,1)}, bf16[896,128]{1,0:T(8,128)(2,1)S(1)}, u32[]{:S(2)}, u32[]{:S(2)}) collective-permute-start(bf16[896,128]{1,0:T(8,128)(2,1)} %get-tuple-element.13), channel_id=1, source_target_pairs={{0,1},{2,3},{4,5},{6,7},{8,9},{10,11},{12,13},{14,15},{16,17},{18,... | collective-permute-start | bytes 688136 | tf_op jit(solution)/shard_map/rim_near/ppermute | solution.py:416
  3.7 3.7 %collective-permute-start.1 = (bf16[896,128]{1,0:T(8,128)(2,1)}, bf16[896,128]{1,0:T(8,128)(2,1)S(1)}, u32[]{:S(2)}, u32[]{:S(2)}) collective-permute-start(bf16[896,128]{1,0:T(8,128)(2,1)} %get-tuple-element.14), channel_id=1, source_target_pairs={{1,2},{3,4},{5,6},{7,8},{9,10},{11,12},{13,14},{15,16},{17,18},{19... | collective-permute-start | bytes 688136 | tf_op jit(solution)/shard_map/rim_far/ppermute | solution.py:414
  7.4 0.0 copy-done.5
  7.5 0.1 rev.3
  7.6 0.0 copy-done.2
  7.6 0.0 copy-done.3
  7.6 1.4 %inner.1 = (bf16[864,128]{1,0:T(8,128)(2,1)S(1)}, bf16[864,128]{1,0:T(8,128)(2,1)S(1)}) custom-call(s32[1]{0:T(128)} %bitcast.t_ref.refs_0_, bf16[32,64,128]{2,1,0:T(8,128)(2,1)S(1)} %copy-done.2, bf16[32,64,128]{2,1,0:T(8,128)(2,1)S(1)} %copy-done.3, bf16[992,128]{1,0:T(8,128)(2,1)S(1)} %bitcast.3), custom_call_target="tpu_custom_call" | custom-call | tf_op jit(solution)/shard_map/inner/pallas_call | solution.py:136
  9.1 0.1 collective-permute-start.4
  9.2 0.0 collective-permute-done.a_ref.refs_4_
  9.2 2.2 %collective-permute-done.1.b_ref.refs_5_ = bf16[896,128]{1,0:T(8,128)(2,1)S(1)} collective-permute-done((bf16[896,128]{1,0:T(8,128)(2,1)}, bf16[896,128]{1,0:T(8,128)(2,1)S(1)}, u32[]{:S(2)}, u32[]{:S(2)}) %collective-permute-start.1) | collective-permute-done | bytes 229408 | tf_op jit(solution)/shard_map/rim_far/ppermute | solution.py:414
  11.3 0.0 copy-done
  11.3 0.0 copy-start.6
  11.3 0.0 copy-start.1
  11.3 0.0 copy-start.4
  11.3 1.2 %edge.1 = (bf16[368,128]{1,0:T(8,128)(2,1)S(1)}, bf16[1232,128]{1,0:T(8,128)(2,1)S(1)}, bf16[32,128]{1,0:T(8,128)(2,1)S(1)}, bf16[32,128]{1,0:T(8,128)(2,1)S(1)}) custom-call(s32[1]{0:T(128)} %bitcast.t_ref.refs_0_, s32[1]{0:T(128)} %bitcast.1.l_ref.refs_1_, bf16[32,64,128]{2,1,0:T(8,128)(2,1)S(1)} %copy-done.2, bf16[32,64,128]{2,1,0:T(8,128)(2,1)S(1)} %copy-done.3, ...), custom_call_target="tpu_custom_call" | custom-call | tf_op jit(solution)/shard_map/edge/pallas_call | solution.py:230
  12.6 6.7 %collective-permute-start.5 = (bf16[368,128]{1,0:T(8,128)(2,1)S(1)}, bf16[368,128]{1,0:T(8,128)(2,1)S(1)}, u32[]{:S(2)}, u32[]{:S(2)}) collective-permute-start(bf16[368,128]{1,0:T(8,128)(2,1)S(1)} %get-tuple-element.19), channel_id=1, source_target_pairs={{0,2},{1,3},{2,0},{3,1},{4,6},{5,7},{6,4},{7,5},{8,10},{9,11},{10,... | collective-permute-start | bytes 282632 | tf_op jit(solution)/shard_map/edge_chip/ppermute | solution.py:422
  19.2 0.5 %collective-permute-start.2 = (bf16[32,128]{1,0:T(8,128)(2,1)S(1)}, bf16[32,128]{1,0:T(8,128)(2,1)S(1)}, u32[]{:S(2)}, u32[]{:S(2)}) collective-permute-start(bf16[32,128]{1,0:T(8,128)(2,1)S(1)} %get-tuple-element.16), channel_id=1, source_target_pairs={{0,4},{8,12},{16,20},{24,28},{32,36},{40,44},{48,52},{56,60},{64,6... | collective-permute-start | bytes 24584 | tf_op jit(solution)/shard_map/state_near/ppermute | solution.py:424
  19.7 8.0 %collective-permute-start.3 = (bf16[32,128]{1,0:T(8,128)(2,1)S(1)}, bf16[32,128]{1,0:T(8,128)(2,1)S(1)}, u32[]{:S(2)}, u32[]{:S(2)}) collective-permute-start(bf16[32,128]{1,0:T(8,128)(2,1)S(1)} %get-tuple-element.17), channel_id=1, source_target_pairs={{4,8},{12,16},{20,24},{28,32},{36,40},{44,48},{52,56},{60,64},{68,... | collective-permute-start | bytes 24584 | tf_op jit(solution)/shard_map/state_far/ppermute | solution.py:426
  27.7 0.0 collective-permute-start.7
  27.7 0.0 collective-permute-done.4.i_ref
  27.7 0.0 collective-permute-done.2.near_ref.refs_6_
  27.7 1.0 %collective-permute-done.3.far_ref.refs_7_ = bf16[32,128]{1,0:T(8,128)(2,1)S(1)} collective-permute-done((bf16[32,128]{1,0:T(8,128)(2,1)S(1)}, bf16[32,128]{1,0:T(8,128)(2,1)S(1)}, u32[]{:S(2)}, u32[]{:S(2)}) %collective-permute-start.3) | collective-permute-done | bytes 8224 | tf_op jit(solution)/shard_map/state_far/ppermute | solution.py:426
  28.7 0.0 collective-permute-done.5.e_ref
  28.8 0.1 collective-permute-start.6
  28.9 0.0 copy-done.6
  28.9 0.1 pad.8.refs_2_
  29.0 0.4 collective-permute-done.7.refs_9_
  29.3 0.0 copy-done.1
  29.3 0.0 copy-done.4
  29.3 3.8 %first_half.1.refs_12_ = bf16[8,128,128]{2,1,0:T(8,128)(2,1)S(1)} custom-call(s32[1]{0:T(128)} %bitcast.t_ref.refs_0_, s32[1]{0:T(128)} %bitcast.1.l_ref.refs_1_, f32[34]{0:T(128)S(1)} %pad.8.refs_2_, bf16[8,256,128]{2,1,0:T(8,128)(2,1)S(1)} %copy-done, bf16[896,128]{1,0:T(8,128)(2,1)S(1)} %collective-permute-done.a_ref.refs_4_, ...), custom_call_target="tpu_custom_call" | custom-call | tf_op jit(solution)/shard_map/first_half/pallas_call | solution.py:376
  33.1 0.0 collective-permute-done.6.refs_9_
  33.1 4.6 %second_half.1 = bf16[8,256,128]{2,1,0:T(8,128)(2,1)} custom-call(s32[1]{0:T(128)} %bitcast.t_ref.refs_0_, s32[1]{0:T(128)} %bitcast.1.l_ref.refs_1_, f32[34]{0:T(128)S(1)} %pad.8.refs_2_, bf16[8,256,128]{2,1,0:T(8,128)(2,1)S(1)} %copy-done, bf16[896,128]{1,0:T(8,128)(2,1)S(1)} %collective-permute-done.a_ref.refs_4_, ...), custom_call_target="tpu_custom_call" | custom-call | tf_op jit(solution)/shard_map/second_half/pallas_call | solution.py:376
  (3 shorter events, 0.1 us)
Async XLA Ops:
  0.0 7.6 %copy-start.2 = (bf16[32,64,128]{2,1,0:T(8,128)(2,1)S(1)}, bf16[32,64,128]{2,1,0:T(8,128)(2,1)}, u32[]{:S(2)}) copy-start(bf16[32,64,128]{2,1,0:T(8,128)(2,1)} %f_ref.5) | copy-start | bytes 1572868
  0.0 7.6 %copy-start.3 = (bf16[32,64,128]{2,1,0:T(8,128)(2,1)S(1)}, bf16[32,64,128]{2,1,0:T(8,128)(2,1)}, u32[]{:S(2)}) copy-start(bf16[32,64,128]{2,1,0:T(8,128)(2,1)} %s_ref.5) | copy-start | bytes 1572868
  0.0 7.4 %copy-start.5 = (bf16[289,128]{1,0:T(8,128)(2,1)S(1)}, bf16[289,128]{1,0:T(8,128)(2,1)}, u32[]{:S(2)}) copy-start(bf16[289,128]{1,0:T(8,128)(2,1)} %param.10) | copy-start | bytes 221956
  2.2 9.1 %copy-start = (bf16[8,256,128]{2,1,0:T(8,128)(2,1)S(1)}, bf16[8,256,128]{2,1,0:T(8,128)(2,1)}, u32[]{:S(2)}) copy-start(bf16[8,256,128]{2,1,0:T(8,128)(2,1)} %refs_3_.3) | copy-start | bytes 1572868
  2.3 6.9 %collective-permute-start = (bf16[896,128]{1,0:T(8,128)(2,1)}, bf16[896,128]{1,0:T(8,128)(2,1)S(1)}, u32[]{:S(2)}, u32[]{:S(2)}) collective-permute-start(bf16[896,128]{1,0:T(8,128)(2,1)} %get-tuple-element.13), channel_id=1, source_target_pairs={{0,1},{2,3},{4,5},{6,7},{8,9},{10,11},{12,13},{14,15},{16,17},{18,... | collective-permute-start | bytes 688136 | tf_op jit(solution)/shard_map/rim_near/ppermute | solution.py:416
  3.7 7.6 %collective-permute-start.1 = (bf16[896,128]{1,0:T(8,128)(2,1)}, bf16[896,128]{1,0:T(8,128)(2,1)S(1)}, u32[]{:S(2)}, u32[]{:S(2)}) collective-permute-start(bf16[896,128]{1,0:T(8,128)(2,1)} %get-tuple-element.14), channel_id=1, source_target_pairs={{1,2},{3,4},{5,6},{7,8},{9,10},{11,12},{13,14},{15,16},{17,18},{19... | collective-permute-start | bytes 688136 | tf_op jit(solution)/shard_map/rim_far/ppermute | solution.py:414
  9.1 18.7 %collective-permute-start.4 = (bf16[864,128]{1,0:T(8,128)(2,1)S(1)}, bf16[864,128]{1,0:T(8,128)(2,1)S(1)}, u32[]{:S(2)}, u32[]{:S(2)}) collective-permute-start(bf16[864,128]{1,0:T(8,128)(2,1)S(1)} %get-tuple-element.18), channel_id=1, source_target_pairs={{0,2},{1,3},{2,0},{3,1},{4,6},{5,7},{6,4},{7,5},{8,10},{9,11},{10,... | collective-permute-start | bytes 663560 | tf_op jit(solution)/shard_map/inner_chip/ppermute | solution.py:419
  11.3 17.5 %copy-start.6 = (f32[32]{0:T(128)S(1)}, f32[32]{0:T(128)}, u32[]{:S(2)}) copy-start(f32[32]{0:T(128)} %param.13) | copy-start | bytes 388
  11.3 18.0 %copy-start.1 = (bf16[3,3,256,256]{3,2,1,0:T(8,128)(2,1)S(1)}, bf16[3,3,256,256]{3,2,1,0:T(8,128)(2,1)}, u32[]{:S(2)}) copy-start(bf16[3,3,256,256]{3,2,1,0:T(8,128)(2,1)} %refs_10_.3) | copy-start | bytes 3538948
  11.3 18.0 %copy-start.4 = (bf16[3,3,256,128]{3,2,1,0:T(8,128)(2,1)S(1)}, bf16[3,3,256,128]{3,2,1,0:T(8,128)(2,1)}, u32[]{:S(2)}) copy-start(bf16[3,3,256,128]{3,2,1,0:T(8,128)(2,1)} %refs_11_.3) | copy-start | bytes 1769476
  12.6 16.2 %collective-permute-start.5 = (bf16[368,128]{1,0:T(8,128)(2,1)S(1)}, bf16[368,128]{1,0:T(8,128)(2,1)S(1)}, u32[]{:S(2)}, u32[]{:S(2)}) collective-permute-start(bf16[368,128]{1,0:T(8,128)(2,1)S(1)} %get-tuple-element.19), channel_id=1, source_target_pairs={{0,2},{1,3},{2,0},{3,1},{4,6},{5,7},{6,4},{7,5},{8,10},{9,11},{10,... | collective-permute-start | bytes 282632 | tf_op jit(solution)/shard_map/edge_chip/ppermute | solution.py:422
  19.2 8.5 %collective-permute-start.2 = (bf16[32,128]{1,0:T(8,128)(2,1)S(1)}, bf16[32,128]{1,0:T(8,128)(2,1)S(1)}, u32[]{:S(2)}, u32[]{:S(2)}) collective-permute-start(bf16[32,128]{1,0:T(8,128)(2,1)S(1)} %get-tuple-element.16), channel_id=1, source_target_pairs={{0,4},{8,12},{16,20},{24,28},{32,36},{40,44},{48,52},{56,60},{64,6... | collective-permute-start | bytes 24584 | tf_op jit(solution)/shard_map/state_near/ppermute | solution.py:424
  19.7 9.0 %collective-permute-start.3 = (bf16[32,128]{1,0:T(8,128)(2,1)S(1)}, bf16[32,128]{1,0:T(8,128)(2,1)S(1)}, u32[]{:S(2)}, u32[]{:S(2)}) collective-permute-start(bf16[32,128]{1,0:T(8,128)(2,1)S(1)} %get-tuple-element.17), channel_id=1, source_target_pairs={{4,8},{12,16},{20,24},{28,32},{36,40},{44,48},{52,56},{60,64},{68,... | collective-permute-start | bytes 24584 | tf_op jit(solution)/shard_map/state_far/ppermute | solution.py:426
  27.7 1.6 %collective-permute-start.7 = (bf16[1232,128]{1,0:T(8,128)(2,1)S(1)}, bf16[1232,128]{1,0:T(8,128)(2,1)S(1)}, u32[]{:S(2)}, u32[]{:S(2)}) collective-permute-start(bf16[1232,128]{1,0:T(8,128)(2,1)S(1)} %get-tuple-element.20.refs_8_), channel_id=1, source_target_pairs={{0,1},{1,0},{2,3},{3,2},{4,5},{5,4},{6,7},{7,6},{8,9},{9,8},{10,11... | collective-permute-start | bytes 946184 | tf_op jit(solution)/shard_map/own_core/ppermute | solution.py:428
  28.8 4.3 %collective-permute-start.6 = (bf16[1232,128]{1,0:T(8,128)(2,1)S(1)}, bf16[1232,128]{1,0:T(8,128)(2,1)S(1)}, u32[]{:S(2)}, u32[]{:S(2)}) collective-permute-start(bf16[1232,128]{1,0:T(8,128)(2,1)S(1)} %join.1.refs_8_), channel_id=1, source_target_pairs={{0,1},{1,0},{2,3},{3,2},{4,5},{5,4},{6,7},{7,6},{8,9},{9,8},{10,11... | collective-permute-start | bytes 946184 | tf_op jit(solution)/shard_map/chip_core/ppermute | solution.py:431

commit v3 on v2

v3 whole, which is shorter than its diff:
```python
import functools

import jax
import jax.numpy as jnp
from jax import lax
from jax.experimental import pallas as pl
from jax.experimental.pallas import tpu as pltpu
from jax.sharding import PartitionSpec as P

RADIUS, WIN = 8, 17
G, S = 16, 5
BF, F32 = jnp.bfloat16, jnp.float32
NT = (((1,), (1,)), ((), ()))
BOTH = ("lon", "lat")
VM = pl.BlockSpec(memory_space=pltpu.VMEM)
SM = pl.BlockSpec(memory_space=pltpu.SMEM)


def mirror(x):
    n = x.shape[0] // 8
    ids = 7 - lax.broadcasted_iota(jnp.int32, (8, 128), 0)
    tiles = [
        jnp.take_along_axis(x[8 * k : 8 * k + 8], ids, axis=0, mode="promise_in_bounds")
        for k in reversed(range(n))
    ]
    return jnp.concatenate(tiles, axis=0)


def pack_kernel(t_ref, l_ref, f_ref, s_ref, h_ref, a_ref, b_ref, near_ref, far_ref, up, down, sb, fb, hb, cb, sem):
    rows = f_ref.shape[0]
    moves = []
    for n, col in enumerate((48, 0)):
        moves.append((s_ref.at[:, col : col + 16], sb.at[n]))
        moves.append((f_ref.at[:, col : col + 16], fb.at[n]))
        moves.append((h_ref.at[6 - 6 * n : 8 - 6 * n], hb.at[n]))
        moves.append((h_ref.at[:, 240 - 240 * n : 256 - 240 * n], cb.at[n]))
    copies = [pltpu.make_async_copy(a, b, sem.at[k]) for k, (a, b) in enumerate(moves)]
    for c in copies:
        c.start()
    for c in copies:
        c.wait()
    for r in range(rows):
        up[10 * r : 10 * r + 10] = sb[0, r].astype(F32)[6:16]
        down[10 * r : 10 * r + 10] = sb[1, r].astype(F32)[0:10]
        up[320 + 2 * r : 322 + 2 * r] = fb[0, r].astype(F32)[14:16]
        down[320 + 2 * r : 322 + 2 * r] = fb[1, r].astype(F32)[0:2]
    east = jnp.concatenate([cb[0, i].astype(F32)[14:16] for i in range(8)], axis=0)
    west = jnp.concatenate([cb[1, i].astype(F32)[0:2] for i in range(8)], axis=0)
    even = lax.rem(l_ref[0], 2) == 0
    near_ref[...] = jnp.where(even, east, west).astype(BF)
    far_ref[...] = jnp.where(even, west, east).astype(BF)
    even = lax.rem(t_ref[0], 2) == 0

    def put(n_ref, p_ref):
        n_ref[0:384] = up[...].astype(BF)
        p_ref[0:384] = down[...].astype(BF)
        for i in range(2):
            n_ref[384 + 256 * i : 640 + 256 * i] = hb[0, i]
            p_ref[384 + 256 * i : 640 + 256 * i] = hb[1, i]

    @pl.when(even)
    def _():
        put(a_ref, b_ref)

    @pl.when(jnp.logical_not(even))
    def _():
        put(b_ref, a_ref)


def pack(t, l, f, s, h):
    hbm = pl.BlockSpec(memory_space=pl.ANY)
    return pl.pallas_call(
        pack_kernel,
        out_shape=(jax.ShapeDtypeStruct((896, 128), BF),) * 2 + (jax.ShapeDtypeStruct((16, 128), BF),) * 2,
        in_specs=[SM, SM, hbm, hbm, hbm],
        out_specs=(VM,) * 4,
        scratch_shapes=[
            pltpu.VMEM((384, 128), F32),
            pltpu.VMEM((384, 128), F32),
            pltpu.VMEM((2, 32, 16, 128), BF),
            pltpu.VMEM((2, 32, 16, 128), BF),
            pltpu.VMEM((2, 2, 256, 128), BF),
            pltpu.VMEM((2, 8, 16, 128), BF),
            pltpu.SemaphoreType.DMA((8,)),
        ],
        name="pack",
    )(t, l, f, s, h)


def correlate_groups(fe, se, w_ref, band, acc, groups):
    rows = fe.shape[0]
    blocks = rows // 8
    width = G * len(groups)
    scale = 128**-0.5
    for n, (fcol, scol) in enumerate(groups):
        for b in range(blocks):
            lo, hi = max(0, 8 * b - 8), min(rows, 8 * b + 16)
            keys = se[8 * b : 8 * b + 8, scol : scol + 32, :].reshape(256, 128)
            query = fe[lo:hi, fcol : fcol + G, :].reshape((hi - lo) * G, 128).astype(BF)
            c = lax.dot_general(query, keys, NT, preferred_element_type=F32)
            c = (c * scale).reshape(hi - lo, G, 256)
            for h in range(2):
                part = pltpu.roll(c[:, :, 128 * h : 128 * h + 128], 0, 2, stride=1, stride_axis=1)
                band[b, lo - 8 * b + 8 : hi - 8 * b + 8, G * n : G * n + G, 128 * h : 128 * h + 128] = part.astype(BF)
    done = set()
    for d in range(-8, 16):
        bs = [b for b in range(blocks) if 0 <= 8 * b + d < rows]
        b0, b1 = bs[0], bs[-1] + 1
        lhs = band[b0:b1, d + 8].reshape((b1 - b0) * width, 256)
        o = 15 - d
        part = jnp.dot(lhs, w_ref[32 * o : 32 * o + 256, :], preferred_element_type=F32)
        part = part.reshape(b1 - b0, width, 128)
        for n, b in enumerate(bs):
            i = 8 * b + d
            if i in done:
                acc[i + 2] += part[n]
            else:
                acc[i + 2] = part[n]
                done.add(i)
    zero = jnp.zeros((2, width, 128), F32)
    acc[0:2] = zero
    acc[rows + 2 : rows + 4] = zero


def widen(enc_ref, wide_ref, enc, wide):
    wide[...] = jnp.zeros(wide.shape, F32)
    enc[0:8] = jnp.zeros((8, 128), F32)
    enc[8:297] = enc_ref[...].astype(F32)
    for a in range(WIN):
        at = 32 * (a + 7) + 15
        wide[at : at + 17] = mirror(enc[17 * a + 1 : 17 * a + 25])[0:17]
    wide_ref[...] = wide[...].astype(BF)


def inner_kernel(t_ref, f_ref, s_ref, enc_ref, z_ref, o_ref, c_ref, w_ref, fe, se, band, acc, enc, wide):
    widen(enc_ref, w_ref, enc, wide)
    for r in range(f_ref.shape[0]):
        fe[r] = f_ref[r].astype(F32)
        se[r] = mirror(s_ref[r].astype(F32)).astype(BF)
    correlate_groups(fe, se, w_ref, band, acc, [(8 + G * g, 32 - G * g) for g in range(3)])
    high = t_ref[0] // 2
    for base, ref in ((14 * (1 - high) + 2, z_ref), (14 * high + 2, o_ref)):
        for r in range(18):
            ref[48 * r : 48 * r + 48] = jnp.maximum(acc[base + r], 0.0).astype(BF)
    base = 8 * (t_ref[0] ^ 1)
    for r in range(12):
        c_ref[48 * r : 48 * r + 48] = jnp.maximum(acc[base + r], 0.0).astype(BF)


def inner(t, f, s, enc):
    return pl.pallas_call(
        inner_kernel,
        out_shape=(jax.ShapeDtypeStruct((864, 128), BF),) * 2 + (jax.ShapeDtypeStruct((576, 128), BF), jax.ShapeDtypeStruct((992, 128), BF)),
        in_specs=[SM] + [VM] * 3,
        out_specs=(VM,) * 4,
        scratch_shapes=[
            pltpu.VMEM((32, 64, 128), F32),
            pltpu.VMEM((32, 64, 128), BF),
            pltpu.VMEM((4, 24, 48, 256), BF),
            pltpu.VMEM((36, 48, 128), F32),
            pltpu.VMEM((304, 128), F32),
            pltpu.VMEM((992, 128), F32),
        ],
        compiler_params=pltpu.CompilerParams(vmem_limit_bytes=24 << 20),
        cost_estimate=pl.CostEstimate(flops=1000000000, bytes_accessed=1000000, transcendentals=0),
        name="inner",
    )(t, f, s, enc)


def edge_kernel(t_ref, f_ref, s_ref, a_ref, b_ref, near_ref, far_ref, w_ref, oi_ref, ci_ref, z_ref, o_ref, c_ref, fe, se, hal, band, acc):
    t = t_ref[0]
    odd = lax.rem(t, 2)
    for n, ref in ((1 - odd, a_ref), (odd, b_ref)):
        hal[n, 0:16] = jnp.zeros((16, 128), F32)
        hal[n, 16:400] = ref[0:384].astype(F32)
    fpad = jnp.zeros((8, 128), F32)
    for r in range(f_ref.shape[0]):
        fe[r, 0:8] = fpad
        fe[r, 24:32] = fpad
        fe[r, 8:16] = f_ref[r, 0:16].astype(F32)[0:8]
        fe[r, 16:24] = f_ref[r, 48:64].astype(F32)[8:16]
        fe[r, 6:8] = hal[0, 336 + 2 * r : 338 + 2 * r]
        fe[r, 24:26] = hal[1, 336 + 2 * r : 338 + 2 * r]
        se[r, 32:48] = mirror(s_ref[r, 0:16].astype(F32)).astype(BF)
        se[r, 48:64] = mirror(hal[0, 10 + 10 * r : 26 + 10 * r]).astype(BF)
        se[r, 0:16] = mirror(hal[1, 16 + 10 * r : 32 + 10 * r]).astype(BF)
        se[r, 16:32] = mirror(s_ref[r, 48:64].astype(F32)).astype(BF)
    correlate_groups(fe, se, w_ref, band, acc, [(0, 32), (16, 0)])

    def write(ref, base, count=18):
        rims = []
        for r in range(count):
            m = jnp.maximum(acc[base + r], 0.0)
            ref[16 * r : 16 * r + 16] = m[8:24].astype(BF)
            rims += [m[6:8], m[24:26]]
        if count % 4:
            rims.append(jnp.zeros((8, 128), F32))
        at, n = 16 * count, -(-count // 4) * 16
        ref[at : at + n] = jnp.concatenate(rims, axis=0).astype(BF)

    write(z_ref, 14 * (1 - t // 2) + 2)
    o_ref[0:864] = oi_ref[...]
    write(o_ref.at[864:1232], 14 * (t // 2) + 2)
    c_ref[0:576] = ci_ref[...]
    write(c_ref.at[576:816], 8 * (t ^ 1), 12)
    for ref, at in ((z_ref, 368), (c_ref, 816)):
        ref[at : at + 16] = near_ref[...]
        ref[at + 16 : at + 32] = far_ref[...]


def side_rows(t, a_ref, b_ref, top, bot):
    even = lax.rem(t, 2) == 0

    @pl.when(even)
    def _():
        bot[...] = a_ref[384:896].astype(F32)
        top[...] = jnp.where(t == 2, b_ref[384:896].astype(F32), 0.0)

    @pl.when(jnp.logical_not(even))
    def _():
        top[...] = a_ref[384:896].astype(F32)
        bot[...] = jnp.where(t == 1, b_ref[384:896].astype(F32), 0.0)


def edge(t, f, s, a, b, near, far, w_wide, oi, ci):
    return pl.pallas_call(
        edge_kernel,
        out_shape=(jax.ShapeDtypeStruct((400, 128), BF), jax.ShapeDtypeStruct((1232, 128), BF), jax.ShapeDtypeStruct((848, 128), BF)),
        in_specs=[SM] + [VM] * 9,
        out_specs=(VM,) * 3,
        scratch_shapes=[
            pltpu.VMEM((32, 32, 128), F32),
            pltpu.VMEM((32, 64, 128), BF),
            pltpu.VMEM((2, 400, 128), F32),
            pltpu.VMEM((4, 24, 32, 256), BF),
            pltpu.VMEM((36, 32, 128), F32),
        ],
        compiler_params=pltpu.CompilerParams(vmem_limit_bytes=24 << 20),
        cost_estimate=pl.CostEstimate(flops=1000000000, bytes_accessed=1000000, transcendentals=0),
        name="edge",
    )(t, f, s, a, b, near, far, w_wide, oi, ci)


def join_kernel(i_ref, e_ref, one_ref, o_ref):
    o_ref[0:864] = i_ref[...]
    o_ref[864:1264] = e_ref[...]


def join(zi, ze, one):
    return pl.pallas_call(
        join_kernel,
        out_shape=jax.ShapeDtypeStruct((1264, 128), BF),
        in_specs=[VM] * 3,
        out_specs=VM,
        compiler_params=pltpu.CompilerParams(vmem_limit_bytes=8 << 20),
        name="join",
    )(zi, ze, one)


def state_rows(t, a_ref, b_ref, h_ref, hs, top, bot):
    side_rows(t, a_ref, b_ref, top, bot)
    hs[0:512] = top[...]
    hs[2560:3072] = bot[...]
    for i in range(8):
        hs[512 + 256 * i : 768 + 256 * i] = h_ref[i].astype(F32)


def gates(metric_ref, t, x, gw_ref, width, put):
    sides_w = jnp.concatenate([gw_ref[p, q] for q in (0, 2) for p in range(3)], axis=0)
    center_w = jnp.concatenate([gw_ref[p, 1] for p in range(3)], axis=0)
    for i in range(0, 10, 2):
        lhs = jnp.concatenate([x[q, i + p : i + p + 2].reshape(2 * width, 256) for q in (0, 2) for p in range(3)], axis=1)
        sides = jnp.dot(lhs, sides_w, preferred_element_type=F32)
        lhs = jnp.concatenate([x[1, i + p : i + p + 2].reshape(2 * width, 256) for p in range(3)], axis=1)
        center = jnp.dot(lhs, center_w, preferred_element_type=F32)
        for n in range(2):
            cut = slice(width * n, width * n + width)
            gate = center[cut] + sides[cut] * metric_ref[jnp.clip(8 * t + i + n - 1, 0, 31)]
            put(i + n, 0.5 * jnp.tanh(0.5 * gate) + 0.5)


def candidates(metric_ref, t, x, m3s, r, cw_ref, width, put):
    zero = jnp.zeros((256, 128), BF)

    def pair(rr, q):
        first = cw_ref[rr, q] if rr < 3 else zero
        second = cw_ref[rr - 1, q] if rr > 0 else zero
        return jnp.concatenate([first, second], axis=1)

    sides_w = jnp.concatenate([pair(rr, q) for q in (0, 2) for rr in range(4)], axis=0)
    center_w = jnp.concatenate([pair(rr, 1) for rr in range(4)], axis=0)

    def taps(q, row):
        mm = m3s[row + 1] if q == 2 else x[q + 1, row + 1, 0:width, 128:256]
        return [r[q, row], mm]

    def stack(qs, i):
        one = [jnp.concatenate(sum([taps(q, i + k + rr) for q in qs for rr in range(4)], []), axis=1) for k in (0, 2)]
        return jnp.concatenate(one, axis=0)

    for i in range(0, 8, 4):
        sides = jnp.dot(stack((0, 2), i), sides_w, preferred_element_type=F32)
        center = jnp.dot(stack((1,), i), center_w, preferred_element_type=F32)
        for n in range(4):
            cut = (slice(width * (n // 2), width * (n // 2) + width), slice(128 * (n % 2), 128 * (n % 2) + 128))
            put(i + n, jnp.tanh(center[cut] + sides[cut] * metric_ref[8 * t + i + n]))


def piece_row(ref, row, inside, count):
    mid = ref[pl.ds(pl.multiple_of(48 * row, 16), 48)].astype(F32)
    ends = ref[pl.ds(pl.multiple_of(48 * count + 16 * row, 16), 16)].astype(F32)
    if inside is not None:
        mid, ends = jnp.where(inside, mid, 0.0), jnp.where(inside, ends, 0.0)
    return mid, ends


def first_kernel(t_ref, metric_ref, h_ref, a_ref, b_ref, own_ref, mate_ref, zi_ref, gw_ref, cw_ref, out_ref, hs, mf, x, m3s, rf, r, ug, top, bot, rims):
    t = t_ref[0]
    high = t // 2
    base = 112 * high
    state_rows(t, a_ref, b_ref, h_ref, hs, top, bot)
    start = 8 * t - 2 - 14 * high
    odd = lax.rem(t, 2)
    for s, ref, count in ((odd, own_ref, 18), (1 - odd, mate_ref, 12)):
        rims[0:80] = ref[1152:1232].astype(F32) if count == 18 else jnp.pad(ref[768:816].astype(F32), ((0, 32), (0, 0)))
        for i in range(12):
            row, inside = i, None
            if count == 18:
                row = start + i
                inside = (row >= 0) & (row < 18)
                row = jnp.clip(row, 0, 17)
            mid, ends = piece_row(ref, row, inside, count)
            at = 64 * s + 16 * high
            mf[i, pl.ds(at + 8, 48)] = mid
            mf[i, pl.ds(at, 8)] = ends[0:8]
            mf[i, pl.ds(at + 56, 8)] = ends[8:16]

            @pl.when(s != high)
            def _(i=i, row=row, s=s, inside=inside):
                v = rims[pl.ds(4 * row + 2 * s, 2)]
                mf[i, pl.ds(128 - 114 * high, 2)] = v if inside is None else jnp.where(inside, v, 0.0)

    for q in range(3):
        for i in range(12):
            x[q, i, :, 0:128] = hs[pl.ds(256 * i + base + 14 + q, 128)].astype(BF)
            x[q, i, :, 128:256] = mf[i, 14 + q : 142 + q].astype(BF)
    for i in range(12):
        m3s[i] = mf[i, 17:129].astype(BF)

    def put_gate(i, gate):
        rf[i, 0:128] = gate[:, 128:] * hs[pl.ds(256 * (i + 1) + base + 15, 128)]
        if 1 <= i < 9:
            ug[i - 1] = gate[:, 0:128]

    gates(metric_ref, t, x, gw_ref, 128, put_gate)
    for q in range(3):
        for i in range(10):
            r[q, i] = rf[i, q : q + 112].astype(BF)

    def put_new(i, cand):
        u = ug[i, 1:113]
        h = hs[pl.ds(256 * (i + 2) + base + 16, 112)]
        out_ref[i] = ((1.0 - u) * h + u * cand).astype(BF)

    candidates(metric_ref, t, x, m3s, r, cw_ref, 112, put_new)


def first_part(t, metric, h, a, b, own, mate, zi, gw, cw):
    return pl.pallas_call(
        first_kernel,
        out_shape=jax.ShapeDtypeStruct((8, 112, 128), BF),
        in_specs=[SM, SM] + [VM] * 8,
        out_specs=VM,
        scratch_shapes=[
            pltpu.VMEM((3072, 128), F32),
            pltpu.VMEM((12, 152, 128), F32),
            pltpu.VMEM((3, 12, 128, 256), BF),
            pltpu.VMEM((12, 112, 128), BF),
            pltpu.VMEM((10, 136, 128), F32),
            pltpu.VMEM((3, 10, 112, 128), BF),
            pltpu.VMEM((8, 128, 128), F32),
            pltpu.VMEM((512, 128), F32),
            pltpu.VMEM((512, 128), F32),
            pltpu.VMEM((80, 128), F32),
        ],
        compiler_params=pltpu.CompilerParams(vmem_limit_bytes=24 << 20),
        cost_estimate=pl.CostEstimate(flops=4000000000, bytes_accessed=4000000, transcendentals=0),
        name="first_part",
    )(t, metric, h, a, b, own, mate, zi, gw, cw)


def second_kernel(
    t_ref, l_ref, metric_ref, h_ref, a_ref, b_ref, near_ref, far_ref, own_ref, mate_ref, z_ref, k_ref, gw_ref, cw_ref, one_ref, out_ref,
    hs, hf, mf, x, m3s, rf, r, ug, top, bot, rims,
):
    t = t_ref[0]
    high = t // 2
    c0 = pl.multiple_of(128 - 128 * high, 128)
    state_rows(t, a_ref, b_ref, h_ref, hs, top, bot)
    west_even = lax.rem(l_ref[0], 2) == 0
    odd = lax.rem(t, 2)
    low = high == 0

    def twelve(own, at):
        mates, others = mate_ref[816 + at : 832 + at].astype(F32), k_ref[1232 + at : 1248 + at].astype(F32)
        others = jnp.where((t == 1) | (t == 2), others, 0.0)
        above = jnp.where(odd == 1, mates, others)[12:16]
        below = jnp.where(odd == 1, others, mates)[0:4]
        return jnp.concatenate([above, own[...].astype(F32), below], axis=0)

    near, far = twelve(near_ref, 0), twelve(far_ref, 16)
    hr = jnp.where(west_even, near, far)
    hl = jnp.where(west_even, far, near)
    for i in range(12):
        hf[i, 2:130] = hs[pl.ds(256 * i + c0, 128)]
        side_w, side_e = hl[2 * i : 2 * i + 2], hr[2 * i : 2 * i + 2]
        hf[i, 0:2] = jnp.where(low, hs[256 * i + 126 : 256 * i + 128], side_w)
        hf[i, 130:132] = jnp.where(low, side_e, hs[256 * i + 128 : 256 * i + 130])
        hf[i, pl.ds(146 - 2 * high, 18)] = hs[pl.ds(256 * i + 238 * high, 18)]
        hf[i, pl.ds(144 + 18 * high, 2)] = jnp.where(low, side_w, side_e)
    start = 8 * t - 2 - 14 * high
    for s, ref in ((odd, z_ref), (1 - odd, k_ref)):
        rims[0:80] = ref[1152:1232].astype(F32)
        for i in range(12):
            row = start + i
            inside = (row >= 0) & (row < 18)
            row = jnp.clip(row, 0, 17)
            mid = ref[pl.ds(pl.multiple_of(48 * row, 16), 48)].astype(F32)
            ends = ref[pl.ds(pl.multiple_of(864 + 16 * row, 16), 16)].astype(F32)
            mf[i, pl.ds(10 + 64 * s, 48)] = jnp.where(inside, mid, 0.0)
            ends = jnp.where(inside, ends, 0.0)
            mf[i, pl.ds(2 + 64 * s, 8)] = ends[0:8]
            mf[i, pl.ds(58 + 64 * s, 8)] = ends[8:16]
            v = rims[pl.ds(4 * row + 2 * s, 2)]
            mf[i, pl.ds(130 * s, 2)] = jnp.where(inside, v, 0.0)
    mine = odd == high
    mates = jnp.pad(mate_ref[768:816].astype(F32), ((0, 32), (0, 0)))
    rims[0:80] = jnp.where(mine, own_ref[1152:1232].astype(F32), mates)
    for i in range(12):
        row = start + i
        inside = (row >= 0) & (row < 18)
        row = jnp.clip(row, 0, 17)
        at = pl.multiple_of(48 * row + 32 * high, 16)
        mid = jnp.where(inside, own_ref[pl.ds(at, 16)].astype(F32), 0.0)
        at = pl.multiple_of(864 + 16 * row, 16)
        ends = jnp.where(inside, own_ref[pl.ds(at, 16)].astype(F32), 0.0)
        at = pl.multiple_of(48 * i + 32 * high, 16)
        mid = jnp.where(mine, mid, mate_ref[pl.ds(at, 16)].astype(F32))
        ends = jnp.where(mine, ends, mate_ref[576 + 16 * i : 592 + 16 * i].astype(F32))
        mf[i, pl.ds(154 - 10 * high, 10)] = jnp.where(low, mid[0:10], mid[6:16])
        mf[i, pl.ds(146 + 8 * high, 8)] = jnp.where(low, ends[0:8], ends[8:16])
        row = jnp.where(mine, row, i)
        inside = inside | jnp.logical_not(mine)
        v = rims[pl.ds(4 * row + 2 * high, 2)]
        mf[i, pl.ds(144 + 18 * high, 2)] = jnp.where(inside, v, 0.0)
    for q in range(3):
        for i in range(12):
            x[q, i, :, 0:128] = hf[i, q : q + 176].astype(BF)
            x[q, i, :, 128:256] = mf[i, q : q + 176].astype(BF)
    for i in range(12):
        m3s[i] = mf[i, 3:163].astype(BF)

    def put_gate(i, gate):
        rf[i, 0:176] = gate[:, 128:] * hf[i + 1, 1:177]
        if 1 <= i < 9:
            ug[i - 1] = gate[:, 0:128]

    gates(metric_ref, t, x, gw_ref, 176, put_gate)
    for q in range(3):
        for i in range(10):
            r[q, i] = rf[i, q : q + 160].astype(BF)

    def put_new(i, cand):
        u = ug[i, 1:161]
        h = hf[i + 2, 2:162]
        new = ((1.0 - u) * h + u * cand).astype(BF)
        out_ref[i, pl.ds(c0, 128)] = new[0:128]
        out_ref[i, pl.ds(pl.multiple_of(240 * high, 16), 16)] = new[144:160]
        out_ref[i, pl.ds(pl.multiple_of(16 + 112 * high, 16), 112)] = one_ref[i]

    candidates(metric_ref, t, x, m3s, r, cw_ref, 160, put_new)


def second_part(t, l, metric, h, a, b, near, far, own, mate, z, k, gw, cw, one):
    return pl.pallas_call(
        second_kernel,
        out_shape=jax.ShapeDtypeStruct((8, 256, 128), BF),
        in_specs=[SM, SM, SM] + [VM] * 12,
        out_specs=VM,
        scratch_shapes=[
            pltpu.VMEM((3072, 128), F32),
            pltpu.VMEM((12, 184, 128), F32),
            pltpu.VMEM((12, 184, 128), F32),
            pltpu.VMEM((3, 12, 176, 256), BF),
            pltpu.VMEM((12, 160, 128), BF),
            pltpu.VMEM((10, 184, 128), F32),
            pltpu.VMEM((3, 10, 160, 128), BF),
            pltpu.VMEM((8, 176, 128), F32),
            pltpu.VMEM((512, 128), F32),
            pltpu.VMEM((512, 128), F32),
            pltpu.VMEM((80, 128), F32),
        ],
        compiler_params=pltpu.CompilerParams(vmem_limit_bytes=24 << 20),
        cost_estimate=pl.CostEstimate(flops=5000000000, bytes_accessed=4000000, transcendentals=0),
        name="second_part",
    )(t, l, metric, h, a, b, near, far, own, mate, z, k, gw, cw, one)


def swaps(n, first):
    pairs = [(i % n, (i + 1) % n) for i in range(first, n, 2)]
    return pairs + [(j, i) for i, j in pairs]


def body(first, second, hidden, encoder_weight, gates_weight, candidate_weight, row_metric):
    t = lax.axis_index("lat").astype(jnp.int32)[None]
    l = lax.axis_index("lon").astype(jnp.int32)[None]
    count = lax.axis_size("lon")
    slabs = count * lax.axis_size("lat")
    core = [(i, i ^ 1) for i in range(4)]
    chip = [(i, i ^ 2) for i in range(4)]

    a_send, b_send, near_send, far_send = pack(t, l, first, second, hidden)
    with jax.named_scope("rim_far"):
        b = lax.ppermute(b_send, BOTH, swaps(slabs, 1))
    with jax.named_scope("rim_near"):
        a = lax.ppermute(a_send, BOTH, swaps(slabs, 0))
    with jax.named_scope("state_near"):
        near = lax.ppermute(near_send, "lon", swaps(count, 0))
    with jax.named_scope("state_far"):
        far = lax.ppermute(far_send, "lon", swaps(count, 1))
    zi_send, oi, ci, w_wide = inner(t, first, second, encoder_weight)
    with jax.named_scope("inner_chip"):
        zi = lax.ppermute(zi_send, "lat", chip)
    ze_send, own, own_send = edge(t, first, second, a, b, near, far, w_wide, oi, ci)
    with jax.named_scope("edge_chip"):
        ze = lax.ppermute(ze_send, "lat", chip)
    with jax.named_scope("own_core"):
        mate = lax.ppermute(own_send, "lat", core)
    one = first_part(t, row_metric, hidden, a, b, own, mate, zi, gates_weight, candidate_weight)
    z = join(zi, ze, one)
    with jax.named_scope("chip_core"):
        k = lax.ppermute(z, "lat", core)
    return second_part(t, l, row_metric, hidden, a, b, near, far, own, mate, z, k, gates_weight, candidate_weight, one)


def solution(mesh):
    return jax.shard_map(
        body,
        mesh=mesh,
        in_specs=(
            P(None, BOTH, None),
            P(None, BOTH, None),
            P("lat", "lon", None),
            P(),
            P(),
            P(),
            P(),
        ),
        out_specs=P("lat", "lon", None),
        check_vma=False,
    )
```

time: 37.8 us -> 35.7 us (0.944)
  starting transfers between devices: 20.5 us -> 17.7 us
  Pallas kernels: 13.2 us -> 13.9 us
    ppermute x1, starting transfers between devices: 6.67 us -> 0.01 us  [body(): ze = lax.ppermute(ze_send, 'lat', chip)]
    ppermute x2, starting transfers between devices: 0.1 us -> 5.52 us  [the longest x1 5.42 us: body(): mate = lax.ppermute(own_send, 'lat', core)]
    ppermute x1, starting transfers between devices: 8.01 us -> 5.37 us  [body(): far = lax.ppermute(far_send, 'lon', swaps(count, 1))]
    ppermute x1, waiting for transfers between devices: 2.17 us -> 0.01 us  [body(): b = lax.ppermute(b_send, BOTH, swaps(slabs, 1))]
    ppermute x1, waiting for transfers between devices: 0.01 us -> 1.29 us  [body(): ze = lax.ppermute(ze_send, 'lat', chip)]
    ppermute x1, waiting for transfers between devices: 0.01 us -> 1.25 us  [body(): k = lax.ppermute(z, 'lat', core)]
    ppermute x1, starting transfers between devices: 0.09 us -> 0.95 us  [body(): k = lax.ppermute(z, 'lat', core)]
    ppermute x1, waiting for transfers between devices: 1.03 us -> 0.18 us  [body(): far = lax.ppermute(far_send, 'lon', swaps(count, 1))]
  transfers between devices with their start and end apart: 8 -> 8, of which waited for: 3 -> 5; matrix products, arithmetic and copies ran while one was open for 1% -> 0% of each run, Pallas kernels for 17% -> 18%
where the time goes in v3:
time: 35.7 us; the launch traced here: 35.6 us
  starting transfers between devices  17.7 us (50%)
  Pallas kernels  13.9 us (39%)
  waiting for transfers between devices  3.82 us (11%)
    ppermute x1, starting transfers between devices, body(): mate = lax.ppermute(own_send, 'lat', core)  5.42 us
    pallas_call x1, Pallas kernels, second_part(): pl.pallas_call(second_kernel, out_shape=jax.ShapeDtypeStruct((8, 256, 128...  5.39 us
    ppermute x1, starting transfers between devices, body(): far = lax.ppermute(far_send, 'lon', swaps(count, 1))  5.37 us
    ppermute x1, starting transfers between devices, body(): b = lax.ppermute(b_send, BOTH, swaps(slabs, 1))  3.67 us
    pallas_call x1, Pallas kernels, first_part(): pl.pallas_call(first_kernel, out_shape=jax.ShapeDtypeStruct((8, 112, 128)...  3.54 us
    pallas_call x1, Pallas kernels, pack(): pl.pallas_call(pack_kernel, out_shape=(jax.ShapeDtypeStruct((896, 128), B...  2.24 us
    pallas_call x1, Pallas kernels, inner(): pl.pallas_call(inner_kernel, out_shape=(jax.ShapeDtypeStruct((864, 128),...  1.51 us
    ppermute x1, starting transfers between devices, body(): a = lax.ppermute(a_send, BOTH, swaps(slabs, 0))  1.49 us
  transfers between devices with their start and end apart: 8, of which 5 were waited for; matrix products, arithmetic and copies ran while one was open for 0% of the time, Pallas kernels for 18%

profile of v3, /device:TPU:1, one launch (start us, length us, event | category | flops | bytes accessed | tf_op | source)
XLA Modules:
  0.0 35.6 jit_solution(15222761002526427164)
XLA Ops:
  0.0 0.0 copy-start.1
  0.0 0.0 copy-start
  0.0 0.0 copy-start.5
  0.0 2.2 %pack.1 = (bf16[896,128]{1,0:T(8,128)(2,1)}, bf16[896,128]{1,0:T(8,128)(2,1)}, bf16[16,128]{1,0:T(8,128)(2,1)}, bf16[16,128]{1,0:T(8,128)(2,1)}) custom-call(s32[1]{0:T(128)} %bitcast.t_ref, s32[1]{0:T(128)} %bitcast.1.l_ref, bf16[32,64,128]{2,1,0:T(8,128)(2,1)} %f_ref.5, bf16[32,64,128]{2,1,0:T(8,128)(2,1)} %s_ref.5, bf16[8,256,128]{2,1,0:T(8,128)(2,1)} %h_ref.5), custom_call_target="tpu_custom_call" | custom-call | tf_op jit(solution)/shard_map/pack/pallas_call | solution.py:72
  2.3 1.5 %collective-permute-start = (bf16[896,128]{1,0:T(8,128)(2,1)}, bf16[896,128]{1,0:T(8,128)(2,1)S(1)}, u32[]{:S(2)}, u32[]{:S(2)}) collective-permute-start(bf16[896,128]{1,0:T(8,128)(2,1)} %get-tuple-element.16), channel_id=1, source_target_pairs={{0,1},{2,3},{4,5},{6,7},{8,9},{10,11},{12,13},{14,15},{16,17},{18,... | collective-permute-start | bytes 688136 | tf_op jit(solution)/shard_map/rim_near/ppermute | solution.py:526
  3.8 3.7 %collective-permute-start.1 = (bf16[896,128]{1,0:T(8,128)(2,1)}, bf16[896,128]{1,0:T(8,128)(2,1)S(1)}, u32[]{:S(2)}, u32[]{:S(2)}) collective-permute-start(bf16[896,128]{1,0:T(8,128)(2,1)} %get-tuple-element.17), channel_id=1, source_target_pairs={{1,2},{3,4},{5,6},{7,8},{9,10},{11,12},{13,14},{15,16},{17,18},{19... | collective-permute-start | bytes 688136 | tf_op jit(solution)/shard_map/rim_far/ppermute | solution.py:524
  7.4 0.7 %collective-permute-start.2 = (bf16[16,128]{1,0:T(8,128)(2,1)}, bf16[16,128]{1,0:T(8,128)(2,1)S(1)}, u32[]{:S(2)}, u32[]{:S(2)}) collective-permute-start(bf16[16,128]{1,0:T(8,128)(2,1)} %get-tuple-element.18), channel_id=1, source_target_pairs={{0,4},{8,12},{16,20},{24,28},{32,36},{40,44},{48,52},{56,60},{64,6... | collective-permute-start | bytes 12296 | tf_op jit(solution)/shard_map/state_near/ppermute | solution.py:528
  8.2 5.4 %collective-permute-start.3 = (bf16[16,128]{1,0:T(8,128)(2,1)}, bf16[16,128]{1,0:T(8,128)(2,1)S(1)}, u32[]{:S(2)}, u32[]{:S(2)}) collective-permute-start(bf16[16,128]{1,0:T(8,128)(2,1)} %get-tuple-element.19), channel_id=1, source_target_pairs={{4,8},{12,16},{20,24},{28,32},{36,40},{44,48},{52,56},{60,64},{68,... | collective-permute-start | bytes 12296 | tf_op jit(solution)/shard_map/state_far/ppermute | solution.py:530
  13.5 0.0 copy-done.1
  13.5 0.0 copy-done
  13.5 0.0 copy-done.5
  13.5 1.5 %inner.1 = (bf16[864,128]{1,0:T(8,128)(2,1)S(1)}, bf16[864,128]{1,0:T(8,128)(2,1)S(1)}, bf16[576,128]{1,0:T(8,128)(2,1)S(1)}, bf16[992,128]{1,0:T(8,128)(2,1)S(1)}) custom-call(s32[1]{0:T(128)} %bitcast.t_ref, bf16[32,64,128]{2,1,0:T(8,128)(2,1)S(1)} %copy-done, bf16[32,64,128]{2,1,0:T(8,128)(2,1)S(1)} %copy-done.1, bf16[289,128]{1,0:T(8,128)(2,1)S(1)} %copy-done.5), custom_call_target="tpu_custom_call" | custom-call | flops 1000000000 | bytes 1000000 | tf_op jit(solution)/shard_map/inner/pallas_call | solution.py:151
  15.1 0.1 collective-permute-start.5
  15.2 0.0 collective-permute-done.2.near_ref
  15.2 0.2 collective-permute-done.3.far_ref
  15.3 0.0 collective-permute-done.a_ref
  15.3 0.0 collective-permute-done.1.b_ref
  15.3 0.0 copy-start.2
  15.4 0.0 copy-start.3
  15.4 0.0 copy-start.4
  15.4 0.0 copy-start.6
  15.4 1.2 %edge.1 = (bf16[400,128]{1,0:T(8,128)(2,1)S(1)}, bf16[1232,128]{1,0:T(8,128)(2,1)S(1)}, bf16[848,128]{1,0:T(8,128)(2,1)S(1)}) custom-call(s32[1]{0:T(128)} %bitcast.t_ref, bf16[32,64,128]{2,1,0:T(8,128)(2,1)S(1)} %copy-done, bf16[32,64,128]{2,1,0:T(8,128)(2,1)S(1)} %copy-done.1, bf16[896,128]{1,0:T(8,128)(2,1)S(1)} %collective-permute-done.a_ref, ...), custom_call_target="tpu_custom_call" | custom-call | flops 1000000000 | bytes 1000000 | tf_op jit(solution)/shard_map/edge/pallas_call | solution.py:226
  16.6 5.4 %collective-permute-start.4 = (bf16[848,128]{1,0:T(8,128)(2,1)S(1)}, bf16[848,128]{1,0:T(8,128)(2,1)S(1)}, u32[]{:S(2)}, u32[]{:S(2)}) collective-permute-start(bf16[848,128]{1,0:T(8,128)(2,1)S(1)} %get-tuple-element.24), channel_id=1, source_target_pairs={{0,1},{1,0},{2,3},{3,2},{4,5},{5,4},{6,7},{7,6},{8,9},{9,8},{10,11... | collective-permute-start | bytes 651272 | tf_op jit(solution)/shard_map/own_core/ppermute | solution.py:538
  22.0 0.0 collective-permute-start.6
  22.0 0.2 collective-permute-done.5.zi_ref.i_ref
  22.2 0.9 %collective-permute-done.4.mate_ref = bf16[848,128]{1,0:T(8,128)(2,1)S(1)} collective-permute-done((bf16[848,128]{1,0:T(8,128)(2,1)S(1)}, bf16[848,128]{1,0:T(8,128)(2,1)S(1)}, u32[]{:S(2)}, u32[]{:S(2)}) %collective-permute-start.4) | collective-permute-done | bytes 217120 | tf_op jit(solution)/shard_map/own_core/ppermute | solution.py:538
  23.1 0.0 copy-done.2
  23.1 0.0 copy-done.3
  23.1 0.0 copy-done.4
  23.1 0.0 copy-done.6
  23.1 3.5 %first_part.1.one_ref = bf16[8,112,128]{2,1,0:T(8,128)(2,1)S(1)} custom-call(s32[1]{0:T(128)} %bitcast.t_ref, f32[32]{0:T(128)S(1)} %copy-done.6, bf16[8,256,128]{2,1,0:T(8,128)(2,1)S(1)} %copy-done.2, bf16[896,128]{1,0:T(8,128)(2,1)S(1)} %collective-permute-done.a_ref, bf16[896,128]{1,0:T(8,128)(2,1)S(1)} %collective-permute-done.1.b_ref, ...), custom_call_target="tpu_custom_call" | custom-call | flops 4000000000 | bytes 4000000 | tf_op jit(solution)/shard_map/first_part/pallas_call | solution.py:369
  26.7 1.3 %collective-permute-done.6.e_ref = bf16[400,128]{1,0:T(8,128)(2,1)S(1)} collective-permute-done((bf16[400,128]{1,0:T(8,128)(2,1)S(1)}, bf16[400,128]{1,0:T(8,128)(2,1)S(1)}, u32[]{:S(2)}, u32[]{:S(2)}) %collective-permute-start.6) | collective-permute-done | bytes 102432 | tf_op jit(solution)/shard_map/edge_chip/ppermute | solution.py:536
  28.0 1.0 %collective-permute-start.7 = (bf16[1264,128]{1,0:T(8,128)(2,1)S(1)}, bf16[1264,128]{1,0:T(8,128)(2,1)S(1)}, u32[]{:S(2)}, u32[]{:S(2)}) collective-permute-start(bf16[1264,128]{1,0:T(8,128)(2,1)S(1)} %join.1.z_ref), channel_id=1, source_target_pairs={{0,1},{1,0},{2,3},{3,2},{4,5},{5,4},{6,7},{7,6},{8,9},{9,8},{10,11... | collective-permute-start | bytes 970760 | tf_op jit(solution)/shard_map/chip_core/ppermute | solution.py:542
  28.9 1.2 %collective-permute-done.7.k_ref = bf16[1264,128]{1,0:T(8,128)(2,1)S(1)} collective-permute-done((bf16[1264,128]{1,0:T(8,128)(2,1)S(1)}, bf16[1264,128]{1,0:T(8,128)(2,1)S(1)}, u32[]{:S(2)}, u32[]{:S(2)}) %collective-permute-start.7) | collective-permute-done | bytes 323616 | tf_op jit(solution)/shard_map/chip_core/ppermute | solution.py:542
  30.2 5.4 %second_part.1 = bf16[8,256,128]{2,1,0:T(8,128)(2,1)} custom-call(s32[1]{0:T(128)} %bitcast.t_ref, s32[1]{0:T(128)} %bitcast.1.l_ref, f32[32]{0:T(128)S(1)} %copy-done.6, bf16[8,256,128]{2,1,0:T(8,128)(2,1)S(1)} %copy-done.2, bf16[896,128]{1,0:T(8,128)(2,1)S(1)} %collective-permute-done.a_ref, bf16[896,128]{1,0:T(8,128)(2,1)S(1)} %collective-permute-done.1.b_ref, ...), custom_call_target="tpu_custom_call" | custom-call | flops 5000000000 | bytes 4000000 | tf_op jit(solution)/shard_map/second_part/pallas_call | solution.py:485
  (1 shorter events, 0.0 us)
Async XLA Ops:
  0.0 13.5 %copy-start.1 = (bf16[32,64,128]{2,1,0:T(8,128)(2,1)S(1)}, bf16[32,64,128]{2,1,0:T(8,128)(2,1)}, u32[]{:S(2)}) copy-start(bf16[32,64,128]{2,1,0:T(8,128)(2,1)} %s_ref.5) | copy-start | bytes 1572868
  0.0 13.5 %copy-start = (bf16[32,64,128]{2,1,0:T(8,128)(2,1)S(1)}, bf16[32,64,128]{2,1,0:T(8,128)(2,1)}, u32[]{:S(2)}) copy-start(bf16[32,64,128]{2,1,0:T(8,128)(2,1)} %f_ref.5) | copy-start | bytes 1572868
  0.0 13.5 %copy-start.5 = (bf16[289,128]{1,0:T(8,128)(2,1)S(1)}, bf16[289,128]{1,0:T(8,128)(2,1)}, u32[]{:S(2)}) copy-start(bf16[289,128]{1,0:T(8,128)(2,1)} %enc_ref.1) | copy-start | bytes 221956
  2.3 13.1 %collective-permute-start = (bf16[896,128]{1,0:T(8,128)(2,1)}, bf16[896,128]{1,0:T(8,128)(2,1)S(1)}, u32[]{:S(2)}, u32[]{:S(2)}) collective-permute-start(bf16[896,128]{1,0:T(8,128)(2,1)} %get-tuple-element.16), channel_id=1, source_target_pairs={{0,1},{2,3},{4,5},{6,7},{8,9},{10,11},{12,13},{14,15},{16,17},{18,... | collective-permute-start | bytes 688136 | tf_op jit(solution)/shard_map/rim_near/ppermute | solution.py:526
  3.8 11.6 %collective-permute-start.1 = (bf16[896,128]{1,0:T(8,128)(2,1)}, bf16[896,128]{1,0:T(8,128)(2,1)S(1)}, u32[]{:S(2)}, u32[]{:S(2)}) collective-permute-start(bf16[896,128]{1,0:T(8,128)(2,1)} %get-tuple-element.17), channel_id=1, source_target_pairs={{1,2},{3,4},{5,6},{7,8},{9,10},{11,12},{13,14},{15,16},{17,18},{19... | collective-permute-start | bytes 688136 | tf_op jit(solution)/shard_map/rim_far/ppermute | solution.py:524
  7.4 7.7 %collective-permute-start.2 = (bf16[16,128]{1,0:T(8,128)(2,1)}, bf16[16,128]{1,0:T(8,128)(2,1)S(1)}, u32[]{:S(2)}, u32[]{:S(2)}) collective-permute-start(bf16[16,128]{1,0:T(8,128)(2,1)} %get-tuple-element.18), channel_id=1, source_target_pairs={{0,4},{8,12},{16,20},{24,28},{32,36},{40,44},{48,52},{56,60},{64,6... | collective-permute-start | bytes 12296 | tf_op jit(solution)/shard_map/state_near/ppermute | solution.py:528
  8.2 7.2 %collective-permute-start.3 = (bf16[16,128]{1,0:T(8,128)(2,1)}, bf16[16,128]{1,0:T(8,128)(2,1)S(1)}, u32[]{:S(2)}, u32[]{:S(2)}) collective-permute-start(bf16[16,128]{1,0:T(8,128)(2,1)} %get-tuple-element.19), channel_id=1, source_target_pairs={{4,8},{12,16},{20,24},{28,32},{36,40},{44,48},{52,56},{60,64},{68,... | collective-permute-start | bytes 12296 | tf_op jit(solution)/shard_map/state_far/ppermute | solution.py:530
  15.1 7.1 %collective-permute-start.5 = (bf16[864,128]{1,0:T(8,128)(2,1)S(1)}, bf16[864,128]{1,0:T(8,128)(2,1)S(1)}, u32[]{:S(2)}, u32[]{:S(2)}) collective-permute-start(bf16[864,128]{1,0:T(8,128)(2,1)S(1)} %get-tuple-element.25), channel_id=1, source_target_pairs={{0,2},{1,3},{2,0},{3,1},{4,6},{5,7},{6,4},{7,5},{8,10},{9,11},{10,... | collective-permute-start | bytes 663560 | tf_op jit(solution)/shard_map/inner_chip/ppermute | solution.py:533
  15.3 7.8 %copy-start.2 = (bf16[8,256,128]{2,1,0:T(8,128)(2,1)S(1)}, bf16[8,256,128]{2,1,0:T(8,128)(2,1)}, u32[]{:S(2)}) copy-start(bf16[8,256,128]{2,1,0:T(8,128)(2,1)} %h_ref.5) | copy-start | bytes 1572868
  15.4 7.8 %copy-start.3 = (bf16[3,3,256,256]{3,2,1,0:T(8,128)(2,1)S(1)}, bf16[3,3,256,256]{3,2,1,0:T(8,128)(2,1)}, u32[]{:S(2)}) copy-start(bf16[3,3,256,256]{3,2,1,0:T(8,128)(2,1)} %gw_ref.3) | copy-start | bytes 3538948
  15.4 7.7 %copy-start.4 = (bf16[3,3,256,128]{3,2,1,0:T(8,128)(2,1)S(1)}, bf16[3,3,256,128]{3,2,1,0:T(8,128)(2,1)}, u32[]{:S(2)}) copy-start(bf16[3,3,256,128]{3,2,1,0:T(8,128)(2,1)} %cw_ref.3) | copy-start | bytes 1769476
  15.4 7.7 %copy-start.6 = (f32[32]{0:T(128)S(1)}, f32[32]{0:T(128)}, u32[]{:S(2)}) copy-start(f32[32]{0:T(128)} %metric_ref.3) | copy-start | bytes 388
  16.6 6.5 %collective-permute-start.4 = (bf16[848,128]{1,0:T(8,128)(2,1)S(1)}, bf16[848,128]{1,0:T(8,128)(2,1)S(1)}, u32[]{:S(2)}, u32[]{:S(2)}) collective-permute-start(bf16[848,128]{1,0:T(8,128)(2,1)S(1)} %get-tuple-element.24), channel_id=1, source_target_pairs={{0,1},{1,0},{2,3},{3,2},{4,5},{5,4},{6,7},{7,6},{8,9},{9,8},{10,11... | collective-permute-start | bytes 651272 | tf_op jit(solution)/shard_map/own_core/ppermute | solution.py:538
  22.0 5.9 %collective-permute-start.6 = (bf16[400,128]{1,0:T(8,128)(2,1)S(1)}, bf16[400,128]{1,0:T(8,128)(2,1)S(1)}, u32[]{:S(2)}, u32[]{:S(2)}) collective-permute-start(bf16[400,128]{1,0:T(8,128)(2,1)S(1)} %get-tuple-element.26), channel_id=1, source_target_pairs={{0,2},{1,3},{2,0},{3,1},{4,6},{5,7},{6,4},{7,5},{8,10},{9,11},{10,... | collective-permute-start | bytes 307208 | tf_op jit(solution)/shard_map/edge_chip/ppermute | solution.py:536
  28.0 2.2 %collective-permute-start.7 = (bf16[1264,128]{1,0:T(8,128)(2,1)S(1)}, bf16[1264,128]{1,0:T(8,128)(2,1)S(1)}, u32[]{:S(2)}, u32[]{:S(2)}) collective-permute-start(bf16[1264,128]{1,0:T(8,128)(2,1)S(1)} %join.1.z_ref), channel_id=1, source_target_pairs={{0,1},{1,0},{2,3},{3,2},{4,5},{5,4},{6,7},{7,6},{8,9},{9,8},{10,11... | collective-permute-start | bytes 970760 | tf_op jit(solution)/shard_map/chip_core/ppermute | solution.py:542

commit v4 on v3

--- a/solution.py
+++ b/solution.py
@@ -71,7 +71,7 @@
     hbm = pl.BlockSpec(memory_space=pl.ANY)
     return pl.pallas_call(
         pack_kernel,
-        out_shape=(jax.ShapeDtypeStruct((896, 128), BF),) * 2 + (jax.ShapeDtypeStruct((16, 128), BF),) * 2,
+        out_shape=(pltpu.VMEM((896, 128), BF),) * 2 + (pltpu.VMEM((16, 128), BF),) * 2,
         in_specs=[SM, SM, hbm, hbm, hbm],
         out_specs=(VM,) * 4,
         scratch_shapes=[
@@ -391,7 +391,7 @@
 
 def second_kernel(
     t_ref, l_ref, metric_ref, h_ref, a_ref, b_ref, near_ref, far_ref, own_ref, mate_ref, z_ref, k_ref, gw_ref, cw_ref, one_ref, out_ref,
-    hs, hf, mf, x, m3s, rf, r, ug, top, bot, rims,
+    ob, sem, hs, hf, mf, x, m3s, rf, r, ug, top, bot, rims,
 ):
     t = t_ref[0]
     high = t // 2
@@ -474,11 +474,14 @@
         u = ug[i, 1:161]
         h = hf[i + 2, 2:162]
         new = ((1.0 - u) * h + u * cand).astype(BF)
-        out_ref[i, pl.ds(c0, 128)] = new[0:128]
-        out_ref[i, pl.ds(pl.multiple_of(240 * high, 16), 16)] = new[144:160]
-        out_ref[i, pl.ds(pl.multiple_of(16 + 112 * high, 16), 112)] = one_ref[i]
+        ob[i, pl.ds(c0, 128)] = new[0:128]
+        ob[i, pl.ds(pl.multiple_of(240 * high, 16), 16)] = new[144:160]
+        ob[i, pl.ds(pl.multiple_of(16 + 112 * high, 16), 112)] = one_ref[i]
+        pltpu.make_async_copy(ob.at[i], out_ref.at[i], sem.at[i]).start()
 
     candidates(metric_ref, t, x, m3s, r, cw_ref, 160, put_new)
+    for i in range(8):
+        pltpu.make_async_copy(ob.at[i], out_ref.at[i], sem.at[i]).wait()
 
 
 def second_part(t, l, metric, h, a, b, near, far, own, mate, z, k, gw, cw, one):
@@ -486,8 +489,10 @@
         second_kernel,
         out_shape=jax.ShapeDtypeStruct((8, 256, 128), BF),
         in_specs=[SM, SM, SM] + [VM] * 12,
-        out_specs=VM,
+        out_specs=pl.BlockSpec(memory_space=pl.ANY),
         scratch_shapes=[
+            pltpu.VMEM((8, 256, 128), BF),
+            pltpu.SemaphoreType.DMA((8,)),
             pltpu.VMEM((3072, 128), F32),
             pltpu.VMEM((12, 184, 128), F32),
             pltpu.VMEM((12, 184, 128), F32),

time: 35.7 us -> 34.6 us (0.969)
  Pallas kernels: 13.9 us -> 13.1 us
    pallas_call x1, Pallas kernels: 2.24 us -> 1.47 us  [pack(): pl.pallas_call(pack_kernel, out_shape=(pltpu.VMEM((896, 128), BF),) * 2 +...]
  transfers between devices with their start and end apart: 8 -> 8, of which waited for: 5 -> 4; matrix products, arithmetic and copies ran while one was open for 0% -> 0% of each run, Pallas kernels for 18% -> 18%
where the time goes in v4:
time: 34.6 us; the launch traced here: 34.5 us
  starting transfers between devices  17.7 us (51%)
  Pallas kernels  13.1 us (38%)
  waiting for transfers between devices  3.64 us (11%)
    ppermute x1, starting transfers between devices, body(): far = lax.ppermute(far_send, 'lon', swaps(count, 1))  5.37 us
    ppermute x1, starting transfers between devices, body(): mate = lax.ppermute(own_send, 'lat', core)  5.35 us
    pallas_call x1, Pallas kernels, second_part(): pl.pallas_call(second_kernel, out_shape=jax.ShapeDtypeStruct((8, 256, 128...  5.31 us
    ppermute x1, starting transfers between devices, body(): b = lax.ppermute(b_send, BOTH, swaps(slabs, 1))  3.67 us
    pallas_call x1, Pallas kernels, first_part(): pl.pallas_call(first_kernel, out_shape=jax.ShapeDtypeStruct((8, 112, 128)...  3.54 us
    pallas_call x1, Pallas kernels, inner(): pl.pallas_call(inner_kernel, out_shape=(jax.ShapeDtypeStruct((864, 128),...  1.52 us
    ppermute x1, starting transfers between devices, body(): a = lax.ppermute(a_send, BOTH, swaps(slabs, 0))  1.49 us
    pallas_call x1, Pallas kernels, pack(): pl.pallas_call(pack_kernel, out_shape=(pltpu.VMEM((896, 128), BF),) * 2 +...  1.47 us
  transfers between devices with their start and end apart: 8, of which 4 were waited for; matrix products, arithmetic and copies ran while one was open for 0% of the time, Pallas kernels for 18%

profile of v4, /device:TPU:1, one launch (start us, length us, event | category | flops | bytes accessed | tf_op | source)
XLA Modules:
  0.0 34.5 jit_solution(1823053641194194055)
XLA Ops:
  0.0 0.0 copy-start.1
  0.0 0.0 copy-start
  0.0 0.0 copy-start.5
  0.0 1.5 %pack.1 = (bf16[896,128]{1,0:T(8,128)(2,1)S(1)}, bf16[896,128]{1,0:T(8,128)(2,1)S(1)}, bf16[16,128]{1,0:T(8,128)(2,1)S(1)}, bf16[16,128]{1,0:T(8,128)(2,1)S(1)}) custom-call(s32[1]{0:T(128)} %bitcast.t_ref, s32[1]{0:T(128)} %bitcast.1.l_ref, bf16[32,64,128]{2,1,0:T(8,128)(2,1)} %f_ref.5, bf16[32,64,128]{2,1,0:T(8,128)(2,1)} %s_ref.5, bf16[8,256,128]{2,1,0:T(8,128)(2,1)} %h_ref.5), custom_call_target="tpu_custom_call" | custom-call | tf_op jit(solution)/shard_map/pack/pallas_call | solution.py:72
  1.5 1.5 %collective-permute-start = (bf16[896,128]{1,0:T(8,128)(2,1)S(1)}, bf16[896,128]{1,0:T(8,128)(2,1)S(1)}, u32[]{:S(2)}, u32[]{:S(2)}) collective-permute-start(bf16[896,128]{1,0:T(8,128)(2,1)S(1)} %get-tuple-element.16), channel_id=1, source_target_pairs={{0,1},{2,3},{4,5},{6,7},{8,9},{10,11},{12,13},{14,15},{16,17},{18,... | collective-permute-start | bytes 688136 | tf_op jit(solution)/shard_map/rim_near/ppermute | solution.py:531
  3.0 3.7 %collective-permute-start.1 = (bf16[896,128]{1,0:T(8,128)(2,1)S(1)}, bf16[896,128]{1,0:T(8,128)(2,1)S(1)}, u32[]{:S(2)}, u32[]{:S(2)}) collective-permute-start(bf16[896,128]{1,0:T(8,128)(2,1)S(1)} %get-tuple-element.17), channel_id=1, source_target_pairs={{1,2},{3,4},{5,6},{7,8},{9,10},{11,12},{13,14},{15,16},{17,18},{19... | collective-permute-start | bytes 688136 | tf_op jit(solution)/shard_map/rim_far/ppermute | solution.py:529
  6.7 0.7 %collective-permute-start.2 = (bf16[16,128]{1,0:T(8,128)(2,1)S(1)}, bf16[16,128]{1,0:T(8,128)(2,1)S(1)}, u32[]{:S(2)}, u32[]{:S(2)}) collective-permute-start(bf16[16,128]{1,0:T(8,128)(2,1)S(1)} %get-tuple-element.18), channel_id=1, source_target_pairs={{0,4},{8,12},{16,20},{24,28},{32,36},{40,44},{48,52},{56,60},{64,6... | collective-permute-start | bytes 12296 | tf_op jit(solution)/shard_map/state_near/ppermute | solution.py:533
  7.4 5.4 %collective-permute-start.3 = (bf16[16,128]{1,0:T(8,128)(2,1)S(1)}, bf16[16,128]{1,0:T(8,128)(2,1)S(1)}, u32[]{:S(2)}, u32[]{:S(2)}) collective-permute-start(bf16[16,128]{1,0:T(8,128)(2,1)S(1)} %get-tuple-element.19), channel_id=1, source_target_pairs={{4,8},{12,16},{20,24},{28,32},{36,40},{44,48},{52,56},{60,64},{68,... | collective-permute-start | bytes 12296 | tf_op jit(solution)/shard_map/state_far/ppermute | solution.py:535
  12.8 0.0 copy-done.1
  12.8 0.0 copy-done
  12.8 0.0 copy-done.5
  12.8 1.5 %inner.1 = (bf16[864,128]{1,0:T(8,128)(2,1)S(1)}, bf16[864,128]{1,0:T(8,128)(2,1)S(1)}, bf16[576,128]{1,0:T(8,128)(2,1)S(1)}, bf16[992,128]{1,0:T(8,128)(2,1)S(1)}) custom-call(s32[1]{0:T(128)} %bitcast.t_ref, bf16[32,64,128]{2,1,0:T(8,128)(2,1)S(1)} %copy-done, bf16[32,64,128]{2,1,0:T(8,128)(2,1)S(1)} %copy-done.1, bf16[289,128]{1,0:T(8,128)(2,1)S(1)} %copy-done.5), custom_call_target="tpu_custom_call" | custom-call | flops 1000000000 | bytes 1000000 | tf_op jit(solution)/shard_map/inner/pallas_call | solution.py:151
  14.3 0.1 collective-permute-start.5
  14.4 0.0 collective-permute-done.2.near_ref
  14.4 0.0 collective-permute-done.3.far_ref
  14.4 0.0 collective-permute-done.a_ref
  14.4 0.0 collective-permute-done.1.b_ref
  14.4 0.0 copy-start.2
  14.4 0.0 copy-start.3
  14.5 0.0 copy-start.4
  14.5 0.0 copy-start.6
  14.5 1.2 %edge.1 = (bf16[400,128]{1,0:T(8,128)(2,1)S(1)}, bf16[1232,128]{1,0:T(8,128)(2,1)S(1)}, bf16[848,128]{1,0:T(8,128)(2,1)S(1)}) custom-call(s32[1]{0:T(128)} %bitcast.t_ref, bf16[32,64,128]{2,1,0:T(8,128)(2,1)S(1)} %copy-done, bf16[32,64,128]{2,1,0:T(8,128)(2,1)S(1)} %copy-done.1, bf16[896,128]{1,0:T(8,128)(2,1)S(1)} %collective-permute-done.a_ref, ...), custom_call_target="tpu_custom_call" | custom-call | flops 1000000000 | bytes 1000000 | tf_op jit(solution)/shard_map/edge/pallas_call | solution.py:226
  15.7 5.4 %collective-permute-start.4 = (bf16[848,128]{1,0:T(8,128)(2,1)S(1)}, bf16[848,128]{1,0:T(8,128)(2,1)S(1)}, u32[]{:S(2)}, u32[]{:S(2)}) collective-permute-start(bf16[848,128]{1,0:T(8,128)(2,1)S(1)} %get-tuple-element.24), channel_id=1, source_target_pairs={{0,1},{1,0},{2,3},{3,2},{4,5},{5,4},{6,7},{7,6},{8,9},{9,8},{10,11... | collective-permute-start | bytes 651272 | tf_op jit(solution)/shard_map/own_core/ppermute | solution.py:543
  21.0 0.0 collective-permute-start.6
  21.0 0.4 %collective-permute-done.5.zi_ref.i_ref = bf16[864,128]{1,0:T(8,128)(2,1)S(1)} collective-permute-done((bf16[864,128]{1,0:T(8,128)(2,1)S(1)}, bf16[864,128]{1,0:T(8,128)(2,1)S(1)}, u32[]{:S(2)}, u32[]{:S(2)}) %collective-permute-start.5) | collective-permute-done | bytes 221216 | tf_op jit(solution)/shard_map/inner_chip/ppermute | solution.py:538
  21.4 0.7 %collective-permute-done.4.mate_ref = bf16[848,128]{1,0:T(8,128)(2,1)S(1)} collective-permute-done((bf16[848,128]{1,0:T(8,128)(2,1)S(1)}, bf16[848,128]{1,0:T(8,128)(2,1)S(1)}, u32[]{:S(2)}, u32[]{:S(2)}) %collective-permute-start.4) | collective-permute-done | bytes 217120 | tf_op jit(solution)/shard_map/own_core/ppermute | solution.py:543
  22.1 0.0 copy-done.2
  22.1 0.0 copy-done.3
  22.1 0.0 copy-done.4
  22.1 0.0 copy-done.6
  22.1 3.5 %first_part.1.one_ref = bf16[8,112,128]{2,1,0:T(8,128)(2,1)S(1)} custom-call(s32[1]{0:T(128)} %bitcast.t_ref, f32[32]{0:T(128)S(1)} %copy-done.6, bf16[8,256,128]{2,1,0:T(8,128)(2,1)S(1)} %copy-done.2, bf16[896,128]{1,0:T(8,128)(2,1)S(1)} %collective-permute-done.a_ref, bf16[896,128]{1,0:T(8,128)(2,1)S(1)} %collective-permute-done.1.b_ref, ...), custom_call_target="tpu_custom_call" | custom-call | flops 4000000000 | bytes 4000000 | tf_op jit(solution)/shard_map/first_part/pallas_call | solution.py:369
  25.7 1.3 %collective-permute-done.6.e_ref = bf16[400,128]{1,0:T(8,128)(2,1)S(1)} collective-permute-done((bf16[400,128]{1,0:T(8,128)(2,1)S(1)}, bf16[400,128]{1,0:T(8,128)(2,1)S(1)}, u32[]{:S(2)}, u32[]{:S(2)}) %collective-permute-start.6) | collective-permute-done | bytes 102432 | tf_op jit(solution)/shard_map/edge_chip/ppermute | solution.py:541
  27.0 1.0 %collective-permute-start.7 = (bf16[1264,128]{1,0:T(8,128)(2,1)S(1)}, bf16[1264,128]{1,0:T(8,128)(2,1)S(1)}, u32[]{:S(2)}, u32[]{:S(2)}) collective-permute-start(bf16[1264,128]{1,0:T(8,128)(2,1)S(1)} %join.1.z_ref), channel_id=1, source_target_pairs={{0,1},{1,0},{2,3},{3,2},{4,5},{5,4},{6,7},{7,6},{8,9},{9,8},{10,11... | collective-permute-start | bytes 970760 | tf_op jit(solution)/shard_map/chip_core/ppermute | solution.py:547
  28.0 1.2 %collective-permute-done.7.k_ref = bf16[1264,128]{1,0:T(8,128)(2,1)S(1)} collective-permute-done((bf16[1264,128]{1,0:T(8,128)(2,1)S(1)}, bf16[1264,128]{1,0:T(8,128)(2,1)S(1)}, u32[]{:S(2)}, u32[]{:S(2)}) %collective-permute-start.7) | collective-permute-done | bytes 323616 | tf_op jit(solution)/shard_map/chip_core/ppermute | solution.py:547
  29.2 5.3 %second_part.1 = bf16[8,256,128]{2,1,0:T(8,128)(2,1)} custom-call(s32[1]{0:T(128)} %bitcast.t_ref, s32[1]{0:T(128)} %bitcast.1.l_ref, f32[32]{0:T(128)S(1)} %copy-done.6, bf16[8,256,128]{2,1,0:T(8,128)(2,1)S(1)} %copy-done.2, bf16[896,128]{1,0:T(8,128)(2,1)S(1)} %collective-permute-done.a_ref, bf16[896,128]{1,0:T(8,128)(2,1)S(1)} %collective-permute-done.1.b_ref, ...), custom_call_target="tpu_custom_call" | custom-call | flops 5000000000 | bytes 4000000 | tf_op jit(solution)/shard_map/second_part/pallas_call | solution.py:488
  (1 shorter events, 0.0 us)
Async XLA Ops:
  0.0 12.8 %copy-start.1 = (bf16[32,64,128]{2,1,0:T(8,128)(2,1)S(1)}, bf16[32,64,128]{2,1,0:T(8,128)(2,1)}, u32[]{:S(2)}) copy-start(bf16[32,64,128]{2,1,0:T(8,128)(2,1)} %s_ref.5) | copy-start | bytes 1572868
  0.0 12.8 %copy-start = (bf16[32,64,128]{2,1,0:T(8,128)(2,1)S(1)}, bf16[32,64,128]{2,1,0:T(8,128)(2,1)}, u32[]{:S(2)}) copy-start(bf16[32,64,128]{2,1,0:T(8,128)(2,1)} %f_ref.5) | copy-start | bytes 1572868
  0.0 12.8 %copy-start.5 = (bf16[289,128]{1,0:T(8,128)(2,1)S(1)}, bf16[289,128]{1,0:T(8,128)(2,1)}, u32[]{:S(2)}) copy-start(bf16[289,128]{1,0:T(8,128)(2,1)} %enc_ref.1) | copy-start | bytes 221956
  1.5 12.9 %collective-permute-start = (bf16[896,128]{1,0:T(8,128)(2,1)S(1)}, bf16[896,128]{1,0:T(8,128)(2,1)S(1)}, u32[]{:S(2)}, u32[]{:S(2)}) collective-permute-start(bf16[896,128]{1,0:T(8,128)(2,1)S(1)} %get-tuple-element.16), channel_id=1, source_target_pairs={{0,1},{2,3},{4,5},{6,7},{8,9},{10,11},{12,13},{14,15},{16,17},{18,... | collective-permute-start | bytes 688136 | tf_op jit(solution)/shard_map/rim_near/ppermute | solution.py:531
  3.0 11.4 %collective-permute-start.1 = (bf16[896,128]{1,0:T(8,128)(2,1)S(1)}, bf16[896,128]{1,0:T(8,128)(2,1)S(1)}, u32[]{:S(2)}, u32[]{:S(2)}) collective-permute-start(bf16[896,128]{1,0:T(8,128)(2,1)S(1)} %get-tuple-element.17), channel_id=1, source_target_pairs={{1,2},{3,4},{5,6},{7,8},{9,10},{11,12},{13,14},{15,16},{17,18},{19... | collective-permute-start | bytes 688136 | tf_op jit(solution)/shard_map/rim_far/ppermute | solution.py:529
  6.7 7.8 %collective-permute-start.2 = (bf16[16,128]{1,0:T(8,128)(2,1)S(1)}, bf16[16,128]{1,0:T(8,128)(2,1)S(1)}, u32[]{:S(2)}, u32[]{:S(2)}) collective-permute-start(bf16[16,128]{1,0:T(8,128)(2,1)S(1)} %get-tuple-element.18), channel_id=1, source_target_pairs={{0,4},{8,12},{16,20},{24,28},{32,36},{40,44},{48,52},{56,60},{64,6... | collective-permute-start | bytes 12296 | tf_op jit(solution)/shard_map/state_near/ppermute | solution.py:533
  7.4 7.0 %collective-permute-start.3 = (bf16[16,128]{1,0:T(8,128)(2,1)S(1)}, bf16[16,128]{1,0:T(8,128)(2,1)S(1)}, u32[]{:S(2)}, u32[]{:S(2)}) collective-permute-start(bf16[16,128]{1,0:T(8,128)(2,1)S(1)} %get-tuple-element.19), channel_id=1, source_target_pairs={{4,8},{12,16},{20,24},{28,32},{36,40},{44,48},{52,56},{60,64},{68,... | collective-permute-start | bytes 12296 | tf_op jit(solution)/shard_map/state_far/ppermute | solution.py:535
  14.3 7.1 %collective-permute-start.5 = (bf16[864,128]{1,0:T(8,128)(2,1)S(1)}, bf16[864,128]{1,0:T(8,128)(2,1)S(1)}, u32[]{:S(2)}, u32[]{:S(2)}) collective-permute-start(bf16[864,128]{1,0:T(8,128)(2,1)S(1)} %get-tuple-element.25), channel_id=1, source_target_pairs={{0,2},{1,3},{2,0},{3,1},{4,6},{5,7},{6,4},{7,5},{8,10},{9,11},{10,... | collective-permute-start | bytes 663560 | tf_op jit(solution)/shard_map/inner_chip/ppermute | solution.py:538
  14.4 7.7 %copy-start.2 = (bf16[8,256,128]{2,1,0:T(8,128)(2,1)S(1)}, bf16[8,256,128]{2,1,0:T(8,128)(2,1)}, u32[]{:S(2)}) copy-start(bf16[8,256,128]{2,1,0:T(8,128)(2,1)} %h_ref.5) | copy-start | bytes 1572868
  14.4 7.7 %copy-start.3 = (bf16[3,3,256,256]{3,2,1,0:T(8,128)(2,1)S(1)}, bf16[3,3,256,256]{3,2,1,0:T(8,128)(2,1)}, u32[]{:S(2)}) copy-start(bf16[3,3,256,256]{3,2,1,0:T(8,128)(2,1)} %gw_ref.3) | copy-start | bytes 3538948
  14.5 7.7 %copy-start.4 = (bf16[3,3,256,128]{3,2,1,0:T(8,128)(2,1)S(1)}, bf16[3,3,256,128]{3,2,1,0:T(8,128)(2,1)}, u32[]{:S(2)}) copy-start(bf16[3,3,256,128]{3,2,1,0:T(8,128)(2,1)} %cw_ref.3) | copy-start | bytes 1769476
  14.5 7.7 %copy-start.6 = (f32[32]{0:T(128)S(1)}, f32[32]{0:T(128)}, u32[]{:S(2)}) copy-start(f32[32]{0:T(128)} %metric_ref.3) | copy-start | bytes 388
  15.7 6.4 %collective-permute-start.4 = (bf16[848,128]{1,0:T(8,128)(2,1)S(1)}, bf16[848,128]{1,0:T(8,128)(2,1)S(1)}, u32[]{:S(2)}, u32[]{:S(2)}) collective-permute-start(bf16[848,128]{1,0:T(8,128)(2,1)S(1)} %get-tuple-element.24), channel_id=1, source_target_pairs={{0,1},{1,0},{2,3},{3,2},{4,5},{5,4},{6,7},{7,6},{8,9},{9,8},{10,11... | collective-permute-start | bytes 651272 | tf_op jit(solution)/shard_map/own_core/ppermute | solution.py:543
  21.0 5.9 %collective-permute-start.6 = (bf16[400,128]{1,0:T(8,128)(2,1)S(1)}, bf16[400,128]{1,0:T(8,128)(2,1)S(1)}, u32[]{:S(2)}, u32[]{:S(2)}) collective-permute-start(bf16[400,128]{1,0:T(8,128)(2,1)S(1)} %get-tuple-element.26), channel_id=1, source_target_pairs={{0,2},{1,3},{2,0},{3,1},{4,6},{5,7},{6,4},{7,5},{8,10},{9,11},{10,... | collective-permute-start | bytes 307208 | tf_op jit(solution)/shard_map/edge_chip/ppermute | solution.py:541
  27.0 2.2 %collective-permute-start.7 = (bf16[1264,128]{1,0:T(8,128)(2,1)S(1)}, bf16[1264,128]{1,0:T(8,128)(2,1)S(1)}, u32[]{:S(2)}, u32[]{:S(2)}) collective-permute-start(bf16[1264,128]{1,0:T(8,128)(2,1)S(1)} %join.1.z_ref), channel_id=1, source_target_pairs={{0,1},{1,0},{2,3},{3,2},{4,5},{5,4},{6,7},{7,6},{8,9},{9,8},{10,11... | collective-permute-start | bytes 970760 | tf_op jit(solution)/shard_map/chip_core/ppermute | solution.py:547

commit v5 on v4

--- a/solution.py
+++ b/solution.py
@@ -51,6 +51,8 @@
     far_ref[...] = jnp.where(even, west, east).astype(BF)
     even = lax.rem(t_ref[0], 2) == 0
 
+    b_ref[896:912] = jnp.zeros((16, 128), BF)
+
     def put(n_ref, p_ref):
         n_ref[0:384] = up[...].astype(BF)
         p_ref[0:384] = down[...].astype(BF)
@@ -71,7 +73,7 @@
     hbm = pl.BlockSpec(memory_space=pl.ANY)
     return pl.pallas_call(
         pack_kernel,
-        out_shape=(pltpu.VMEM((896, 128), BF),) * 2 + (pltpu.VMEM((16, 128), BF),) * 2,
+        out_shape=(pltpu.VMEM((896, 128), BF), pltpu.VMEM((912, 128), BF)) + (pltpu.VMEM((16, 128), BF),) * 2,
         in_specs=[SM, SM, hbm, hbm, hbm],
         out_specs=(VM,) * 4,
         scratch_shapes=[
@@ -167,7 +169,7 @@
     )(t, f, s, enc)
 
 
-def edge_kernel(t_ref, f_ref, s_ref, a_ref, b_ref, near_ref, far_ref, w_ref, oi_ref, ci_ref, z_ref, o_ref, c_ref, fe, se, hal, band, acc):
+def edge_kernel(t_ref, f_ref, s_ref, a_ref, b_ref, near_ref, far_ref, w_ref, oi_ref, ci_ref, state_ref, z_ref, o_ref, c_ref, fe, se, hal, band, acc):
     t = t_ref[0]
     odd = lax.rem(t, 2)
     for n, ref in ((1 - odd, a_ref), (odd, b_ref)):
@@ -222,11 +224,11 @@
         bot[...] = jnp.where(t == 1, b_ref[384:896].astype(F32), 0.0)
 
 
-def edge(t, f, s, a, b, near, far, w_wide, oi, ci):
+def edge(t, f, s, a, b, near, far, w_wide, oi, ci, state):
     return pl.pallas_call(
         edge_kernel,
         out_shape=(jax.ShapeDtypeStruct((400, 128), BF), jax.ShapeDtypeStruct((1232, 128), BF), jax.ShapeDtypeStruct((848, 128), BF)),
-        in_specs=[SM] + [VM] * 9,
+        in_specs=[SM] + [VM] * 10,
         out_specs=(VM,) * 3,
         scratch_shapes=[
             pltpu.VMEM((32, 32, 128), F32),
@@ -238,7 +240,7 @@
         compiler_params=pltpu.CompilerParams(vmem_limit_bytes=24 << 20),
         cost_estimate=pl.CostEstimate(flops=1000000000, bytes_accessed=1000000, transcendentals=0),
         name="edge",
-    )(t, f, s, a, b, near, far, w_wide, oi, ci)
+    )(t, f, s, a, b, near, far, w_wide, oi, ci, state)
 
 
 def join_kernel(i_ref, e_ref, one_ref, o_ref):
@@ -265,18 +267,97 @@
         hs[512 + 256 * i : 768 + 256 * i] = h_ref[i].astype(F32)
 
 
-def gates(metric_ref, t, x, gw_ref, width, put):
-    sides_w = jnp.concatenate([gw_ref[p, q] for q in (0, 2) for p in range(3)], axis=0)
-    center_w = jnp.concatenate([gw_ref[p, 1] for p in range(3)], axis=0)
+def gate_products(x, gw_ref, width, i, lanes):
+    def part(qs):
+        lhs = jnp.concatenate([x[q, i + p : i + p + 2, :, lanes[0]].reshape(2 * width, -1) for q in qs for p in range(3)], axis=1)
+        rhs = jnp.concatenate([gw_ref[p, q, lanes[1]] for q in qs for p in range(3)], axis=0)
+        return jnp.dot(lhs, rhs, preferred_element_type=F32)
+
+    return part((0, 2)), part((1,))
+
+
+def gates(metric_ref, t, x, gw_ref, state_ref, width, put):
     for i in range(0, 10, 2):
-        lhs = jnp.concatenate([x[q, i + p : i + p + 2].reshape(2 * width, 256) for q in (0, 2) for p in range(3)], axis=1)
-        sides = jnp.dot(lhs, sides_w, preferred_element_type=F32)
-        lhs = jnp.concatenate([x[1, i + p : i + p + 2].reshape(2 * width, 256) for p in range(3)], axis=1)
-        center = jnp.dot(lhs, center_w, preferred_element_type=F32)
+        known = 2 <= i < 8
+        half = slice(128, 256)
+        sides, center = gate_products(x, gw_ref, width, i, (half, half) if known else (slice(0, 256), slice(0, 256)))
         for n in range(2):
             cut = slice(width * n, width * n + width)
             gate = center[cut] + sides[cut] * metric_ref[jnp.clip(8 * t + i + n - 1, 0, 31)]
+            if known:
+                gate = gate + state_ref[i + n - 2]
             put(i + n, 0.5 * jnp.tanh(0.5 * gate) + 0.5)
+
+
+def state_products(metric_ref, t, x, gw_ref, width, out):
+    for i in range(0, 6, 2):
+        sides, center = gate_products(x, gw_ref, width, i, (slice(0, 128), slice(0, 128)))
+        for n in range(2):
+            cut = slice(width * n, width * n + width)
+            out[i + n] = center[cut] + sides[cut] * metric_ref[8 * t + i + n + 1]
+
+
+def state_first_kernel(t_ref, metric_ref, h_ref, gw_ref, out_ref, hs, x):
+    t = t_ref[0]
+    for i in range(8):
+        hs[256 * i : 256 * i + 256] = h_ref[i].astype(F32)
+    for q in range(3):
+        for i in range(8):
+            x[q, i] = hs[pl.ds(256 * i + 112 * (t // 2) + 14 + q, 128)].astype(BF)
+    state_products(metric_ref, t, x, gw_ref, 128, out_ref)
+
+
+def state_second_kernel(t_ref, l_ref, metric_ref, h_ref, near_ref, far_ref, gw_ref, out_ref, hs, hf, x):
+    t = t_ref[0]
+    high = t // 2
+    c0 = pl.multiple_of(128 - 128 * high, 128)
+    west_even = lax.rem(l_ref[0], 2) == 0
+    near, far = near_ref[...].astype(F32), far_ref[...].astype(F32)
+    hr = jnp.where(west_even, near, far)
+    hl = jnp.where(west_even, far, near)
+    for i in range(8):
+        hs[256 * i : 256 * i + 256] = h_ref[i].astype(F32)
+    for i in range(8):
+        outer(hf, hs, i, c0, high, hl[2 * i : 2 * i + 2], hr[2 * i : 2 * i + 2])
+    for q in range(3):
+        for i in range(8):
+            x[q, i] = hf[i, q : q + 176].astype(BF)
+    state_products(metric_ref, t, x, gw_ref, 176, out_ref)
+
+
+def outer(hf, hs, i, c0, high, side_w, side_e):
+    low = high == 0
+    hf[i, 2:130] = hs[pl.ds(256 * i + c0, 128)]
+    hf[i, 0:2] = jnp.where(low, hs[256 * i + 126 : 256 * i + 128], side_w)
+    hf[i, 130:132] = jnp.where(low, side_e, hs[256 * i + 128 : 256 * i + 130])
+    hf[i, pl.ds(146 - 2 * high, 18)] = hs[pl.ds(256 * i + 238 * high, 18)]
+    hf[i, pl.ds(144 + 18 * high, 2)] = jnp.where(low, side_w, side_e)
+
+
+def state_first(t, metric, h, gw):
+    return pl.pallas_call(
+        state_first_kernel,
+        out_shape=jax.ShapeDtypeStruct((6, 128, 256), F32),
+        in_specs=[SM, SM] + [VM] * 2,
+        out_specs=VM,
+        scratch_shapes=[pltpu.VMEM((2048, 128), F32), pltpu.VMEM((3, 8, 128, 128), BF)],
+        compiler_params=pltpu.CompilerParams(vmem_limit_bytes=24 << 20),
+        cost_estimate=pl.CostEstimate(flops=10**9, bytes_accessed=2 << 20, transcendentals=0),
+        name="state_first",
+    )(t, metric, h, gw)
+
+
+def state_second(t, l, metric, h, near, far, gw):
+    return pl.pallas_call(
+        state_second_kernel,
+        out_shape=jax.ShapeDtypeStruct((6, 176, 256), F32),
+        in_specs=[SM, SM, SM] + [VM] * 4,
+        out_specs=VM,
+        scratch_shapes=[pltpu.VMEM((2048, 128), F32), pltpu.VMEM((8, 184, 128), F32), pltpu.VMEM((3, 8, 176, 128), BF)],
+        compiler_params=pltpu.CompilerParams(vmem_limit_bytes=24 << 20),
+        cost_estimate=pl.CostEstimate(flops=10**9, bytes_accessed=2 << 20, transcendentals=0),
+        name="state_second",
+    )(t, l, metric, h, near, far, gw)
 
 
 def candidates(metric_ref, t, x, m3s, r, cw_ref, width, put):
@@ -314,7 +395,7 @@
     return mid, ends
 
 
-def first_kernel(t_ref, metric_ref, h_ref, a_ref, b_ref, own_ref, mate_ref, zi_ref, gw_ref, cw_ref, out_ref, hs, mf, x, m3s, rf, r, ug, top, bot, rims):
+def first_kernel(t_ref, metric_ref, h_ref, a_ref, b_ref, own_ref, mate_ref, state_ref, gw_ref, cw_ref, out_ref, hs, mf, x, m3s, rf, r, ug, top, bot, rims):
     t = t_ref[0]
     high = t // 2
     base = 112 * high
@@ -342,7 +423,8 @@
 
     for q in range(3):
         for i in range(12):
-            x[q, i, :, 0:128] = hs[pl.ds(256 * i + base + 14 + q, 128)].astype(BF)
+            if not 4 <= i < 8:
+                x[q, i, :, 0:128] = hs[pl.ds(256 * i + base + 14 + q, 128)].astype(BF)
             x[q, i, :, 128:256] = mf[i, 14 + q : 142 + q].astype(BF)
     for i in range(12):
         m3s[i] = mf[i, 17:129].astype(BF)
@@ -352,7 +434,7 @@
         if 1 <= i < 9:
             ug[i - 1] = gate[:, 0:128]
 
-    gates(metric_ref, t, x, gw_ref, 128, put_gate)
+    gates(metric_ref, t, x, gw_ref, state_ref, 128, put_gate)
     for q in range(3):
         for i in range(10):
             r[q, i] = rf[i, q : q + 112].astype(BF)
@@ -365,7 +447,7 @@
     candidates(metric_ref, t, x, m3s, r, cw_ref, 112, put_new)
 
 
-def first_part(t, metric, h, a, b, own, mate, zi, gw, cw):
+def first_part(t, metric, h, a, b, own, mate, state, gw, cw):
     return pl.pallas_call(
         first_kernel,
         out_shape=jax.ShapeDtypeStruct((8, 112, 128), BF),
@@ -384,13 +466,13 @@
             pltpu.VMEM((80, 128), F32),
         ],
         compiler_params=pltpu.CompilerParams(vmem_limit_bytes=24 << 20),
-        cost_estimate=pl.CostEstimate(flops=4000000000, bytes_accessed=4000000, transcendentals=0),
+        cost_estimate=pl.CostEstimate(flops=10**7, bytes_accessed=10**5, transcendentals=0),
         name="first_part",
-    )(t, metric, h, a, b, own, mate, zi, gw, cw)
+    )(t, metric, h, a, b, own, mate, state, gw, cw)
 
 
 def second_kernel(
-    t_ref, l_ref, metric_ref, h_ref, a_ref, b_ref, near_ref, far_ref, own_ref, mate_ref, z_ref, k_ref, gw_ref, cw_ref, one_ref, out_ref,
+    t_ref, l_ref, metric_ref, h_ref, a_ref, b_ref, near_ref, far_ref, own_ref, mate_ref, z_ref, k_ref, state_ref, gw_ref, cw_ref, one_ref, out_ref,
     ob, sem, hs, hf, mf, x, m3s, rf, r, ug, top, bot, rims,
 ):
     t = t_ref[0]
@@ -412,12 +494,7 @@
     hr = jnp.where(west_even, near, far)
     hl = jnp.where(west_even, far, near)
     for i in range(12):
-        hf[i, 2:130] = hs[pl.ds(256 * i + c0, 128)]
-        side_w, side_e = hl[2 * i : 2 * i + 2], hr[2 * i : 2 * i + 2]
-        hf[i, 0:2] = jnp.where(low, hs[256 * i + 126 : 256 * i + 128], side_w)
-        hf[i, 130:132] = jnp.where(low, side_e, hs[256 * i + 128 : 256 * i + 130])
-        hf[i, pl.ds(146 - 2 * high, 18)] = hs[pl.ds(256 * i + 238 * high, 18)]
-        hf[i, pl.ds(144 + 18 * high, 2)] = jnp.where(low, side_w, side_e)
+        outer(hf, hs, i, c0, high, hl[2 * i : 2 * i + 2], hr[2 * i : 2 * i + 2])
     start = 8 * t - 2 - 14 * high
     for s, ref in ((odd, z_ref), (1 - odd, k_ref)):
         rims[0:80] = ref[1152:1232].astype(F32)
@@ -455,7 +532,8 @@
         mf[i, pl.ds(144 + 18 * high, 2)] = jnp.where(inside, v, 0.0)
     for q in range(3):
         for i in range(12):
-            x[q, i, :, 0:128] = hf[i, q : q + 176].astype(BF)
+            if not 4 <= i < 8:
+                x[q, i, :, 0:128] = hf[i, q : q + 176].astype(BF)
             x[q, i, :, 128:256] = mf[i, q : q + 176].astype(BF)
     for i in range(12):
         m3s[i] = mf[i, 3:163].astype(BF)
@@ -465,7 +543,7 @@
         if 1 <= i < 9:
             ug[i - 1] = gate[:, 0:128]
 
-    gates(metric_ref, t, x, gw_ref, 176, put_gate)
+    gates(metric_ref, t, x, gw_ref, state_ref, 176, put_gate)
     for q in range(3):
         for i in range(10):
             r[q, i] = rf[i, q : q + 160].astype(BF)
@@ -484,11 +562,11 @@
         pltpu.make_async_copy(ob.at[i], out_ref.at[i], sem.at[i]).wait()
 
 
-def second_part(t, l, metric, h, a, b, near, far, own, mate, z, k, gw, cw, one):
+def second_part(t, l, metric, h, a, b, near, far, own, mate, z, k, state, gw, cw, one):
     return pl.pallas_call(
         second_kernel,
         out_shape=jax.ShapeDtypeStruct((8, 256, 128), BF),
-        in_specs=[SM, SM, SM] + [VM] * 12,
+        in_specs=[SM, SM, SM] + [VM] * 13,
         out_specs=pl.BlockSpec(memory_space=pl.ANY),
         scratch_shapes=[
             pltpu.VMEM((8, 256, 128), BF),
@@ -508,7 +586,7 @@
         compiler_params=pltpu.CompilerParams(vmem_limit_bytes=24 << 20),
         cost_estimate=pl.CostEstimate(flops=5000000000, bytes_accessed=4000000, transcendentals=0),
         name="second_part",
-    )(t, l, metric, h, a, b, near, far, own, mate, z, k, gw, cw, one)
+    )(t, l, metric, h, a, b, near, far, own, mate, z, k, state, gw, cw, one)
 
 
 def swaps(n, first):
@@ -536,16 +614,18 @@
     zi_send, oi, ci, w_wide = inner(t, first, second, encoder_weight)
     with jax.named_scope("inner_chip"):
         zi = lax.ppermute(zi_send, "lat", chip)
-    ze_send, own, own_send = edge(t, first, second, a, b, near, far, w_wide, oi, ci)
+    state_one = state_first(t, row_metric, hidden, gates_weight)
+    state_two = state_second(t, l, row_metric, hidden, near, far, gates_weight)
+    ze_send, own, own_send = edge(t, first, second, a, b, near, far, w_wide, oi, ci, state_one)
     with jax.named_scope("edge_chip"):
         ze = lax.ppermute(ze_send, "lat", chip)
     with jax.named_scope("own_core"):
         mate = lax.ppermute(own_send, "lat", core)
-    one = first_part(t, row_metric, hidden, a, b, own, mate, zi, gates_weight, candidate_weight)
+    one = first_part(t, row_metric, hidden, a, b, own, mate, state_one, gates_weight, candidate_weight)
     z = join(zi, ze, one)
     with jax.named_scope("chip_core"):
         k = lax.ppermute(z, "lat", core)
-    return second_part(t, l, row_metric, hidden, a, b, near, far, own, mate, z, k, gates_weight, candidate_weight, one)
+    return second_part(t, l, row_metric, hidden, a, b, near, far, own, mate, z, k, state_two, gates_weight, candidate_weight, one)
 
 
 def solution(mesh):

time: 34.6 us -> 33.9 us (0.980)
  starting transfers between devices: 17.7 us -> 14.5 us
  Pallas kernels: 13.1 us -> 15.1 us
  waiting for transfers between devices: 3.64 us -> 4.02 us
    ppermute x1, starting transfers between devices: 5.35 us -> 1.15 us  [body(): mate = lax.ppermute(own_send, 'lat', core)]
    ppermute x1, starting transfers between devices: 5.37 us -> 1.72 us  [body(): far = lax.ppermute(far_send, 'lon', swaps(count, 1))]
    ppermute x1, starting transfers between devices: 1.49 us -> 4.64 us  [body(): a = lax.ppermute(a_send, BOTH, swaps(slabs, 0))]
    pallas_call x1 -> x3, Pallas kernels: 1.47 us -> 4.36 us  [the longest x1 1.57 us: state_second(): pl.pallas_call(state_second_kernel, out_shape=jax.ShapeDtypeStruct((6, 17...]
    ppermute x1, waiting for transfers between devices: 0.01 us -> 2.14 us  [body(): far = lax.ppermute(far_send, 'lon', swaps(count, 1))]
    ppermute x1, starting transfers between devices: 3.67 us -> 5.06 us  [body(): b = lax.ppermute(b_send, BOTH, swaps(slabs, 1))]
    ppermute x1, waiting for transfers between devices: 1.25 us -> 0.01 us  [body(): k = lax.ppermute(z, 'lat', core)]
    ppermute x1, starting transfers between devices: 0.01 us -> 0.86 us  [body(): ze = lax.ppermute(ze_send, 'lat', chip)]
  transfers between devices with their start and end apart: 8 -> 8, of which waited for: 4 -> 3; matrix products, arithmetic and copies ran while one was open for 0% -> 0% of each run, Pallas kernels for 18% -> 26%
where the time goes in v5:
time: 33.9 us; the launch traced here: 33.7 us
  Pallas kernels  15.1 us (45%)
  starting transfers between devices  14.5 us (43%)
  waiting for transfers between devices  4.02 us (12%)
    ppermute x1, starting transfers between devices, body(): b = lax.ppermute(b_send, BOTH, swaps(slabs, 1))  5.06 us
    pallas_call x1, Pallas kernels, second_part(): pl.pallas_call(second_kernel, out_shape=jax.ShapeDtypeStruct((8, 256, 128...  4.78 us
    ppermute x1, starting transfers between devices, body(): a = lax.ppermute(a_send, BOTH, swaps(slabs, 0))  4.64 us
    pallas_call x1, Pallas kernels, first_part(): pl.pallas_call(first_kernel, out_shape=jax.ShapeDtypeStruct((8, 112, 128)...  3.19 us
    ppermute x1, waiting for transfers between devices, body(): far = lax.ppermute(far_send, 'lon', swaps(count, 1))  2.14 us
    ppermute x1, starting transfers between devices, body(): far = lax.ppermute(far_send, 'lon', swaps(count, 1))  1.72 us
    ppermute x1, waiting for transfers between devices, body(): ze = lax.ppermute(ze_send, 'lat', chip)  1.64 us
    pallas_call x1, Pallas kernels, state_second(): pl.pallas_call(state_second_kernel, out_shape=jax.ShapeDtypeStruct((6, 17...  1.57 us
  transfers between devices with their start and end apart: 8, of which 3 were waited for; matrix products, arithmetic and copies ran while one was open for 0% of the time, Pallas kernels for 26%

profile of v5, /device:TPU:1, one launch (start us, length us, event | category | flops | bytes accessed | tf_op | source)
XLA Modules:
  0.0 33.7 jit_solution(11846214095571536224)
XLA Ops:
  0.0 0.0 copy-start.4
  0.0 0.0 copy-start.3
  0.0 0.0 copy-start.6
  0.0 1.5 %pack.1 = (bf16[896,128]{1,0:T(8,128)(2,1)S(1)}, bf16[912,128]{1,0:T(8,128)(2,1)S(1)}, bf16[16,128]{1,0:T(8,128)(2,1)S(1)}, bf16[16,128]{1,0:T(8,128)(2,1)S(1)}) custom-call(s32[1]{0:T(128)} %bitcast.t_ref, s32[1]{0:T(128)} %bitcast.1.l_ref, bf16[32,64,128]{2,1,0:T(8,128)(2,1)} %f_ref.5, bf16[32,64,128]{2,1,0:T(8,128)(2,1)} %s_ref.5, bf16[8,256,128]{2,1,0:T(8,128)(2,1)} %h_ref.9), custom_call_target="tpu_custom_call" | custom-call | tf_op jit(solution)/shard_map/pack/pallas_call | solution.py:74
  1.5 5.1 %collective-permute-start.1 = (bf16[912,128]{1,0:T(8,128)(2,1)S(1)}, bf16[912,128]{1,0:T(8,128)(2,1)S(1)}, u32[]{:S(2)}, u32[]{:S(2)}) collective-permute-start(bf16[912,128]{1,0:T(8,128)(2,1)S(1)} %get-tuple-element.17), channel_id=1, source_target_pairs={{1,2},{3,4},{5,6},{7,8},{9,10},{11,12},{13,14},{15,16},{17,18},{19... | collective-permute-start | bytes 700424 | tf_op jit(solution)/shard_map/rim_far/ppermute | solution.py:607
  6.6 4.6 %collective-permute-start = (bf16[896,128]{1,0:T(8,128)(2,1)S(1)}, bf16[896,128]{1,0:T(8,128)(2,1)S(1)}, u32[]{:S(2)}, u32[]{:S(2)}) collective-permute-start(bf16[896,128]{1,0:T(8,128)(2,1)S(1)} %get-tuple-element.16), channel_id=1, source_target_pairs={{0,1},{2,3},{4,5},{6,7},{8,9},{10,11},{12,13},{14,15},{16,17},{18,... | collective-permute-start | bytes 688136 | tf_op jit(solution)/shard_map/rim_near/ppermute | solution.py:609
  11.2 0.0 collective-permute-start.2
  11.2 0.0 copy-start
  11.2 0.0 copy-start.1
  11.2 0.0 copy-start.5
  11.2 1.7 %collective-permute-start.3 = (bf16[16,128]{1,0:T(8,128)(2,1)S(1)}, bf16[16,128]{1,0:T(8,128)(2,1)S(1)}, u32[]{:S(2)}, u32[]{:S(2)}) collective-permute-start(bf16[16,128]{1,0:T(8,128)(2,1)S(1)} %get-tuple-element.19), channel_id=1, source_target_pairs={{4,8},{12,16},{20,24},{28,32},{36,40},{44,48},{52,56},{60,64},{68,... | collective-permute-start | bytes 12296 | tf_op jit(solution)/shard_map/state_far/ppermute | solution.py:613
  12.9 0.0 copy-done.4
  12.9 0.0 copy-done.3
  12.9 0.0 copy-done.6
  13.0 1.5 %inner.1 = (bf16[864,128]{1,0:T(8,128)(2,1)S(1)}, bf16[864,128]{1,0:T(8,128)(2,1)S(1)}, bf16[576,128]{1,0:T(8,128)(2,1)S(1)}, bf16[992,128]{1,0:T(8,128)(2,1)S(1)}) custom-call(s32[1]{0:T(128)} %bitcast.t_ref, bf16[32,64,128]{2,1,0:T(8,128)(2,1)S(1)} %copy-done.3, bf16[32,64,128]{2,1,0:T(8,128)(2,1)S(1)} %copy-done.4, bf16[289,128]{1,0:T(8,128)(2,1)S(1)} %copy-done.6), custom_call_target="tpu_custom_call" | custom-call | flops 1000000000 | bytes 1000000 | tf_op jit(solution)/shard_map/inner/pallas_call | solution.py:153
  14.5 0.1 collective-permute-start.5
  14.6 0.0 copy-done
  14.6 0.0 copy-done.1
  14.6 0.0 copy-done.5
  14.6 1.3 %state_first.1.state_ref = f32[6,128,256]{2,1,0:T(8,128)S(1)} custom-call(s32[1]{0:T(128)} %bitcast.t_ref, f32[32]{0:T(128)S(1)} %copy-done.5, bf16[8,256,128]{2,1,0:T(8,128)(2,1)S(1)} %copy-done, bf16[3,3,256,256]{3,2,1,0:T(8,128)(2,1)S(1)} %copy-done.1), custom_call_target="tpu_custom_call" | custom-call | flops 1000000000 | bytes 2097152 | tf_op jit(solution)/shard_map/state_first/pallas_call | solution.py:338
  15.9 0.0 collective-permute-done.2.near_ref
  15.9 2.1 %collective-permute-done.3.far_ref = bf16[16,128]{1,0:T(8,128)(2,1)S(1)} collective-permute-done((bf16[16,128]{1,0:T(8,128)(2,1)S(1)}, bf16[16,128]{1,0:T(8,128)(2,1)S(1)}, u32[]{:S(2)}, u32[]{:S(2)}) %collective-permute-start.3) | collective-permute-done | bytes 4128 | tf_op jit(solution)/shard_map/state_far/ppermute | solution.py:613
  18.1 0.0 collective-permute-done.a_ref
  18.1 0.0 collective-permute-done.1.b_ref
  18.1 0.0 copy-start.2
  18.1 1.2 %edge.1 = (bf16[400,128]{1,0:T(8,128)(2,1)S(1)}, bf16[1232,128]{1,0:T(8,128)(2,1)S(1)}, bf16[848,128]{1,0:T(8,128)(2,1)S(1)}) custom-call(s32[1]{0:T(128)} %bitcast.t_ref, bf16[32,64,128]{2,1,0:T(8,128)(2,1)S(1)} %copy-done.3, bf16[32,64,128]{2,1,0:T(8,128)(2,1)S(1)} %copy-done.4, bf16[896,128]{1,0:T(8,128)(2,1)S(1)} %collective-permute-done.a_ref, ...), custom_call_target="tpu_custom_call" | custom-call | flops 1000000000 | bytes 1000000 | tf_op jit(solution)/shard_map/edge/pallas_call | solution.py:228
  19.3 1.1 %collective-permute-start.4 = (bf16[848,128]{1,0:T(8,128)(2,1)S(1)}, bf16[848,128]{1,0:T(8,128)(2,1)S(1)}, u32[]{:S(2)}, u32[]{:S(2)}) collective-permute-start(bf16[848,128]{1,0:T(8,128)(2,1)S(1)} %get-tuple-element.24), channel_id=1, source_target_pairs={{0,1},{1,0},{2,3},{3,2},{4,5},{5,4},{6,7},{7,6},{8,9},{9,8},{10,11... | collective-permute-start | bytes 651272 | tf_op jit(solution)/shard_map/own_core/ppermute | solution.py:623
  20.5 0.9 %collective-permute-start.6 = (bf16[400,128]{1,0:T(8,128)(2,1)S(1)}, bf16[400,128]{1,0:T(8,128)(2,1)S(1)}, u32[]{:S(2)}, u32[]{:S(2)}) collective-permute-start(bf16[400,128]{1,0:T(8,128)(2,1)S(1)} %get-tuple-element.26), channel_id=1, source_target_pairs={{0,2},{1,3},{2,0},{3,1},{4,6},{5,7},{6,4},{7,5},{8,10},{9,11},{10,... | collective-permute-start | bytes 307208 | tf_op jit(solution)/shard_map/edge_chip/ppermute | solution.py:621
  21.3 0.2 collective-permute-done.4.mate_ref
  21.6 0.0 copy-done.2
  21.6 3.2 %first_part.1.one_ref = bf16[8,112,128]{2,1,0:T(8,128)(2,1)S(1)} custom-call(s32[1]{0:T(128)} %bitcast.t_ref, f32[32]{0:T(128)S(1)} %copy-done.5, bf16[8,256,128]{2,1,0:T(8,128)(2,1)S(1)} %copy-done, bf16[896,128]{1,0:T(8,128)(2,1)S(1)} %collective-permute-done.a_ref, bf16[912,128]{1,0:T(8,128)(2,1)S(1)} %collective-permute-done.1.b_ref, ...), custom_call_target="tpu_custom_call" | custom-call | flops 10000000 | bytes 100000 | tf_op jit(solution)/shard_map/first_part/pallas_call | solution.py:451
  24.8 0.0 collective-permute-done.5.i_ref
  24.8 1.6 %collective-permute-done.6.e_ref = bf16[400,128]{1,0:T(8,128)(2,1)S(1)} collective-permute-done((bf16[400,128]{1,0:T(8,128)(2,1)S(1)}, bf16[400,128]{1,0:T(8,128)(2,1)S(1)}, u32[]{:S(2)}, u32[]{:S(2)}) %collective-permute-start.6) | collective-permute-done | bytes 102432 | tf_op jit(solution)/shard_map/edge_chip/ppermute | solution.py:621
  26.4 1.0 %collective-permute-start.7 = (bf16[1264,128]{1,0:T(8,128)(2,1)S(1)}, bf16[1264,128]{1,0:T(8,128)(2,1)S(1)}, u32[]{:S(2)}, u32[]{:S(2)}) collective-permute-start(bf16[1264,128]{1,0:T(8,128)(2,1)S(1)} %join.1.z_ref), channel_id=1, source_target_pairs={{0,1},{1,0},{2,3},{3,2},{4,5},{5,4},{6,7},{7,6},{8,9},{9,8},{10,11... | collective-permute-start | bytes 970760 | tf_op jit(solution)/shard_map/chip_core/ppermute | solution.py:627
  27.4 1.6 %state_second.1.state_ref = f32[6,176,256]{2,1,0:T(8,128)S(1)} custom-call(s32[1]{0:T(128)} %bitcast.t_ref, s32[1]{0:T(128)} %bitcast.1.l_ref, f32[32]{0:T(128)S(1)} %copy-done.5, bf16[8,256,128]{2,1,0:T(8,128)(2,1)S(1)} %copy-done, bf16[16,128]{1,0:T(8,128)(2,1)S(1)} %collective-permute-done.2.near_ref, bf16[16,128]{1,0:T(8,128)(2,1)S(1)} %collective-permute-done.3.far_ref, ...), custom_call_target="tpu_custom_call" | custom-call | flops 1000000000 | bytes 2097152 | tf_op jit(solution)/shard_map/state_second/pallas_call | solution.py:351
  29.0 0.0 collective-permute-done.7.k_ref
  29.0 4.8 %second_part.1 = bf16[8,256,128]{2,1,0:T(8,128)(2,1)} custom-call(s32[1]{0:T(128)} %bitcast.t_ref, s32[1]{0:T(128)} %bitcast.1.l_ref, f32[32]{0:T(128)S(1)} %copy-done.5, bf16[8,256,128]{2,1,0:T(8,128)(2,1)S(1)} %copy-done, bf16[896,128]{1,0:T(8,128)(2,1)S(1)} %collective-permute-done.a_ref, bf16[912,128]{1,0:T(8,128)(2,1)S(1)} %collective-permute-done.1.b_ref, ...), custom_call_target="tpu_custom_call" | custom-call | flops 5000000000 | bytes 4000000 | tf_op jit(solution)/shard_map/second_part/pallas_call | solution.py:566
  (1 shorter events, 0.0 us)
Async XLA Ops:
  0.0 12.9 %copy-start.4 = (bf16[32,64,128]{2,1,0:T(8,128)(2,1)S(1)}, bf16[32,64,128]{2,1,0:T(8,128)(2,1)}, u32[]{:S(2)}) copy-start(bf16[32,64,128]{2,1,0:T(8,128)(2,1)} %s_ref.5) | copy-start | bytes 1572868
  0.0 12.9 %copy-start.3 = (bf16[32,64,128]{2,1,0:T(8,128)(2,1)S(1)}, bf16[32,64,128]{2,1,0:T(8,128)(2,1)}, u32[]{:S(2)}) copy-start(bf16[32,64,128]{2,1,0:T(8,128)(2,1)} %f_ref.5) | copy-start | bytes 1572868
  0.0 12.9 %copy-start.6 = (bf16[289,128]{1,0:T(8,128)(2,1)S(1)}, bf16[289,128]{1,0:T(8,128)(2,1)}, u32[]{:S(2)}) copy-start(bf16[289,128]{1,0:T(8,128)(2,1)} %enc_ref.1) | copy-start | bytes 221956
  1.5 16.6 %collective-permute-start.1 = (bf16[912,128]{1,0:T(8,128)(2,1)S(1)}, bf16[912,128]{1,0:T(8,128)(2,1)S(1)}, u32[]{:S(2)}, u32[]{:S(2)}) collective-permute-start(bf16[912,128]{1,0:T(8,128)(2,1)S(1)} %get-tuple-element.17), channel_id=1, source_target_pairs={{1,2},{3,4},{5,6},{7,8},{9,10},{11,12},{13,14},{15,16},{17,18},{19... | collective-permute-start | bytes 700424 | tf_op jit(solution)/shard_map/rim_far/ppermute | solution.py:607
  6.6 11.5 %collective-permute-start = (bf16[896,128]{1,0:T(8,128)(2,1)S(1)}, bf16[896,128]{1,0:T(8,128)(2,1)S(1)}, u32[]{:S(2)}, u32[]{:S(2)}) collective-permute-start(bf16[896,128]{1,0:T(8,128)(2,1)S(1)} %get-tuple-element.16), channel_id=1, source_target_pairs={{0,1},{2,3},{4,5},{6,7},{8,9},{10,11},{12,13},{14,15},{16,17},{18,... | collective-permute-start | bytes 688136 | tf_op jit(solution)/shard_map/rim_near/ppermute | solution.py:609
  11.2 4.7 %collective-permute-start.2 = (bf16[16,128]{1,0:T(8,128)(2,1)S(1)}, bf16[16,128]{1,0:T(8,128)(2,1)S(1)}, u32[]{:S(2)}, u32[]{:S(2)}) collective-permute-start(bf16[16,128]{1,0:T(8,128)(2,1)S(1)} %get-tuple-element.18), channel_id=1, source_target_pairs={{0,4},{8,12},{16,20},{24,28},{32,36},{40,44},{48,52},{56,60},{64,6... | collective-permute-start | bytes 12296 | tf_op jit(solution)/shard_map/state_near/ppermute | solution.py:611
  11.2 3.4 %copy-start = (bf16[8,256,128]{2,1,0:T(8,128)(2,1)S(1)}, bf16[8,256,128]{2,1,0:T(8,128)(2,1)}, u32[]{:S(2)}) copy-start(bf16[8,256,128]{2,1,0:T(8,128)(2,1)} %h_ref.9) | copy-start | bytes 1572868
  11.2 3.4 %copy-start.1 = (bf16[3,3,256,256]{3,2,1,0:T(8,128)(2,1)S(1)}, bf16[3,3,256,256]{3,2,1,0:T(8,128)(2,1)}, u32[]{:S(2)}) copy-start(bf16[3,3,256,256]{3,2,1,0:T(8,128)(2,1)} %gw_ref.7) | copy-start | bytes 3538948
  11.2 3.4 %copy-start.5 = (f32[32]{0:T(128)S(1)}, f32[32]{0:T(128)}, u32[]{:S(2)}) copy-start(f32[32]{0:T(128)} %metric_ref.7) | copy-start | bytes 388
  11.2 6.9 %collective-permute-start.3 = (bf16[16,128]{1,0:T(8,128)(2,1)S(1)}, bf16[16,128]{1,0:T(8,128)(2,1)S(1)}, u32[]{:S(2)}, u32[]{:S(2)}) collective-permute-start(bf16[16,128]{1,0:T(8,128)(2,1)S(1)} %get-tuple-element.19), channel_id=1, source_target_pairs={{4,8},{12,16},{20,24},{28,32},{36,40},{44,48},{52,56},{60,64},{68,... | collective-permute-start | bytes 12296 | tf_op jit(solution)/shard_map/state_far/ppermute | solution.py:613
  14.5 10.3 %collective-permute-start.5 = (bf16[864,128]{1,0:T(8,128)(2,1)S(1)}, bf16[864,128]{1,0:T(8,128)(2,1)S(1)}, u32[]{:S(2)}, u32[]{:S(2)}) collective-permute-start(bf16[864,128]{1,0:T(8,128)(2,1)S(1)} %get-tuple-element.25), channel_id=1, source_target_pairs={{0,2},{1,3},{2,0},{3,1},{4,6},{5,7},{6,4},{7,5},{8,10},{9,11},{10,... | collective-permute-start | bytes 663560 | tf_op jit(solution)/shard_map/inner_chip/ppermute | solution.py:616
  18.1 3.5 %copy-start.2 = (bf16[3,3,256,128]{3,2,1,0:T(8,128)(2,1)S(1)}, bf16[3,3,256,128]{3,2,1,0:T(8,128)(2,1)}, u32[]{:S(2)}) copy-start(bf16[3,3,256,128]{3,2,1,0:T(8,128)(2,1)} %cw_ref.3) | copy-start | bytes 1769476
  19.3 2.2 %collective-permute-start.4 = (bf16[848,128]{1,0:T(8,128)(2,1)S(1)}, bf16[848,128]{1,0:T(8,128)(2,1)S(1)}, u32[]{:S(2)}, u32[]{:S(2)}) collective-permute-start(bf16[848,128]{1,0:T(8,128)(2,1)S(1)} %get-tuple-element.24), channel_id=1, source_target_pairs={{0,1},{1,0},{2,3},{3,2},{4,5},{5,4},{6,7},{7,6},{8,9},{9,8},{10,11... | collective-permute-start | bytes 651272 | tf_op jit(solution)/shard_map/own_core/ppermute | solution.py:623
  20.5 5.9 %collective-permute-start.6 = (bf16[400,128]{1,0:T(8,128)(2,1)S(1)}, bf16[400,128]{1,0:T(8,128)(2,1)S(1)}, u32[]{:S(2)}, u32[]{:S(2)}) collective-permute-start(bf16[400,128]{1,0:T(8,128)(2,1)S(1)} %get-tuple-element.26), channel_id=1, source_target_pairs={{0,2},{1,3},{2,0},{3,1},{4,6},{5,7},{6,4},{7,5},{8,10},{9,11},{10,... | collective-permute-start | bytes 307208 | tf_op jit(solution)/shard_map/edge_chip/ppermute | solution.py:621
  26.4 2.5 %collective-permute-start.7 = (bf16[1264,128]{1,0:T(8,128)(2,1)S(1)}, bf16[1264,128]{1,0:T(8,128)(2,1)S(1)}, u32[]{:S(2)}, u32[]{:S(2)}) collective-permute-start(bf16[1264,128]{1,0:T(8,128)(2,1)S(1)} %join.1.z_ref), channel_id=1, source_target_pairs={{0,1},{1,0},{2,3},{3,2},{4,5},{5,4},{6,7},{7,6},{8,9},{9,8},{10,11... | collective-permute-start | bytes 970760 | tf_op jit(solution)/shard_map/chip_core/ppermute | solution.py:627

commit v6 on v5

--- a/solution.py
+++ b/solution.py
@@ -303,7 +303,7 @@
         hs[256 * i : 256 * i + 256] = h_ref[i].astype(F32)
     for q in range(3):
         for i in range(8):
-            x[q, i] = hs[pl.ds(256 * i + 112 * (t // 2) + 14 + q, 128)].astype(BF)
+            x[q, i] = hs[pl.ds(256 * i + 126 * (t // 2) + q, 128)].astype(BF)
     state_products(metric_ref, t, x, gw_ref, 128, out_ref)
 
 
@@ -321,8 +321,8 @@
         outer(hf, hs, i, c0, high, hl[2 * i : 2 * i + 2], hr[2 * i : 2 * i + 2])
     for q in range(3):
         for i in range(8):
-            x[q, i] = hf[i, q : q + 176].astype(BF)
-    state_products(metric_ref, t, x, gw_ref, 176, out_ref)
+            x[q, i] = hf[i, q : q + 144].astype(BF)
+    state_products(metric_ref, t, x, gw_ref, 144, out_ref)
 
 
 def outer(hf, hs, i, c0, high, side_w, side_e):
@@ -330,8 +330,8 @@
     hf[i, 2:130] = hs[pl.ds(256 * i + c0, 128)]
     hf[i, 0:2] = jnp.where(low, hs[256 * i + 126 : 256 * i + 128], side_w)
     hf[i, 130:132] = jnp.where(low, side_e, hs[256 * i + 128 : 256 * i + 130])
-    hf[i, pl.ds(146 - 2 * high, 18)] = hs[pl.ds(256 * i + 238 * high, 18)]
-    hf[i, pl.ds(144 + 18 * high, 2)] = jnp.where(low, side_w, side_e)
+    hf[i, pl.ds(134 - 2 * high, 4)] = hs[pl.ds(256 * i + 252 * high, 4)]
+    hf[i, pl.ds(132 + 4 * high, 2)] = jnp.where(low, side_w, side_e)
 
 
 def state_first(t, metric, h, gw):
@@ -350,10 +350,10 @@
 def state_second(t, l, metric, h, near, far, gw):
     return pl.pallas_call(
         state_second_kernel,
-        out_shape=jax.ShapeDtypeStruct((6, 176, 256), F32),
+        out_shape=jax.ShapeDtypeStruct((6, 144, 256), F32),
         in_specs=[SM, SM, SM] + [VM] * 4,
         out_specs=VM,
-        scratch_shapes=[pltpu.VMEM((2048, 128), F32), pltpu.VMEM((8, 184, 128), F32), pltpu.VMEM((3, 8, 176, 128), BF)],
+        scratch_shapes=[pltpu.VMEM((2048, 128), F32), pltpu.VMEM((8, 152, 128), F32), pltpu.VMEM((3, 8, 144, 128), BF)],
         compiler_params=pltpu.CompilerParams(vmem_limit_bytes=24 << 20),
         cost_estimate=pl.CostEstimate(flops=10**9, bytes_accessed=2 << 20, transcendentals=0),
         name="state_second",
@@ -398,7 +398,6 @@
 def first_kernel(t_ref, metric_ref, h_ref, a_ref, b_ref, own_ref, mate_ref, state_ref, gw_ref, cw_ref, out_ref, hs, mf, x, m3s, rf, r, ug, top, bot, rims):
     t = t_ref[0]
     high = t // 2
-    base = 112 * high
     state_rows(t, a_ref, b_ref, h_ref, hs, top, bot)
     start = 8 * t - 2 - 14 * high
     odd = lax.rem(t, 2)
@@ -424,43 +423,43 @@
     for q in range(3):
         for i in range(12):
             if not 4 <= i < 8:
-                x[q, i, :, 0:128] = hs[pl.ds(256 * i + base + 14 + q, 128)].astype(BF)
-            x[q, i, :, 128:256] = mf[i, 14 + q : 142 + q].astype(BF)
+                x[q, i, :, 0:128] = hs[pl.ds(256 * i + 126 * high + q, 128)].astype(BF)
+            x[q, i, :, 128:256] = mf[i, pl.ds(14 * high + q, 128)].astype(BF)
     for i in range(12):
-        m3s[i] = mf[i, 17:129].astype(BF)
+        m3s[i] = mf[i, pl.ds(14 * high + 3, 128)].astype(BF)
 
     def put_gate(i, gate):
-        rf[i, 0:128] = gate[:, 128:] * hs[pl.ds(256 * (i + 1) + base + 15, 128)]
+        rf[i, 0:128] = gate[:, 128:] * hs[pl.ds(256 * (i + 1) + 126 * high + 1, 128)]
         if 1 <= i < 9:
-            ug[i - 1] = gate[:, 0:128]
+            ug[i - 1, 0:128] = gate[:, 0:128]
 
     gates(metric_ref, t, x, gw_ref, state_ref, 128, put_gate)
     for q in range(3):
         for i in range(10):
-            r[q, i] = rf[i, q : q + 112].astype(BF)
+            r[q, i] = rf[i, q : q + 128].astype(BF)
 
     def put_new(i, cand):
-        u = ug[i, 1:113]
-        h = hs[pl.ds(256 * (i + 2) + base + 16, 112)]
+        u = ug[i, 1:129]
+        h = hs[pl.ds(256 * (i + 2) + 126 * high + 2, 128)]
         out_ref[i] = ((1.0 - u) * h + u * cand).astype(BF)
 
-    candidates(metric_ref, t, x, m3s, r, cw_ref, 112, put_new)
+    candidates(metric_ref, t, x, m3s, r, cw_ref, 128, put_new)
 
 
 def first_part(t, metric, h, a, b, own, mate, state, gw, cw):
     return pl.pallas_call(
         first_kernel,
-        out_shape=jax.ShapeDtypeStruct((8, 112, 128), BF),
+        out_shape=jax.ShapeDtypeStruct((8, 128, 128), BF),
         in_specs=[SM, SM] + [VM] * 8,
         out_specs=VM,
         scratch_shapes=[
             pltpu.VMEM((3072, 128), F32),
             pltpu.VMEM((12, 152, 128), F32),
             pltpu.VMEM((3, 12, 128, 256), BF),
-            pltpu.VMEM((12, 112, 128), BF),
+            pltpu.VMEM((12, 128, 128), BF),
             pltpu.VMEM((10, 136, 128), F32),
-            pltpu.VMEM((3, 10, 112, 128), BF),
-            pltpu.VMEM((8, 128, 128), F32),
+            pltpu.VMEM((3, 10, 128, 128), BF),
+            pltpu.VMEM((8, 136, 128), F32),
             pltpu.VMEM((512, 128), F32),
             pltpu.VMEM((512, 128), F32),
             pltpu.VMEM((80, 128), F32),
@@ -473,7 +472,7 @@
 
 def second_kernel(
     t_ref, l_ref, metric_ref, h_ref, a_ref, b_ref, near_ref, far_ref, own_ref, mate_ref, z_ref, k_ref, state_ref, gw_ref, cw_ref, one_ref, out_ref,
-    ob, sem, hs, hf, mf, x, m3s, rf, r, ug, top, bot, rims,
+    ob, ow, sem, hs, hf, mf, x, m3s, rf, r, ug, top, bot, rims,
 ):
     t = t_ref[0]
     high = t // 2
@@ -517,47 +516,43 @@
         row = start + i
         inside = (row >= 0) & (row < 18)
         row = jnp.clip(row, 0, 17)
-        at = pl.multiple_of(48 * row + 32 * high, 16)
-        mid = jnp.where(inside, own_ref[pl.ds(at, 16)].astype(F32), 0.0)
         at = pl.multiple_of(864 + 16 * row, 16)
         ends = jnp.where(inside, own_ref[pl.ds(at, 16)].astype(F32), 0.0)
-        at = pl.multiple_of(48 * i + 32 * high, 16)
-        mid = jnp.where(mine, mid, mate_ref[pl.ds(at, 16)].astype(F32))
         ends = jnp.where(mine, ends, mate_ref[576 + 16 * i : 592 + 16 * i].astype(F32))
-        mf[i, pl.ds(154 - 10 * high, 10)] = jnp.where(low, mid[0:10], mid[6:16])
-        mf[i, pl.ds(146 + 8 * high, 8)] = jnp.where(low, ends[0:8], ends[8:16])
+        mf[i, pl.ds(134 - 2 * high, 4)] = jnp.where(low, ends[0:4], ends[12:16])
         row = jnp.where(mine, row, i)
         inside = inside | jnp.logical_not(mine)
         v = rims[pl.ds(4 * row + 2 * high, 2)]
-        mf[i, pl.ds(144 + 18 * high, 2)] = jnp.where(inside, v, 0.0)
+        mf[i, pl.ds(132 + 4 * high, 2)] = jnp.where(inside, v, 0.0)
     for q in range(3):
         for i in range(12):
             if not 4 <= i < 8:
-                x[q, i, :, 0:128] = hf[i, q : q + 176].astype(BF)
-            x[q, i, :, 128:256] = mf[i, q : q + 176].astype(BF)
+                x[q, i, :, 0:128] = hf[i, q : q + 144].astype(BF)
+            x[q, i, :, 128:256] = mf[i, q : q + 144].astype(BF)
     for i in range(12):
-        m3s[i] = mf[i, 3:163].astype(BF)
+        m3s[i] = mf[i, 3:147].astype(BF)
 
     def put_gate(i, gate):
-        rf[i, 0:176] = gate[:, 128:] * hf[i + 1, 1:177]
+        rf[i, 0:144] = gate[:, 128:] * hf[i + 1, 1:145]
         if 1 <= i < 9:
-            ug[i - 1] = gate[:, 0:128]
-
-    gates(metric_ref, t, x, gw_ref, state_ref, 176, put_gate)
+            ug[i - 1, 0:144] = gate[:, 0:128]
+
+    gates(metric_ref, t, x, gw_ref, state_ref, 144, put_gate)
     for q in range(3):
         for i in range(10):
-            r[q, i] = rf[i, q : q + 160].astype(BF)
+            r[q, i] = rf[i, q : q + 144].astype(BF)
 
     def put_new(i, cand):
-        u = ug[i, 1:161]
-        h = hf[i + 2, 2:162]
-        new = ((1.0 - u) * h + u * cand).astype(BF)
-        ob[i, pl.ds(c0, 128)] = new[0:128]
-        ob[i, pl.ds(pl.multiple_of(240 * high, 16), 16)] = new[144:160]
-        ob[i, pl.ds(pl.multiple_of(16 + 112 * high, 16), 112)] = one_ref[i]
+        u = ug[i, 1:145]
+        h = hf[i + 2, 2:146]
+        new = (1.0 - u) * h + u * cand
+        ob[i, pl.ds(c0, 128)] = new[0:128].astype(BF)
+        ow[i, pl.ds(2 - 2 * high, 126)] = one_ref[i].astype(F32)[0:126]
+        ow[i, pl.ds(126 * high, 2)] = new[132:134]
+        ob[i, pl.ds(pl.multiple_of(128 - c0, 128), 128)] = ow[i].astype(BF)
         pltpu.make_async_copy(ob.at[i], out_ref.at[i], sem.at[i]).start()
 
-    candidates(metric_ref, t, x, m3s, r, cw_ref, 160, put_new)
+    candidates(metric_ref, t, x, m3s, r, cw_ref, 144, put_new)
     for i in range(8):
         pltpu.make_async_copy(ob.at[i], out_ref.at[i], sem.at[i]).wait()
 
@@ -570,15 +565,16 @@
         out_specs=pl.BlockSpec(memory_space=pl.ANY),
         scratch_shapes=[
             pltpu.VMEM((8, 256, 128), BF),
+            pltpu.VMEM((8, 128, 128), F32),
             pltpu.SemaphoreType.DMA((8,)),
             pltpu.VMEM((3072, 128), F32),
-            pltpu.VMEM((12, 184, 128), F32),
-            pltpu.VMEM((12, 184, 128), F32),
-            pltpu.VMEM((3, 12, 176, 256), BF),
-            pltpu.VMEM((12, 160, 128), BF),
-            pltpu.VMEM((10, 184, 128), F32),
-            pltpu.VMEM((3, 10, 160, 128), BF),
-            pltpu.VMEM((8, 176, 128), F32),
+            pltpu.VMEM((12, 152, 128), F32),
+            pltpu.VMEM((12, 152, 128), F32),
+            pltpu.VMEM((3, 12, 144, 256), BF),
+            pltpu.VMEM((12, 144, 128), BF),
+            pltpu.VMEM((10, 152, 128), F32),
+            pltpu.VMEM((3, 10, 144, 128), BF),
+            pltpu.VMEM((8, 152, 128), F32),
             pltpu.VMEM((512, 128), F32),
             pltpu.VMEM((512, 128), F32),
             pltpu.VMEM((80, 128), F32),

time: 33.9 us -> 33.2 us (0.979)
  Pallas kernels: 15.1 us -> 14.5 us
    pallas_call x1, Pallas kernels: 4.78 us -> 4.26 us  [second_part(): pl.pallas_call(second_kernel, out_shape=jax.ShapeDtypeStruct((8, 256, 128...]
where the time goes in v6:
time: 33.2 us; the launch traced here: 33.1 us
  Pallas kernels  14.5 us (44%)
  starting transfers between devices  14.5 us (44%)
  waiting for transfers between devices  3.95 us (12%)
    ppermute x1, starting transfers between devices, body(): b = lax.ppermute(b_send, BOTH, swaps(slabs, 1))  5.06 us
    ppermute x1, starting transfers between devices, body(): a = lax.ppermute(a_send, BOTH, swaps(slabs, 0))  4.64 us
    pallas_call x1, Pallas kernels, second_part(): pl.pallas_call(second_kernel, out_shape=jax.ShapeDtypeStruct((8, 256, 128...  4.26 us
    pallas_call x1, Pallas kernels, first_part(): pl.pallas_call(first_kernel, out_shape=jax.ShapeDtypeStruct((8, 128, 128)...  3.28 us
    ppermute x1, waiting for transfers between devices, body(): far = lax.ppermute(far_send, 'lon', swaps(count, 1))  2.16 us
    ppermute x1, starting transfers between devices, body(): far = lax.ppermute(far_send, 'lon', swaps(count, 1))  1.72 us
    ppermute x1, waiting for transfers between devices, body(): ze = lax.ppermute(ze_send, 'lat', chip)  1.54 us
    pallas_call x1, Pallas kernels, inner(): pl.pallas_call(inner_kernel, out_shape=(jax.ShapeDtypeStruct((864, 128),...  1.51 us
  transfers between devices with their start and end apart: 8, of which 3 were waited for; matrix products, arithmetic and copies ran while one was open for 0% of the time, Pallas kernels for 26%

profile of v6, /device:TPU:1, one launch (start us, length us, event | category | flops | bytes accessed | tf_op | source)
XLA Modules:
  0.0 33.1 jit_solution(1877176998687148202)
XLA Ops:
  0.0 0.0 copy-start.4
  0.0 0.0 copy-start.3
  0.0 0.0 copy-start.6
  0.0 1.5 %pack.1 = (bf16[896,128]{1,0:T(8,128)(2,1)S(1)}, bf16[912,128]{1,0:T(8,128)(2,1)S(1)}, bf16[16,128]{1,0:T(8,128)(2,1)S(1)}, bf16[16,128]{1,0:T(8,128)(2,1)S(1)}) custom-call(s32[1]{0:T(128)} %bitcast.t_ref, s32[1]{0:T(128)} %bitcast.1.l_ref, bf16[32,64,128]{2,1,0:T(8,128)(2,1)} %f_ref.5, bf16[32,64,128]{2,1,0:T(8,128)(2,1)} %s_ref.5, bf16[8,256,128]{2,1,0:T(8,128)(2,1)} %h_ref.9), custom_call_target="tpu_custom_call" | custom-call | tf_op jit(solution)/shard_map/pack/pallas_call | solution.py:74
  1.5 5.1 %collective-permute-start.1 = (bf16[912,128]{1,0:T(8,128)(2,1)S(1)}, bf16[912,128]{1,0:T(8,128)(2,1)S(1)}, u32[]{:S(2)}, u32[]{:S(2)}) collective-permute-start(bf16[912,128]{1,0:T(8,128)(2,1)S(1)} %get-tuple-element.17), channel_id=1, source_target_pairs={{1,2},{3,4},{5,6},{7,8},{9,10},{11,12},{13,14},{15,16},{17,18},{19... | collective-permute-start | bytes 700424 | tf_op jit(solution)/shard_map/rim_far/ppermute | solution.py:603
  6.6 4.6 %collective-permute-start = (bf16[896,128]{1,0:T(8,128)(2,1)S(1)}, bf16[896,128]{1,0:T(8,128)(2,1)S(1)}, u32[]{:S(2)}, u32[]{:S(2)}) collective-permute-start(bf16[896,128]{1,0:T(8,128)(2,1)S(1)} %get-tuple-element.16), channel_id=1, source_target_pairs={{0,1},{2,3},{4,5},{6,7},{8,9},{10,11},{12,13},{14,15},{16,17},{18,... | collective-permute-start | bytes 688136 | tf_op jit(solution)/shard_map/rim_near/ppermute | solution.py:605
  11.2 0.0 collective-permute-start.2
  11.2 0.0 copy-start
  11.2 0.0 copy-start.1
  11.2 0.0 copy-start.5
  11.2 1.7 %collective-permute-start.3 = (bf16[16,128]{1,0:T(8,128)(2,1)S(1)}, bf16[16,128]{1,0:T(8,128)(2,1)S(1)}, u32[]{:S(2)}, u32[]{:S(2)}) collective-permute-start(bf16[16,128]{1,0:T(8,128)(2,1)S(1)} %get-tuple-element.19), channel_id=1, source_target_pairs={{4,8},{12,16},{20,24},{28,32},{36,40},{44,48},{52,56},{60,64},{68,... | collective-permute-start | bytes 12296 | tf_op jit(solution)/shard_map/state_far/ppermute | solution.py:609
  12.9 0.0 copy-done.4
  12.9 0.0 copy-done.3
  12.9 0.0 copy-done.6
  13.0 1.5 %inner.1 = (bf16[864,128]{1,0:T(8,128)(2,1)S(1)}, bf16[864,128]{1,0:T(8,128)(2,1)S(1)}, bf16[576,128]{1,0:T(8,128)(2,1)S(1)}, bf16[992,128]{1,0:T(8,128)(2,1)S(1)}) custom-call(s32[1]{0:T(128)} %bitcast.t_ref, bf16[32,64,128]{2,1,0:T(8,128)(2,1)S(1)} %copy-done.3, bf16[32,64,128]{2,1,0:T(8,128)(2,1)S(1)} %copy-done.4, bf16[289,128]{1,0:T(8,128)(2,1)S(1)} %copy-done.6), custom_call_target="tpu_custom_call" | custom-call | flops 1000000000 | bytes 1000000 | tf_op jit(solution)/shard_map/inner/pallas_call | solution.py:153
  14.5 0.1 collective-permute-start.5
  14.6 0.0 copy-done
  14.6 0.0 copy-done.1
  14.6 0.0 copy-done.5
  14.6 1.3 %state_first.1.state_ref = f32[6,128,256]{2,1,0:T(8,128)S(1)} custom-call(s32[1]{0:T(128)} %bitcast.t_ref, f32[32]{0:T(128)S(1)} %copy-done.5, bf16[8,256,128]{2,1,0:T(8,128)(2,1)S(1)} %copy-done, bf16[3,3,256,256]{3,2,1,0:T(8,128)(2,1)S(1)} %copy-done.1), custom_call_target="tpu_custom_call" | custom-call | flops 1000000000 | bytes 2097152 | tf_op jit(solution)/shard_map/state_first/pallas_call | solution.py:338
  15.9 0.0 collective-permute-done.2.near_ref
  15.9 2.2 %collective-permute-done.3.far_ref = bf16[16,128]{1,0:T(8,128)(2,1)S(1)} collective-permute-done((bf16[16,128]{1,0:T(8,128)(2,1)S(1)}, bf16[16,128]{1,0:T(8,128)(2,1)S(1)}, u32[]{:S(2)}, u32[]{:S(2)}) %collective-permute-start.3) | collective-permute-done | bytes 4128 | tf_op jit(solution)/shard_map/state_far/ppermute | solution.py:609
  18.1 0.0 collective-permute-done.a_ref
  18.1 0.0 collective-permute-done.1.b_ref
  18.1 0.0 copy-start.2
  18.1 1.2 %edge.1 = (bf16[400,128]{1,0:T(8,128)(2,1)S(1)}, bf16[1232,128]{1,0:T(8,128)(2,1)S(1)}, bf16[848,128]{1,0:T(8,128)(2,1)S(1)}) custom-call(s32[1]{0:T(128)} %bitcast.t_ref, bf16[32,64,128]{2,1,0:T(8,128)(2,1)S(1)} %copy-done.3, bf16[32,64,128]{2,1,0:T(8,128)(2,1)S(1)} %copy-done.4, bf16[896,128]{1,0:T(8,128)(2,1)S(1)} %collective-permute-done.a_ref, ...), custom_call_target="tpu_custom_call" | custom-call | flops 1000000000 | bytes 1000000 | tf_op jit(solution)/shard_map/edge/pallas_call | solution.py:228
  19.3 1.1 %collective-permute-start.4 = (bf16[848,128]{1,0:T(8,128)(2,1)S(1)}, bf16[848,128]{1,0:T(8,128)(2,1)S(1)}, u32[]{:S(2)}, u32[]{:S(2)}) collective-permute-start(bf16[848,128]{1,0:T(8,128)(2,1)S(1)} %get-tuple-element.24), channel_id=1, source_target_pairs={{0,1},{1,0},{2,3},{3,2},{4,5},{5,4},{6,7},{7,6},{8,9},{9,8},{10,11... | collective-permute-start | bytes 651272 | tf_op jit(solution)/shard_map/own_core/ppermute | solution.py:619
  20.4 0.9 %collective-permute-start.6 = (bf16[400,128]{1,0:T(8,128)(2,1)S(1)}, bf16[400,128]{1,0:T(8,128)(2,1)S(1)}, u32[]{:S(2)}, u32[]{:S(2)}) collective-permute-start(bf16[400,128]{1,0:T(8,128)(2,1)S(1)} %get-tuple-element.26), channel_id=1, source_target_pairs={{0,2},{1,3},{2,0},{3,1},{4,6},{5,7},{6,4},{7,5},{8,10},{9,11},{10,... | collective-permute-start | bytes 307208 | tf_op jit(solution)/shard_map/edge_chip/ppermute | solution.py:617
  21.3 0.2 collective-permute-done.4.mate_ref
  21.5 0.0 copy-done.2
  21.5 3.3 %first_part.1.one_ref = bf16[8,128,128]{2,1,0:T(8,128)(2,1)S(1)} custom-call(s32[1]{0:T(128)} %bitcast.t_ref, f32[32]{0:T(128)S(1)} %copy-done.5, bf16[8,256,128]{2,1,0:T(8,128)(2,1)S(1)} %copy-done, bf16[896,128]{1,0:T(8,128)(2,1)S(1)} %collective-permute-done.a_ref, bf16[912,128]{1,0:T(8,128)(2,1)S(1)} %collective-permute-done.1.b_ref, ...), custom_call_target="tpu_custom_call" | custom-call | flops 10000000 | bytes 100000 | tf_op jit(solution)/shard_map/first_part/pallas_call | solution.py:450
  24.8 0.0 collective-permute-done.5.i_ref
  24.8 1.5 %collective-permute-done.6.e_ref = bf16[400,128]{1,0:T(8,128)(2,1)S(1)} collective-permute-done((bf16[400,128]{1,0:T(8,128)(2,1)S(1)}, bf16[400,128]{1,0:T(8,128)(2,1)S(1)}, u32[]{:S(2)}, u32[]{:S(2)}) %collective-permute-start.6) | collective-permute-done | bytes 102432 | tf_op jit(solution)/shard_map/edge_chip/ppermute | solution.py:617
  26.4 1.0 %collective-permute-start.7 = (bf16[1264,128]{1,0:T(8,128)(2,1)S(1)}, bf16[1264,128]{1,0:T(8,128)(2,1)S(1)}, u32[]{:S(2)}, u32[]{:S(2)}) collective-permute-start(bf16[1264,128]{1,0:T(8,128)(2,1)S(1)} %join.1.z_ref), channel_id=1, source_target_pairs={{0,1},{1,0},{2,3},{3,2},{4,5},{5,4},{6,7},{7,6},{8,9},{9,8},{10,11... | collective-permute-start | bytes 970760 | tf_op jit(solution)/shard_map/chip_core/ppermute | solution.py:623
  27.4 1.4 %state_second.1.state_ref = f32[6,144,256]{2,1,0:T(8,128)S(1)} custom-call(s32[1]{0:T(128)} %bitcast.t_ref, s32[1]{0:T(128)} %bitcast.1.l_ref, f32[32]{0:T(128)S(1)} %copy-done.5, bf16[8,256,128]{2,1,0:T(8,128)(2,1)S(1)} %copy-done, bf16[16,128]{1,0:T(8,128)(2,1)S(1)} %collective-permute-done.2.near_ref, bf16[16,128]{1,0:T(8,128)(2,1)S(1)} %collective-permute-done.3.far_ref, ...), custom_call_target="tpu_custom_call" | custom-call | flops 1000000000 | bytes 2097152 | tf_op jit(solution)/shard_map/state_second/pallas_call | solution.py:351
  28.8 0.0 collective-permute-done.7.k_ref
  28.8 4.3 %second_part.1 = bf16[8,256,128]{2,1,0:T(8,128)(2,1)} custom-call(s32[1]{0:T(128)} %bitcast.t_ref, s32[1]{0:T(128)} %bitcast.1.l_ref, f32[32]{0:T(128)S(1)} %copy-done.5, bf16[8,256,128]{2,1,0:T(8,128)(2,1)S(1)} %copy-done, bf16[896,128]{1,0:T(8,128)(2,1)S(1)} %collective-permute-done.a_ref, bf16[912,128]{1,0:T(8,128)(2,1)S(1)} %collective-permute-done.1.b_ref, ...), custom_call_target="tpu_custom_call" | custom-call | flops 5000000000 | bytes 4000000 | tf_op jit(solution)/shard_map/second_part/pallas_call | solution.py:561
  (1 shorter events, 0.0 us)
Async XLA Ops:
  0.0 12.9 %copy-start.4 = (bf16[32,64,128]{2,1,0:T(8,128)(2,1)S(1)}, bf16[32,64,128]{2,1,0:T(8,128)(2,1)}, u32[]{:S(2)}) copy-start(bf16[32,64,128]{2,1,0:T(8,128)(2,1)} %s_ref.5) | copy-start | bytes 1572868
  0.0 12.9 %copy-start.3 = (bf16[32,64,128]{2,1,0:T(8,128)(2,1)S(1)}, bf16[32,64,128]{2,1,0:T(8,128)(2,1)}, u32[]{:S(2)}) copy-start(bf16[32,64,128]{2,1,0:T(8,128)(2,1)} %f_ref.5) | copy-start | bytes 1572868
  0.0 12.9 %copy-start.6 = (bf16[289,128]{1,0:T(8,128)(2,1)S(1)}, bf16[289,128]{1,0:T(8,128)(2,1)}, u32[]{:S(2)}) copy-start(bf16[289,128]{1,0:T(8,128)(2,1)} %enc_ref.1) | copy-start | bytes 221956
  1.5 16.6 %collective-permute-start.1 = (bf16[912,128]{1,0:T(8,128)(2,1)S(1)}, bf16[912,128]{1,0:T(8,128)(2,1)S(1)}, u32[]{:S(2)}, u32[]{:S(2)}) collective-permute-start(bf16[912,128]{1,0:T(8,128)(2,1)S(1)} %get-tuple-element.17), channel_id=1, source_target_pairs={{1,2},{3,4},{5,6},{7,8},{9,10},{11,12},{13,14},{15,16},{17,18},{19... | collective-permute-start | bytes 700424 | tf_op jit(solution)/shard_map/rim_far/ppermute | solution.py:603
  6.6 11.5 %collective-permute-start = (bf16[896,128]{1,0:T(8,128)(2,1)S(1)}, bf16[896,128]{1,0:T(8,128)(2,1)S(1)}, u32[]{:S(2)}, u32[]{:S(2)}) collective-permute-start(bf16[896,128]{1,0:T(8,128)(2,1)S(1)} %get-tuple-element.16), channel_id=1, source_target_pairs={{0,1},{2,3},{4,5},{6,7},{8,9},{10,11},{12,13},{14,15},{16,17},{18,... | collective-permute-start | bytes 688136 | tf_op jit(solution)/shard_map/rim_near/ppermute | solution.py:605
  11.2 4.7 %collective-permute-start.2 = (bf16[16,128]{1,0:T(8,128)(2,1)S(1)}, bf16[16,128]{1,0:T(8,128)(2,1)S(1)}, u32[]{:S(2)}, u32[]{:S(2)}) collective-permute-start(bf16[16,128]{1,0:T(8,128)(2,1)S(1)} %get-tuple-element.18), channel_id=1, source_target_pairs={{0,4},{8,12},{16,20},{24,28},{32,36},{40,44},{48,52},{56,60},{64,6... | collective-permute-start | bytes 12296 | tf_op jit(solution)/shard_map/state_near/ppermute | solution.py:607
  11.2 3.4 %copy-start = (bf16[8,256,128]{2,1,0:T(8,128)(2,1)S(1)}, bf16[8,256,128]{2,1,0:T(8,128)(2,1)}, u32[]{:S(2)}) copy-start(bf16[8,256,128]{2,1,0:T(8,128)(2,1)} %h_ref.9) | copy-start | bytes 1572868
  11.2 3.4 %copy-start.1 = (bf16[3,3,256,256]{3,2,1,0:T(8,128)(2,1)S(1)}, bf16[3,3,256,256]{3,2,1,0:T(8,128)(2,1)}, u32[]{:S(2)}) copy-start(bf16[3,3,256,256]{3,2,1,0:T(8,128)(2,1)} %gw_ref.7) | copy-start | bytes 3538948
  11.2 3.4 %copy-start.5 = (f32[32]{0:T(128)S(1)}, f32[32]{0:T(128)}, u32[]{:S(2)}) copy-start(f32[32]{0:T(128)} %metric_ref.7) | copy-start | bytes 388
  11.2 6.9 %collective-permute-start.3 = (bf16[16,128]{1,0:T(8,128)(2,1)S(1)}, bf16[16,128]{1,0:T(8,128)(2,1)S(1)}, u32[]{:S(2)}, u32[]{:S(2)}) collective-permute-start(bf16[16,128]{1,0:T(8,128)(2,1)S(1)} %get-tuple-element.19), channel_id=1, source_target_pairs={{4,8},{12,16},{20,24},{28,32},{36,40},{44,48},{52,56},{60,64},{68,... | collective-permute-start | bytes 12296 | tf_op jit(solution)/shard_map/state_far/ppermute | solution.py:609
  14.5 10.4 %collective-permute-start.5 = (bf16[864,128]{1,0:T(8,128)(2,1)S(1)}, bf16[864,128]{1,0:T(8,128)(2,1)S(1)}, u32[]{:S(2)}, u32[]{:S(2)}) collective-permute-start(bf16[864,128]{1,0:T(8,128)(2,1)S(1)} %get-tuple-element.25), channel_id=1, source_target_pairs={{0,2},{1,3},{2,0},{3,1},{4,6},{5,7},{6,4},{7,5},{8,10},{9,11},{10,... | collective-permute-start | bytes 663560 | tf_op jit(solution)/shard_map/inner_chip/ppermute | solution.py:612
  18.1 3.4 %copy-start.2 = (bf16[3,3,256,128]{3,2,1,0:T(8,128)(2,1)S(1)}, bf16[3,3,256,128]{3,2,1,0:T(8,128)(2,1)}, u32[]{:S(2)}) copy-start(bf16[3,3,256,128]{3,2,1,0:T(8,128)(2,1)} %cw_ref.3) | copy-start | bytes 1769476
  19.3 2.2 %collective-permute-start.4 = (bf16[848,128]{1,0:T(8,128)(2,1)S(1)}, bf16[848,128]{1,0:T(8,128)(2,1)S(1)}, u32[]{:S(2)}, u32[]{:S(2)}) collective-permute-start(bf16[848,128]{1,0:T(8,128)(2,1)S(1)} %get-tuple-element.24), channel_id=1, source_target_pairs={{0,1},{1,0},{2,3},{3,2},{4,5},{5,4},{6,7},{7,6},{8,9},{9,8},{10,11... | collective-permute-start | bytes 651272 | tf_op jit(solution)/shard_map/own_core/ppermute | solution.py:619
  20.4 5.9 %collective-permute-start.6 = (bf16[400,128]{1,0:T(8,128)(2,1)S(1)}, bf16[400,128]{1,0:T(8,128)(2,1)S(1)}, u32[]{:S(2)}, u32[]{:S(2)}) collective-permute-start(bf16[400,128]{1,0:T(8,128)(2,1)S(1)} %get-tuple-element.26), channel_id=1, source_target_pairs={{0,2},{1,3},{2,0},{3,1},{4,6},{5,7},{6,4},{7,5},{8,10},{9,11},{10,... | collective-permute-start | bytes 307208 | tf_op jit(solution)/shard_map/edge_chip/ppermute | solution.py:617
  26.4 2.4 %collective-permute-start.7 = (bf16[1264,128]{1,0:T(8,128)(2,1)S(1)}, bf16[1264,128]{1,0:T(8,128)(2,1)S(1)}, u32[]{:S(2)}, u32[]{:S(2)}) collective-permute-start(bf16[1264,128]{1,0:T(8,128)(2,1)S(1)} %join.1.z_ref), channel_id=1, source_target_pairs={{0,1},{1,0},{2,3},{3,2},{4,5},{5,4},{6,7},{7,6},{8,9},{9,8},{10,11... | collective-permute-start | bytes 970760 | tf_op jit(solution)/shard_map/chip_core/ppermute | solution.py:623

commit v7 on v6

--- a/solution.py
+++ b/solution.py
@@ -449,11 +449,10 @@
 def first_part(t, metric, h, a, b, own, mate, state, gw, cw):
     return pl.pallas_call(
         first_kernel,
-        out_shape=jax.ShapeDtypeStruct((8, 128, 128), BF),
+        out_shape=(jax.ShapeDtypeStruct((8, 128, 128), BF), pltpu.VMEM((3072, 128), F32)),
         in_specs=[SM, SM] + [VM] * 8,
-        out_specs=VM,
+        out_specs=(VM, VM),
         scratch_shapes=[
-            pltpu.VMEM((3072, 128), F32),
             pltpu.VMEM((12, 152, 128), F32),
             pltpu.VMEM((3, 12, 128, 256), BF),
             pltpu.VMEM((12, 128, 128), BF),
@@ -471,13 +470,12 @@
 
 
 def second_kernel(
-    t_ref, l_ref, metric_ref, h_ref, a_ref, b_ref, near_ref, far_ref, own_ref, mate_ref, z_ref, k_ref, state_ref, gw_ref, cw_ref, one_ref, out_ref,
-    ob, ow, sem, hs, hf, mf, x, m3s, rf, r, ug, top, bot, rims,
+    t_ref, l_ref, metric_ref, hs, near_ref, far_ref, own_ref, mate_ref, z_ref, k_ref, state_ref, gw_ref, cw_ref, one_ref, out_ref,
+    ob, ow, sem, hf, mf, x, m3s, rf, r, ug, rims,
 ):
     t = t_ref[0]
     high = t // 2
     c0 = pl.multiple_of(128 - 128 * high, 128)
-    state_rows(t, a_ref, b_ref, h_ref, hs, top, bot)
     west_even = lax.rem(l_ref[0], 2) == 0
     odd = lax.rem(t, 2)
     low = high == 0
@@ -557,17 +555,16 @@
         pltpu.make_async_copy(ob.at[i], out_ref.at[i], sem.at[i]).wait()
 
 
-def second_part(t, l, metric, h, a, b, near, far, own, mate, z, k, state, gw, cw, one):
+def second_part(t, l, metric, hs, near, far, own, mate, z, k, state, gw, cw, one):
     return pl.pallas_call(
         second_kernel,
         out_shape=jax.ShapeDtypeStruct((8, 256, 128), BF),
-        in_specs=[SM, SM, SM] + [VM] * 13,
+        in_specs=[SM, SM, SM] + [VM] * 11,
         out_specs=pl.BlockSpec(memory_space=pl.ANY),
         scratch_shapes=[
             pltpu.VMEM((8, 256, 128), BF),
             pltpu.VMEM((8, 128, 128), F32),
             pltpu.SemaphoreType.DMA((8,)),
-            pltpu.VMEM((3072, 128), F32),
             pltpu.VMEM((12, 152, 128), F32),
             pltpu.VMEM((12, 152, 128), F32),
             pltpu.VMEM((3, 12, 144, 256), BF),
@@ -575,14 +572,12 @@
             pltpu.VMEM((10, 152, 128), F32),
             pltpu.VMEM((3, 10, 144, 128), BF),
             pltpu.VMEM((8, 152, 128), F32),
-            pltpu.VMEM((512, 128), F32),
-            pltpu.VMEM((512, 128), F32),
             pltpu.VMEM((80, 128), F32),
         ],
         compiler_params=pltpu.CompilerParams(vmem_limit_bytes=24 << 20),
         cost_estimate=pl.CostEstimate(flops=5000000000, bytes_accessed=4000000, transcendentals=0),
         name="second_part",
-    )(t, l, metric, h, a, b, near, far, own, mate, z, k, state, gw, cw, one)
+    )(t, l, metric, hs, near, far, own, mate, z, k, state, gw, cw, one)
 
 
 def swaps(n, first):
@@ -617,11 +612,11 @@
         ze = lax.ppermute(ze_send, "lat", chip)
     with jax.named_scope("own_core"):
         mate = lax.ppermute(own_send, "lat", core)
-    one = first_part(t, row_metric, hidden, a, b, own, mate, state_one, gates_weight, candidate_weight)
+    one, laid = first_part(t, row_metric, hidden, a, b, own, mate, state_one, gates_weight, candidate_weight)
     z = join(zi, ze, one)
     with jax.named_scope("chip_core"):
         k = lax.ppermute(z, "lat", core)
-    return second_part(t, l, row_metric, hidden, a, b, near, far, own, mate, z, k, state_two, gates_weight, candidate_weight, one)
+    return second_part(t, l, row_metric, laid, near, far, own, mate, z, k, state_two, gates_weight, candidate_weight, one)
 
 
 def solution(mesh):

time: 33.2 us -> 33 us (level)
  no operation moved by 1% of the time
where the time goes in v7:
time: 33 us; the launch traced here: 32.9 us
  starting transfers between devices  14.5 us (44%)
  Pallas kernels  14.3 us (43%)
  waiting for transfers between devices  3.97 us (12%)
    ppermute x1, starting transfers between devices, body(): b = lax.ppermute(b_send, BOTH, swaps(slabs, 1))  5.06 us
    ppermute x1, starting transfers between devices, body(): a = lax.ppermute(a_send, BOTH, swaps(slabs, 0))  4.64 us
    pallas_call x1, Pallas kernels, second_part(): pl.pallas_call(second_kernel, out_shape=jax.ShapeDtypeStruct((8, 256, 128...  4.1 us
    pallas_call x1, Pallas kernels, first_part(): pl.pallas_call(first_kernel, out_shape=(jax.ShapeDtypeStruct((8, 128, 128...  3.26 us
    ppermute x1, waiting for transfers between devices, body(): far = lax.ppermute(far_send, 'lon', swaps(count, 1))  2.15 us
    ppermute x1, starting transfers between devices, body(): far = lax.ppermute(far_send, 'lon', swaps(count, 1))  1.72 us
    ppermute x1, waiting for transfers between devices, body(): ze = lax.ppermute(ze_send, 'lat', chip)  1.57 us
    pallas_call x1, Pallas kernels, inner(): pl.pallas_call(inner_kernel, out_shape=(jax.ShapeDtypeStruct((864, 128),...  1.53 us
  transfers between devices with their start and end apart: 8, of which 3 were waited for; matrix products, arithmetic and copies ran while one was open for 0% of the time, Pallas kernels for 26%

profile of v7, /device:TPU:1, one launch (start us, length us, event | category | flops | bytes accessed | tf_op | source)
XLA Modules:
  0.0 32.9 jit_solution(14662665778179358498)
XLA Ops:
  0.0 0.0 copy-start.4
  0.0 0.0 copy-start.3
  0.0 0.0 copy-start.6
  0.0 1.5 %pack.1 = (bf16[896,128]{1,0:T(8,128)(2,1)S(1)}, bf16[912,128]{1,0:T(8,128)(2,1)S(1)}, bf16[16,128]{1,0:T(8,128)(2,1)S(1)}, bf16[16,128]{1,0:T(8,128)(2,1)S(1)}) custom-call(s32[1]{0:T(128)} %bitcast.t_ref, s32[1]{0:T(128)} %bitcast.1.l_ref, bf16[32,64,128]{2,1,0:T(8,128)(2,1)} %f_ref.5, bf16[32,64,128]{2,1,0:T(8,128)(2,1)} %s_ref.5, bf16[8,256,128]{2,1,0:T(8,128)(2,1)} %h_ref.7), custom_call_target="tpu_custom_call" | custom-call | tf_op jit(solution)/shard_map/pack/pallas_call | solution.py:74
  1.5 5.1 %collective-permute-start.1 = (bf16[912,128]{1,0:T(8,128)(2,1)S(1)}, bf16[912,128]{1,0:T(8,128)(2,1)S(1)}, u32[]{:S(2)}, u32[]{:S(2)}) collective-permute-start(bf16[912,128]{1,0:T(8,128)(2,1)S(1)} %get-tuple-element.19), channel_id=1, source_target_pairs={{1,2},{3,4},{5,6},{7,8},{9,10},{11,12},{13,14},{15,16},{17,18},{19... | collective-permute-start | bytes 700424 | tf_op jit(solution)/shard_map/rim_far/ppermute | solution.py:598
  6.6 4.6 %collective-permute-start = (bf16[896,128]{1,0:T(8,128)(2,1)S(1)}, bf16[896,128]{1,0:T(8,128)(2,1)S(1)}, u32[]{:S(2)}, u32[]{:S(2)}) collective-permute-start(bf16[896,128]{1,0:T(8,128)(2,1)S(1)} %get-tuple-element.18), channel_id=1, source_target_pairs={{0,1},{2,3},{4,5},{6,7},{8,9},{10,11},{12,13},{14,15},{16,17},{18,... | collective-permute-start | bytes 688136 | tf_op jit(solution)/shard_map/rim_near/ppermute | solution.py:600
  11.2 0.0 collective-permute-start.2
  11.2 0.0 copy-start
  11.2 0.0 copy-start.1
  11.2 0.0 copy-start.5
  11.2 1.7 %collective-permute-start.3 = (bf16[16,128]{1,0:T(8,128)(2,1)S(1)}, bf16[16,128]{1,0:T(8,128)(2,1)S(1)}, u32[]{:S(2)}, u32[]{:S(2)}) collective-permute-start(bf16[16,128]{1,0:T(8,128)(2,1)S(1)} %get-tuple-element.21), channel_id=1, source_target_pairs={{4,8},{12,16},{20,24},{28,32},{36,40},{44,48},{52,56},{60,64},{68,... | collective-permute-start | bytes 12296 | tf_op jit(solution)/shard_map/state_far/ppermute | solution.py:604
  12.9 0.0 copy-done.4
  12.9 0.0 copy-done.3
  12.9 0.0 copy-done.6
  13.0 1.5 %inner.1 = (bf16[864,128]{1,0:T(8,128)(2,1)S(1)}, bf16[864,128]{1,0:T(8,128)(2,1)S(1)}, bf16[576,128]{1,0:T(8,128)(2,1)S(1)}, bf16[992,128]{1,0:T(8,128)(2,1)S(1)}) custom-call(s32[1]{0:T(128)} %bitcast.t_ref, bf16[32,64,128]{2,1,0:T(8,128)(2,1)S(1)} %copy-done.3, bf16[32,64,128]{2,1,0:T(8,128)(2,1)S(1)} %copy-done.4, bf16[289,128]{1,0:T(8,128)(2,1)S(1)} %copy-done.6), custom_call_target="tpu_custom_call" | custom-call | flops 1000000000 | bytes 1000000 | tf_op jit(solution)/shard_map/inner/pallas_call | solution.py:153
  14.5 0.1 collective-permute-start.5
  14.6 0.0 copy-done
  14.6 0.0 copy-done.1
  14.6 0.0 copy-done.5
  14.6 1.3 %state_first.1.state_ref = f32[6,128,256]{2,1,0:T(8,128)S(1)} custom-call(s32[1]{0:T(128)} %bitcast.t_ref, f32[32]{0:T(128)S(1)} %copy-done.5, bf16[8,256,128]{2,1,0:T(8,128)(2,1)S(1)} %copy-done, bf16[3,3,256,256]{3,2,1,0:T(8,128)(2,1)S(1)} %copy-done.1), custom_call_target="tpu_custom_call" | custom-call | flops 1000000000 | bytes 2097152 | tf_op jit(solution)/shard_map/state_first/pallas_call | solution.py:338
  15.9 0.0 collective-permute-done.2.near_ref
  15.9 2.1 %collective-permute-done.3.far_ref = bf16[16,128]{1,0:T(8,128)(2,1)S(1)} collective-permute-done((bf16[16,128]{1,0:T(8,128)(2,1)S(1)}, bf16[16,128]{1,0:T(8,128)(2,1)S(1)}, u32[]{:S(2)}, u32[]{:S(2)}) %collective-permute-start.3) | collective-permute-done | bytes 4128 | tf_op jit(solution)/shard_map/state_far/ppermute | solution.py:604
  18.1 0.0 collective-permute-done.a_ref
  18.1 0.0 collective-permute-done.1.b_ref
  18.1 0.0 copy-start.2
  18.1 1.2 %edge.1 = (bf16[400,128]{1,0:T(8,128)(2,1)S(1)}, bf16[1232,128]{1,0:T(8,128)(2,1)S(1)}, bf16[848,128]{1,0:T(8,128)(2,1)S(1)}) custom-call(s32[1]{0:T(128)} %bitcast.t_ref, bf16[32,64,128]{2,1,0:T(8,128)(2,1)S(1)} %copy-done.3, bf16[32,64,128]{2,1,0:T(8,128)(2,1)S(1)} %copy-done.4, bf16[896,128]{1,0:T(8,128)(2,1)S(1)} %collective-permute-done.a_ref, ...), custom_call_target="tpu_custom_call" | custom-call | flops 1000000000 | bytes 1000000 | tf_op jit(solution)/shard_map/edge/pallas_call | solution.py:228
  19.3 1.1 %collective-permute-start.4 = (bf16[848,128]{1,0:T(8,128)(2,1)S(1)}, bf16[848,128]{1,0:T(8,128)(2,1)S(1)}, u32[]{:S(2)}, u32[]{:S(2)}) collective-permute-start(bf16[848,128]{1,0:T(8,128)(2,1)S(1)} %get-tuple-element.26), channel_id=1, source_target_pairs={{0,1},{1,0},{2,3},{3,2},{4,5},{5,4},{6,7},{7,6},{8,9},{9,8},{10,11... | collective-permute-start | bytes 651272 | tf_op jit(solution)/shard_map/own_core/ppermute | solution.py:614
  20.5 0.9 %collective-permute-start.6 = (bf16[400,128]{1,0:T(8,128)(2,1)S(1)}, bf16[400,128]{1,0:T(8,128)(2,1)S(1)}, u32[]{:S(2)}, u32[]{:S(2)}) collective-permute-start(bf16[400,128]{1,0:T(8,128)(2,1)S(1)} %get-tuple-element.29), channel_id=1, source_target_pairs={{0,2},{1,3},{2,0},{3,1},{4,6},{5,7},{6,4},{7,5},{8,10},{9,11},{10,... | collective-permute-start | bytes 307208 | tf_op jit(solution)/shard_map/edge_chip/ppermute | solution.py:612
  21.3 0.2 collective-permute-done.4.mate_ref
  21.6 0.0 copy-done.2
  21.6 3.3 %first_part.1 = (bf16[8,128,128]{2,1,0:T(8,128)(2,1)S(1)}, f32[3072,128]{1,0:T(8,128)S(1)}) custom-call(s32[1]{0:T(128)} %bitcast.t_ref, f32[32]{0:T(128)S(1)} %copy-done.5, bf16[8,256,128]{2,1,0:T(8,128)(2,1)S(1)} %copy-done, bf16[896,128]{1,0:T(8,128)(2,1)S(1)} %collective-permute-done.a_ref, bf16[912,128]{1,0:T(8,128)(2,1)S(1)} %collective-permute-done.1.b_ref, ...), custom_call_target="tpu_custom_call" | custom-call | flops 10000000 | bytes 100000 | tf_op jit(solution)/shard_map/first_part/pallas_call | solution.py:450
  24.8 0.0 collective-permute-done.5.i_ref
  24.8 1.6 %collective-permute-done.6.e_ref = bf16[400,128]{1,0:T(8,128)(2,1)S(1)} collective-permute-done((bf16[400,128]{1,0:T(8,128)(2,1)S(1)}, bf16[400,128]{1,0:T(8,128)(2,1)S(1)}, u32[]{:S(2)}, u32[]{:S(2)}) %collective-permute-start.6) | collective-permute-done | bytes 102432 | tf_op jit(solution)/shard_map/edge_chip/ppermute | solution.py:612
  26.4 1.0 %collective-permute-start.7 = (bf16[1264,128]{1,0:T(8,128)(2,1)S(1)}, bf16[1264,128]{1,0:T(8,128)(2,1)S(1)}, u32[]{:S(2)}, u32[]{:S(2)}) collective-permute-start(bf16[1264,128]{1,0:T(8,128)(2,1)S(1)} %join.1.z_ref), channel_id=1, source_target_pairs={{0,1},{1,0},{2,3},{3,2},{4,5},{5,4},{6,7},{7,6},{8,9},{9,8},{10,11... | collective-permute-start | bytes 970760 | tf_op jit(solution)/shard_map/chip_core/ppermute | solution.py:618
  27.4 1.4 %state_second.1.state_ref = f32[6,144,256]{2,1,0:T(8,128)S(1)} custom-call(s32[1]{0:T(128)} %bitcast.t_ref, s32[1]{0:T(128)} %bitcast.1.l_ref, f32[32]{0:T(128)S(1)} %copy-done.5, bf16[8,256,128]{2,1,0:T(8,128)(2,1)S(1)} %copy-done, bf16[16,128]{1,0:T(8,128)(2,1)S(1)} %collective-permute-done.2.near_ref, bf16[16,128]{1,0:T(8,128)(2,1)S(1)} %collective-permute-done.3.far_ref, ...), custom_call_target="tpu_custom_call" | custom-call | flops 1000000000 | bytes 2097152 | tf_op jit(solution)/shard_map/state_second/pallas_call | solution.py:351
  28.8 0.0 collective-permute-done.7.k_ref
  28.8 4.1 %second_part.1 = bf16[8,256,128]{2,1,0:T(8,128)(2,1)} custom-call(s32[1]{0:T(128)} %bitcast.t_ref, s32[1]{0:T(128)} %bitcast.1.l_ref, f32[32]{0:T(128)S(1)} %copy-done.5, f32[3072,128]{1,0:T(8,128)S(1)} %get-tuple-element.27.hs, bf16[16,128]{1,0:T(8,128)(2,1)S(1)} %collective-permute-done.2.near_ref, bf16[16,128]{1,0:T(8,128)(2,1)S(1)} %collective-permute-done.3.far_ref, ...), custom_call_target="tpu_custom_call" | custom-call | flops 5000000000 | bytes 4000000 | tf_op jit(solution)/shard_map/second_part/pallas_call | solution.py:559
  (1 shorter events, 0.0 us)
Async XLA Ops:
  0.0 12.9 %copy-start.4 = (bf16[32,64,128]{2,1,0:T(8,128)(2,1)S(1)}, bf16[32,64,128]{2,1,0:T(8,128)(2,1)}, u32[]{:S(2)}) copy-start(bf16[32,64,128]{2,1,0:T(8,128)(2,1)} %s_ref.5) | copy-start | bytes 1572868
  0.0 12.9 %copy-start.3 = (bf16[32,64,128]{2,1,0:T(8,128)(2,1)S(1)}, bf16[32,64,128]{2,1,0:T(8,128)(2,1)}, u32[]{:S(2)}) copy-start(bf16[32,64,128]{2,1,0:T(8,128)(2,1)} %f_ref.5) | copy-start | bytes 1572868
  0.0 12.9 %copy-start.6 = (bf16[289,128]{1,0:T(8,128)(2,1)S(1)}, bf16[289,128]{1,0:T(8,128)(2,1)}, u32[]{:S(2)}) copy-start(bf16[289,128]{1,0:T(8,128)(2,1)} %enc_ref.1) | copy-start | bytes 221956
  1.5 16.6 %collective-permute-start.1 = (bf16[912,128]{1,0:T(8,128)(2,1)S(1)}, bf16[912,128]{1,0:T(8,128)(2,1)S(1)}, u32[]{:S(2)}, u32[]{:S(2)}) collective-permute-start(bf16[912,128]{1,0:T(8,128)(2,1)S(1)} %get-tuple-element.19), channel_id=1, source_target_pairs={{1,2},{3,4},{5,6},{7,8},{9,10},{11,12},{13,14},{15,16},{17,18},{19... | collective-permute-start | bytes 700424 | tf_op jit(solution)/shard_map/rim_far/ppermute | solution.py:598
  6.6 11.5 %collective-permute-start = (bf16[896,128]{1,0:T(8,128)(2,1)S(1)}, bf16[896,128]{1,0:T(8,128)(2,1)S(1)}, u32[]{:S(2)}, u32[]{:S(2)}) collective-permute-start(bf16[896,128]{1,0:T(8,128)(2,1)S(1)} %get-tuple-element.18), channel_id=1, source_target_pairs={{0,1},{2,3},{4,5},{6,7},{8,9},{10,11},{12,13},{14,15},{16,17},{18,... | collective-permute-start | bytes 688136 | tf_op jit(solution)/shard_map/rim_near/ppermute | solution.py:600
  11.2 4.7 %collective-permute-start.2 = (bf16[16,128]{1,0:T(8,128)(2,1)S(1)}, bf16[16,128]{1,0:T(8,128)(2,1)S(1)}, u32[]{:S(2)}, u32[]{:S(2)}) collective-permute-start(bf16[16,128]{1,0:T(8,128)(2,1)S(1)} %get-tuple-element.20), channel_id=1, source_target_pairs={{0,4},{8,12},{16,20},{24,28},{32,36},{40,44},{48,52},{56,60},{64,6... | collective-permute-start | bytes 12296 | tf_op jit(solution)/shard_map/state_near/ppermute | solution.py:602
  11.2 3.4 %copy-start = (bf16[8,256,128]{2,1,0:T(8,128)(2,1)S(1)}, bf16[8,256,128]{2,1,0:T(8,128)(2,1)}, u32[]{:S(2)}) copy-start(bf16[8,256,128]{2,1,0:T(8,128)(2,1)} %h_ref.7) | copy-start | bytes 1572868
  11.2 3.4 %copy-start.1 = (bf16[3,3,256,256]{3,2,1,0:T(8,128)(2,1)S(1)}, bf16[3,3,256,256]{3,2,1,0:T(8,128)(2,1)}, u32[]{:S(2)}) copy-start(bf16[3,3,256,256]{3,2,1,0:T(8,128)(2,1)} %gw_ref.7) | copy-start | bytes 3538948
  11.2 3.4 %copy-start.5 = (f32[32]{0:T(128)S(1)}, f32[32]{0:T(128)}, u32[]{:S(2)}) copy-start(f32[32]{0:T(128)} %metric_ref.7) | copy-start | bytes 388
  11.2 6.9 %collective-permute-start.3 = (bf16[16,128]{1,0:T(8,128)(2,1)S(1)}, bf16[16,128]{1,0:T(8,128)(2,1)S(1)}, u32[]{:S(2)}, u32[]{:S(2)}) collective-permute-start(bf16[16,128]{1,0:T(8,128)(2,1)S(1)} %get-tuple-element.21), channel_id=1, source_target_pairs={{4,8},{12,16},{20,24},{28,32},{36,40},{44,48},{52,56},{60,64},{68,... | collective-permute-start | bytes 12296 | tf_op jit(solution)/shard_map/state_far/ppermute | solution.py:604
  14.5 10.3 %collective-permute-start.5 = (bf16[864,128]{1,0:T(8,128)(2,1)S(1)}, bf16[864,128]{1,0:T(8,128)(2,1)S(1)}, u32[]{:S(2)}, u32[]{:S(2)}) collective-permute-start(bf16[864,128]{1,0:T(8,128)(2,1)S(1)} %get-tuple-element.28), channel_id=1, source_target_pairs={{0,2},{1,3},{2,0},{3,1},{4,6},{5,7},{6,4},{7,5},{8,10},{9,11},{10,... | collective-permute-start | bytes 663560 | tf_op jit(solution)/shard_map/inner_chip/ppermute | solution.py:607
  18.1 3.5 %copy-start.2 = (bf16[3,3,256,128]{3,2,1,0:T(8,128)(2,1)S(1)}, bf16[3,3,256,128]{3,2,1,0:T(8,128)(2,1)}, u32[]{:S(2)}) copy-start(bf16[3,3,256,128]{3,2,1,0:T(8,128)(2,1)} %cw_ref.3) | copy-start | bytes 1769476
  19.3 2.2 %collective-permute-start.4 = (bf16[848,128]{1,0:T(8,128)(2,1)S(1)}, bf16[848,128]{1,0:T(8,128)(2,1)S(1)}, u32[]{:S(2)}, u32[]{:S(2)}) collective-permute-start(bf16[848,128]{1,0:T(8,128)(2,1)S(1)} %get-tuple-element.26), channel_id=1, source_target_pairs={{0,1},{1,0},{2,3},{3,2},{4,5},{5,4},{6,7},{7,6},{8,9},{9,8},{10,11... | collective-permute-start | bytes 651272 | tf_op jit(solution)/shard_map/own_core/ppermute | solution.py:614
  20.5 5.9 %collective-permute-start.6 = (bf16[400,128]{1,0:T(8,128)(2,1)S(1)}, bf16[400,128]{1,0:T(8,128)(2,1)S(1)}, u32[]{:S(2)}, u32[]{:S(2)}) collective-permute-start(bf16[400,128]{1,0:T(8,128)(2,1)S(1)} %get-tuple-element.29), channel_id=1, source_target_pairs={{0,2},{1,3},{2,0},{3,1},{4,6},{5,7},{6,4},{7,5},{8,10},{9,11},{10,... | collective-permute-start | bytes 307208 | tf_op jit(solution)/shard_map/edge_chip/ppermute | solution.py:612
  26.4 2.4 %collective-permute-start.7 = (bf16[1264,128]{1,0:T(8,128)(2,1)S(1)}, bf16[1264,128]{1,0:T(8,128)(2,1)S(1)}, u32[]{:S(2)}, u32[]{:S(2)}) collective-permute-start(bf16[1264,128]{1,0:T(8,128)(2,1)S(1)} %join.1.z_ref), channel_id=1, source_target_pairs={{0,1},{1,0},{2,3},{3,2},{4,5},{5,4},{6,7},{7,6},{8,9},{9,8},{10,11... | collective-permute-start | bytes 970760 | tf_op jit(solution)/shard_map/chip_core/ppermute | solution.py:618

commit v8 on v7

--- a/solution.py
+++ b/solution.py
@@ -37,11 +37,14 @@
     copies = [pltpu.make_async_copy(a, b, sem.at[k]) for k, (a, b) in enumerate(moves)]
     for c in copies:
         c.start()
-    for c in copies:
-        c.wait()
+    for k in (0, 4):
+        copies[k].wait()
     for r in range(rows):
         up[10 * r : 10 * r + 10] = sb[0, r].astype(F32)[6:16]
         down[10 * r : 10 * r + 10] = sb[1, r].astype(F32)[0:10]
+    for k in (1, 5, 2, 6, 3, 7):
+        copies[k].wait()
+    for r in range(rows):
         up[320 + 2 * r : 322 + 2 * r] = fb[0, r].astype(F32)[14:16]
         down[320 + 2 * r : 322 + 2 * r] = fb[1, r].astype(F32)[0:2]
     east = jnp.concatenate([cb[0, i].astype(F32)[14:16] for i in range(8)], axis=0)

time: 33 us -> 33 us (level)
  no operation moved by 1% of the time
where the time goes in v8:
time: 33 us; the launch traced here: 32.9 us
  starting transfers between devices  14.5 us (44%)
  Pallas kernels  14.3 us (43%)
  waiting for transfers between devices  3.97 us (12%)
    ppermute x1, starting transfers between devices, body(): b = lax.ppermute(b_send, BOTH, swaps(slabs, 1))  5.06 us
    ppermute x1, starting transfers between devices, body(): a = lax.ppermute(a_send, BOTH, swaps(slabs, 0))  4.64 us
    pallas_call x1, Pallas kernels, second_part(): pl.pallas_call(second_kernel, out_shape=jax.ShapeDtypeStruct((8, 256, 128...  4.1 us
    pallas_call x1, Pallas kernels, first_part(): pl.pallas_call(first_kernel, out_shape=(jax.ShapeDtypeStruct((8, 128, 128...  3.26 us
    ppermute x1, waiting for transfers between devices, body(): far = lax.ppermute(far_send, 'lon', swaps(count, 1))  2.15 us
    ppermute x1, starting transfers between devices, body(): far = lax.ppermute(far_send, 'lon', swaps(count, 1))  1.72 us
    ppermute x1, waiting for transfers between devices, body(): ze = lax.ppermute(ze_send, 'lat', chip)  1.57 us
    pallas_call x1, Pallas kernels, inner(): pl.pallas_call(inner_kernel, out_shape=(jax.ShapeDtypeStruct((864, 128),...  1.53 us
  transfers between devices with their start and end apart: 8, of which 3 were waited for; matrix products, arithmetic and copies ran while one was open for 0% of the time, Pallas kernels for 26%

profile of v8, /device:TPU:1, one launch (start us, length us, event | category | flops | bytes accessed | tf_op | source)
XLA Modules:
  0.0 32.9 jit_solution(17086902598773009114)
XLA Ops:
  0.0 0.0 copy-start.4
  0.0 0.0 copy-start.3
  0.0 0.0 copy-start.6
  0.0 1.4 %pack.1 = (bf16[896,128]{1,0:T(8,128)(2,1)S(1)}, bf16[912,128]{1,0:T(8,128)(2,1)S(1)}, bf16[16,128]{1,0:T(8,128)(2,1)S(1)}, bf16[16,128]{1,0:T(8,128)(2,1)S(1)}) custom-call(s32[1]{0:T(128)} %bitcast.t_ref, s32[1]{0:T(128)} %bitcast.1.l_ref, bf16[32,64,128]{2,1,0:T(8,128)(2,1)} %f_ref.5, bf16[32,64,128]{2,1,0:T(8,128)(2,1)} %s_ref.5, bf16[8,256,128]{2,1,0:T(8,128)(2,1)} %h_ref.7), custom_call_target="tpu_custom_call" | custom-call | tf_op jit(solution)/shard_map/pack/pallas_call | solution.py:77
  1.5 5.1 %collective-permute-start.1 = (bf16[912,128]{1,0:T(8,128)(2,1)S(1)}, bf16[912,128]{1,0:T(8,128)(2,1)S(1)}, u32[]{:S(2)}, u32[]{:S(2)}) collective-permute-start(bf16[912,128]{1,0:T(8,128)(2,1)S(1)} %get-tuple-element.19), channel_id=1, source_target_pairs={{1,2},{3,4},{5,6},{7,8},{9,10},{11,12},{13,14},{15,16},{17,18},{19... | collective-permute-start | bytes 700424 | tf_op jit(solution)/shard_map/rim_far/ppermute | solution.py:601
  6.5 4.6 %collective-permute-start = (bf16[896,128]{1,0:T(8,128)(2,1)S(1)}, bf16[896,128]{1,0:T(8,128)(2,1)S(1)}, u32[]{:S(2)}, u32[]{:S(2)}) collective-permute-start(bf16[896,128]{1,0:T(8,128)(2,1)S(1)} %get-tuple-element.18), channel_id=1, source_target_pairs={{0,1},{2,3},{4,5},{6,7},{8,9},{10,11},{12,13},{14,15},{16,17},{18,... | collective-permute-start | bytes 688136 | tf_op jit(solution)/shard_map/rim_near/ppermute | solution.py:603
  11.2 0.0 collective-permute-start.2
  11.2 0.0 copy-start
  11.2 0.0 copy-start.1
  11.2 0.0 copy-start.5
  11.2 1.7 %collective-permute-start.3 = (bf16[16,128]{1,0:T(8,128)(2,1)S(1)}, bf16[16,128]{1,0:T(8,128)(2,1)S(1)}, u32[]{:S(2)}, u32[]{:S(2)}) collective-permute-start(bf16[16,128]{1,0:T(8,128)(2,1)S(1)} %get-tuple-element.21), channel_id=1, source_target_pairs={{4,8},{12,16},{20,24},{28,32},{36,40},{44,48},{52,56},{60,64},{68,... | collective-permute-start | bytes 12296 | tf_op jit(solution)/shard_map/state_far/ppermute | solution.py:607
  12.9 0.0 copy-done.4
  12.9 0.0 copy-done.3
  12.9 0.0 copy-done.6
  12.9 1.5 %inner.1 = (bf16[864,128]{1,0:T(8,128)(2,1)S(1)}, bf16[864,128]{1,0:T(8,128)(2,1)S(1)}, bf16[576,128]{1,0:T(8,128)(2,1)S(1)}, bf16[992,128]{1,0:T(8,128)(2,1)S(1)}) custom-call(s32[1]{0:T(128)} %bitcast.t_ref, bf16[32,64,128]{2,1,0:T(8,128)(2,1)S(1)} %copy-done.3, bf16[32,64,128]{2,1,0:T(8,128)(2,1)S(1)} %copy-done.4, bf16[289,128]{1,0:T(8,128)(2,1)S(1)} %copy-done.6), custom_call_target="tpu_custom_call" | custom-call | flops 1000000000 | bytes 1000000 | tf_op jit(solution)/shard_map/inner/pallas_call | solution.py:156
  14.5 0.1 collective-permute-start.5
  14.6 0.0 copy-done
  14.6 0.0 copy-done.1
  14.6 0.0 copy-done.5
  14.6 1.3 %state_first.1.state_ref = f32[6,128,256]{2,1,0:T(8,128)S(1)} custom-call(s32[1]{0:T(128)} %bitcast.t_ref, f32[32]{0:T(128)S(1)} %copy-done.5, bf16[8,256,128]{2,1,0:T(8,128)(2,1)S(1)} %copy-done, bf16[3,3,256,256]{3,2,1,0:T(8,128)(2,1)S(1)} %copy-done.1), custom_call_target="tpu_custom_call" | custom-call | flops 1000000000 | bytes 2097152 | tf_op jit(solution)/shard_map/state_first/pallas_call | solution.py:341
  15.9 0.0 collective-permute-done.2.near_ref
  15.9 2.1 %collective-permute-done.3.far_ref = bf16[16,128]{1,0:T(8,128)(2,1)S(1)} collective-permute-done((bf16[16,128]{1,0:T(8,128)(2,1)S(1)}, bf16[16,128]{1,0:T(8,128)(2,1)S(1)}, u32[]{:S(2)}, u32[]{:S(2)}) %collective-permute-start.3) | collective-permute-done | bytes 4128 | tf_op jit(solution)/shard_map/state_far/ppermute | solution.py:607
  18.1 0.0 collective-permute-done.a_ref
  18.1 0.0 collective-permute-done.1.b_ref
  18.1 0.0 copy-start.2
  18.1 1.2 %edge.1 = (bf16[400,128]{1,0:T(8,128)(2,1)S(1)}, bf16[1232,128]{1,0:T(8,128)(2,1)S(1)}, bf16[848,128]{1,0:T(8,128)(2,1)S(1)}) custom-call(s32[1]{0:T(128)} %bitcast.t_ref, bf16[32,64,128]{2,1,0:T(8,128)(2,1)S(1)} %copy-done.3, bf16[32,64,128]{2,1,0:T(8,128)(2,1)S(1)} %copy-done.4, bf16[896,128]{1,0:T(8,128)(2,1)S(1)} %collective-permute-done.a_ref, ...), custom_call_target="tpu_custom_call" | custom-call | flops 1000000000 | bytes 1000000 | tf_op jit(solution)/shard_map/edge/pallas_call | solution.py:231
  19.3 1.1 %collective-permute-start.4 = (bf16[848,128]{1,0:T(8,128)(2,1)S(1)}, bf16[848,128]{1,0:T(8,128)(2,1)S(1)}, u32[]{:S(2)}, u32[]{:S(2)}) collective-permute-start(bf16[848,128]{1,0:T(8,128)(2,1)S(1)} %get-tuple-element.26), channel_id=1, source_target_pairs={{0,1},{1,0},{2,3},{3,2},{4,5},{5,4},{6,7},{7,6},{8,9},{9,8},{10,11... | collective-permute-start | bytes 651272 | tf_op jit(solution)/shard_map/own_core/ppermute | solution.py:617
  20.4 0.9 %collective-permute-start.6 = (bf16[400,128]{1,0:T(8,128)(2,1)S(1)}, bf16[400,128]{1,0:T(8,128)(2,1)S(1)}, u32[]{:S(2)}, u32[]{:S(2)}) collective-permute-start(bf16[400,128]{1,0:T(8,128)(2,1)S(1)} %get-tuple-element.29), channel_id=1, source_target_pairs={{0,2},{1,3},{2,0},{3,1},{4,6},{5,7},{6,4},{7,5},{8,10},{9,11},{10,... | collective-permute-start | bytes 307208 | tf_op jit(solution)/shard_map/edge_chip/ppermute | solution.py:615
  21.3 0.2 collective-permute-done.4.mate_ref
  21.5 0.0 copy-done.2
  21.5 3.3 %first_part.1 = (bf16[8,128,128]{2,1,0:T(8,128)(2,1)S(1)}, f32[3072,128]{1,0:T(8,128)S(1)}) custom-call(s32[1]{0:T(128)} %bitcast.t_ref, f32[32]{0:T(128)S(1)} %copy-done.5, bf16[8,256,128]{2,1,0:T(8,128)(2,1)S(1)} %copy-done, bf16[896,128]{1,0:T(8,128)(2,1)S(1)} %collective-permute-done.a_ref, bf16[912,128]{1,0:T(8,128)(2,1)S(1)} %collective-permute-done.1.b_ref, ...), custom_call_target="tpu_custom_call" | custom-call | flops 10000000 | bytes 100000 | tf_op jit(solution)/shard_map/first_part/pallas_call | solution.py:453
  24.8 0.0 collective-permute-done.5.i_ref
  24.8 1.6 %collective-permute-done.6.e_ref = bf16[400,128]{1,0:T(8,128)(2,1)S(1)} collective-permute-done((bf16[400,128]{1,0:T(8,128)(2,1)S(1)}, bf16[400,128]{1,0:T(8,128)(2,1)S(1)}, u32[]{:S(2)}, u32[]{:S(2)}) %collective-permute-start.6) | collective-permute-done | bytes 102432 | tf_op jit(solution)/shard_map/edge_chip/ppermute | solution.py:615
  26.4 1.0 %collective-permute-start.7 = (bf16[1264,128]{1,0:T(8,128)(2,1)S(1)}, bf16[1264,128]{1,0:T(8,128)(2,1)S(1)}, u32[]{:S(2)}, u32[]{:S(2)}) collective-permute-start(bf16[1264,128]{1,0:T(8,128)(2,1)S(1)} %join.1.z_ref), channel_id=1, source_target_pairs={{0,1},{1,0},{2,3},{3,2},{4,5},{5,4},{6,7},{7,6},{8,9},{9,8},{10,11... | collective-permute-start | bytes 970760 | tf_op jit(solution)/shard_map/chip_core/ppermute | solution.py:621
  27.4 1.4 %state_second.1.state_ref = f32[6,144,256]{2,1,0:T(8,128)S(1)} custom-call(s32[1]{0:T(128)} %bitcast.t_ref, s32[1]{0:T(128)} %bitcast.1.l_ref, f32[32]{0:T(128)S(1)} %copy-done.5, bf16[8,256,128]{2,1,0:T(8,128)(2,1)S(1)} %copy-done, bf16[16,128]{1,0:T(8,128)(2,1)S(1)} %collective-permute-done.2.near_ref, bf16[16,128]{1,0:T(8,128)(2,1)S(1)} %collective-permute-done.3.far_ref, ...), custom_call_target="tpu_custom_call" | custom-call | flops 1000000000 | bytes 2097152 | tf_op jit(solution)/shard_map/state_second/pallas_call | solution.py:354
  28.8 0.0 collective-permute-done.7.k_ref
  28.8 4.1 %second_part.1 = bf16[8,256,128]{2,1,0:T(8,128)(2,1)} custom-call(s32[1]{0:T(128)} %bitcast.t_ref, s32[1]{0:T(128)} %bitcast.1.l_ref, f32[32]{0:T(128)S(1)} %copy-done.5, f32[3072,128]{1,0:T(8,128)S(1)} %get-tuple-element.27.hs, bf16[16,128]{1,0:T(8,128)(2,1)S(1)} %collective-permute-done.2.near_ref, bf16[16,128]{1,0:T(8,128)(2,1)S(1)} %collective-permute-done.3.far_ref, ...), custom_call_target="tpu_custom_call" | custom-call | flops 5000000000 | bytes 4000000 | tf_op jit(solution)/shard_map/second_part/pallas_call | solution.py:562
  (1 shorter events, 0.0 us)
Async XLA Ops:
  0.0 12.9 %copy-start.4 = (bf16[32,64,128]{2,1,0:T(8,128)(2,1)S(1)}, bf16[32,64,128]{2,1,0:T(8,128)(2,1)}, u32[]{:S(2)}) copy-start(bf16[32,64,128]{2,1,0:T(8,128)(2,1)} %s_ref.5) | copy-start | bytes 1572868
  0.0 12.9 %copy-start.3 = (bf16[32,64,128]{2,1,0:T(8,128)(2,1)S(1)}, bf16[32,64,128]{2,1,0:T(8,128)(2,1)}, u32[]{:S(2)}) copy-start(bf16[32,64,128]{2,1,0:T(8,128)(2,1)} %f_ref.5) | copy-start | bytes 1572868
  0.0 12.9 %copy-start.6 = (bf16[289,128]{1,0:T(8,128)(2,1)S(1)}, bf16[289,128]{1,0:T(8,128)(2,1)}, u32[]{:S(2)}) copy-start(bf16[289,128]{1,0:T(8,128)(2,1)} %enc_ref.1) | copy-start | bytes 221956
  1.5 16.6 %collective-permute-start.1 = (bf16[912,128]{1,0:T(8,128)(2,1)S(1)}, bf16[912,128]{1,0:T(8,128)(2,1)S(1)}, u32[]{:S(2)}, u32[]{:S(2)}) collective-permute-start(bf16[912,128]{1,0:T(8,128)(2,1)S(1)} %get-tuple-element.19), channel_id=1, source_target_pairs={{1,2},{3,4},{5,6},{7,8},{9,10},{11,12},{13,14},{15,16},{17,18},{19... | collective-permute-start | bytes 700424 | tf_op jit(solution)/shard_map/rim_far/ppermute | solution.py:601
  6.5 11.5 %collective-permute-start = (bf16[896,128]{1,0:T(8,128)(2,1)S(1)}, bf16[896,128]{1,0:T(8,128)(2,1)S(1)}, u32[]{:S(2)}, u32[]{:S(2)}) collective-permute-start(bf16[896,128]{1,0:T(8,128)(2,1)S(1)} %get-tuple-element.18), channel_id=1, source_target_pairs={{0,1},{2,3},{4,5},{6,7},{8,9},{10,11},{12,13},{14,15},{16,17},{18,... | collective-permute-start | bytes 688136 | tf_op jit(solution)/shard_map/rim_near/ppermute | solution.py:603
  11.2 4.7 %collective-permute-start.2 = (bf16[16,128]{1,0:T(8,128)(2,1)S(1)}, bf16[16,128]{1,0:T(8,128)(2,1)S(1)}, u32[]{:S(2)}, u32[]{:S(2)}) collective-permute-start(bf16[16,128]{1,0:T(8,128)(2,1)S(1)} %get-tuple-element.20), channel_id=1, source_target_pairs={{0,4},{8,12},{16,20},{24,28},{32,36},{40,44},{48,52},{56,60},{64,6... | collective-permute-start | bytes 12296 | tf_op jit(solution)/shard_map/state_near/ppermute | solution.py:605
  11.2 3.4 %copy-start = (bf16[8,256,128]{2,1,0:T(8,128)(2,1)S(1)}, bf16[8,256,128]{2,1,0:T(8,128)(2,1)}, u32[]{:S(2)}) copy-start(bf16[8,256,128]{2,1,0:T(8,128)(2,1)} %h_ref.7) | copy-start | bytes 1572868
  11.2 3.4 %copy-start.1 = (bf16[3,3,256,256]{3,2,1,0:T(8,128)(2,1)S(1)}, bf16[3,3,256,256]{3,2,1,0:T(8,128)(2,1)}, u32[]{:S(2)}) copy-start(bf16[3,3,256,256]{3,2,1,0:T(8,128)(2,1)} %gw_ref.7) | copy-start | bytes 3538948
  11.2 3.4 %copy-start.5 = (f32[32]{0:T(128)S(1)}, f32[32]{0:T(128)}, u32[]{:S(2)}) copy-start(f32[32]{0:T(128)} %metric_ref.7) | copy-start | bytes 388
  11.2 6.9 %collective-permute-start.3 = (bf16[16,128]{1,0:T(8,128)(2,1)S(1)}, bf16[16,128]{1,0:T(8,128)(2,1)S(1)}, u32[]{:S(2)}, u32[]{:S(2)}) collective-permute-start(bf16[16,128]{1,0:T(8,128)(2,1)S(1)} %get-tuple-element.21), channel_id=1, source_target_pairs={{4,8},{12,16},{20,24},{28,32},{36,40},{44,48},{52,56},{60,64},{68,... | collective-permute-start | bytes 12296 | tf_op jit(solution)/shard_map/state_far/ppermute | solution.py:607
  14.5 10.3 %collective-permute-start.5 = (bf16[864,128]{1,0:T(8,128)(2,1)S(1)}, bf16[864,128]{1,0:T(8,128)(2,1)S(1)}, u32[]{:S(2)}, u32[]{:S(2)}) collective-permute-start(bf16[864,128]{1,0:T(8,128)(2,1)S(1)} %get-tuple-element.28), channel_id=1, source_target_pairs={{0,2},{1,3},{2,0},{3,1},{4,6},{5,7},{6,4},{7,5},{8,10},{9,11},{10,... | collective-permute-start | bytes 663560 | tf_op jit(solution)/shard_map/inner_chip/ppermute | solution.py:610
  18.1 3.5 %copy-start.2 = (bf16[3,3,256,128]{3,2,1,0:T(8,128)(2,1)S(1)}, bf16[3,3,256,128]{3,2,1,0:T(8,128)(2,1)}, u32[]{:S(2)}) copy-start(bf16[3,3,256,128]{3,2,1,0:T(8,128)(2,1)} %cw_ref.3) | copy-start | bytes 1769476
  19.3 2.2 %collective-permute-start.4 = (bf16[848,128]{1,0:T(8,128)(2,1)S(1)}, bf16[848,128]{1,0:T(8,128)(2,1)S(1)}, u32[]{:S(2)}, u32[]{:S(2)}) collective-permute-start(bf16[848,128]{1,0:T(8,128)(2,1)S(1)} %get-tuple-element.26), channel_id=1, source_target_pairs={{0,1},{1,0},{2,3},{3,2},{4,5},{5,4},{6,7},{7,6},{8,9},{9,8},{10,11... | collective-permute-start | bytes 651272 | tf_op jit(solution)/shard_map/own_core/ppermute | solution.py:617
  20.4 5.9 %collective-permute-start.6 = (bf16[400,128]{1,0:T(8,128)(2,1)S(1)}, bf16[400,128]{1,0:T(8,128)(2,1)S(1)}, u32[]{:S(2)}, u32[]{:S(2)}) collective-permute-start(bf16[400,128]{1,0:T(8,128)(2,1)S(1)} %get-tuple-element.29), channel_id=1, source_target_pairs={{0,2},{1,3},{2,0},{3,1},{4,6},{5,7},{6,4},{7,5},{8,10},{9,11},{10,... | collective-permute-start | bytes 307208 | tf_op jit(solution)/shard_map/edge_chip/ppermute | solution.py:615
  26.4 2.4 %collective-permute-start.7 = (bf16[1264,128]{1,0:T(8,128)(2,1)S(1)}, bf16[1264,128]{1,0:T(8,128)(2,1)S(1)}, u32[]{:S(2)}, u32[]{:S(2)}) collective-permute-start(bf16[1264,128]{1,0:T(8,128)(2,1)S(1)} %join.1.z_ref), channel_id=1, source_target_pairs={{0,1},{1,0},{2,3},{3,2},{4,5},{5,4},{6,7},{7,6},{8,9},{9,8},{10,11... | collective-permute-start | bytes 970760 | tf_op jit(solution)/shard_map/chip_core/ppermute | solution.py:621
